TPU v7x, 512 devices: a whole 4x8x8 slice. The times are simulated.
512 devices in a mesh: gx: 16 (over y, x_lo), gz: 32 (over z, x_hi, core).
Axes of the slice: x: 4 (x_hi: 2, x_lo: 2; x = x_hi * 2 + x_lo), y: 8, z: 8, core: 2. Of those that a mesh axis runs over, the one named last changes fastest.
Arguments:
- tangents: float32 [8, 2, 2, 1024, 2048], P(None, None, None, 'gz', 'gx'), may hold values from -6 to 6
- baseline_mass_concentration: float32 [2, 1024, 2048], P(None, 'gz', 'gx'), may hold values from 0.5 to 2
- baseline_internal_value: float32 [2, 1024, 2048], P(None, 'gz', 'gx'), may hold values from 2.5 to 5.5
- base_velocity: float32 [2, 1024, 2048], P(None, 'gz', 'gx'), may hold values from 0.15 to 3, as said below
Outputs:
- renormalized: float32 [8, 2, 2, 1024, 2048], P(None, None, None, 'gz', 'gx')
- growth: float32 [8, 8], replicated
Inputs may be any that keep to these rules, and one draw needn't show every extreme that they name: `base_velocity`: positive streamwise velocity.
All inputs are finite; a program needn't handle non-finite values.
Results may differ from a plain program's by a relative error of at most 0.000098.
Values sent between devices are 32-bit elements; how exact they have to be, the bound alone decides.
No kernel may reach another device: no remote copies, remote signals or barrier semaphores. Data moves between devices by JAX's collectives and lax.ppermute only.
A program may use at most 64 MiB of HBM per device.

v0:
```python
import jax
import jax.numpy as jnp
from jax import lax
from jax.sharding import PartitionSpec as P

NEWTON = 4


isochoric_warmth_coefficient = 3.0
attraction = 0.5
acentric_coefficient_gradient = 0.6
covolume = 0.15
root_two = 1.4142135623730951
viscosity = 0.2
conductivity = 1.0
courant_number = 0.5


def with_halo(array, sides, width):
    for axis, dim in sides:
        size, length = (lax.axis_size(axis), array.shape[dim])
        up = [(i, (i + 1) % size) for i in range(size)]
        down = [(j, i) for i, j in up]
        last = lax.slice_in_dim(array, length - width, length, axis=dim)
        initial = lax.slice_in_dim(array, 0, width, axis=dim)
        before = lax.ppermute(last, axis, up)
        after = lax.ppermute(initial, axis, down)
        array = jnp.concatenate([before, array, after], axis=dim)
    return array


def departure(cell_mass_concentration):
    low_term = 1.0 + (1.0 - root_two) * covolume * cell_mass_concentration
    high_term = 1.0 + (1.0 + root_two) * covolume * cell_mass_concentration
    factor = attraction * (1.0 + acentric_coefficient_gradient) / (2.0 * root_two * covolume)
    value = factor * (jnp.log(low_term) - jnp.log(high_term))
    slope = factor * (
        (1.0 - root_two) * covolume / low_term - (1.0 + root_two) * covolume / high_term
    )
    return (value, slope)


def thermal_linearized_gradients(cell_mass_concentration, cell_internal_value):
    nonideal_deviation, departure_slope = departure(cell_mass_concentration)
    converged_thermal_state = cell_internal_value / isochoric_warmth_coefficient
    for newton_step in range(NEWTON):
        thermal_zero_estimate = jnp.sqrt(converged_thermal_state)
        attractive_correction_multiplier = 1.0 + acentric_coefficient_gradient * (
            1.0 - thermal_zero_estimate
        )
        internal_mismatch = (
            isochoric_warmth_coefficient * converged_thermal_state
            + nonideal_deviation * attractive_correction_multiplier
            - cell_internal_value
        )
        thermal_gradient = (
            isochoric_warmth_coefficient
            - nonideal_deviation * acentric_coefficient_gradient / (2.0 * thermal_zero_estimate)
        )
        converged_thermal_state = converged_thermal_state - internal_mismatch / thermal_gradient
    thermal_zero_estimate = jnp.sqrt(converged_thermal_state)
    attractive_correction_multiplier = 1.0 + acentric_coefficient_gradient * (
        1.0 - thermal_zero_estimate
    )
    thermal_gradient = (
        isochoric_warmth_coefficient
        - nonideal_deviation * acentric_coefficient_gradient / (2.0 * thermal_zero_estimate)
    )
    internal_gradient_contribution = 1.0 / thermal_gradient
    mass_gradient_contribution = (
        -departure_slope * attractive_correction_multiplier * internal_gradient_contribution
    )
    return (mass_gradient_contribution, internal_gradient_contribution)


def fourth_order(minus_two, minus_one, center, plus_one, plus_two):
    return (16.0 * (minus_one + plus_one) - (minus_two + plus_two) - 30.0 * center) / 12.0


def derivative_x(widened):
    along_x = widened[..., 2:-2, :]
    return (
        along_x[..., :-4] - 8.0 * along_x[..., 1:-3] + 8.0 * along_x[..., 3:-1] - along_x[..., 4:]
    ) / 12.0


def laplacian(widened):
    center = widened[..., 2:-2, 2:-2]
    along_x = widened[..., 2:-2, :]
    along_z = widened[..., :, 2:-2]
    term_x = fourth_order(
        along_x[..., :-4], along_x[..., 1:-3], center, along_x[..., 3:-1], along_x[..., 4:]
    )
    term_z = fourth_order(
        along_z[..., :-4, :],
        along_z[..., 1:-3, :],
        center,
        along_z[..., 3:-1, :],
        along_z[..., 4:, :],
    )
    padded = jnp.pad(center, ((0, 0), (2, 2), (0, 0), (0, 0)))
    term_y = fourth_order(padded[:, :-4], padded[:, 1:-3], center, padded[:, 3:-1], padded[:, 4:])
    return term_x + term_z + term_y


def section_rates(wide_pair, wide_temp, velocity):
    wide_density = wide_pair[:, 0]
    wide_energy = wide_pair[:, 1]
    rate_density = -velocity * derivative_x(wide_density) + viscosity * laplacian(wide_density)
    rate_energy = -velocity * derivative_x(wide_energy) + conductivity * laplacian(wide_temp)
    return jnp.stack([rate_density, rate_energy], axis=1)


def operate(tangent_pair, velocity, mass_gradient_contribution, internal_gradient_contribution):
    tangent_temp = (
        mass_gradient_contribution * tangent_pair[:, 0]
        + internal_gradient_contribution * tangent_pair[:, 1]
    )
    stacked = jnp.concatenate([tangent_pair, tangent_temp[:, None]], axis=1)
    widened = with_halo(stacked, (("gx", 4), ("gz", 3)), 2)
    wide_temp = widened[:, 2]
    return section_rates(widened, wide_temp, velocity)


def per_device(tangents, baseline_mass_concentration, baseline_internal_value, base_velocity):
    vectors, fields, planes, span_cells, stream_cells = tangents.shape
    cell_count = float(
        planes * span_cells * stream_cells * lax.axis_size("gx") * lax.axis_size("gz")
    )
    entry_count = float(fields) * cell_count
    mass_gradient_contribution, internal_gradient_contribution = thermal_linearized_gradients(
        baseline_mass_concentration, baseline_internal_value
    )
    rate_one = operate(
        tangents, base_velocity, mass_gradient_contribution, internal_gradient_contribution
    )
    speed_local = jnp.sum(base_velocity * base_velocity)
    speed_total = lax.psum(speed_local, ("gx", "gz"))
    step_size = courant_number / jnp.sqrt(speed_total / cell_count + 1e-05)
    source = tangents + step_size * rate_one
    rate_two = operate(
        source, base_velocity, mass_gradient_contribution, internal_gradient_contribution
    )
    advanced = tangents + 0.5 * step_size * (rate_one + rate_two)
    flattened = advanced.reshape(vectors, -1)
    local_gram = jnp.dot(flattened, flattened.T, precision=lax.Precision.HIGHEST)
    gram_matrix = lax.psum(local_gram, ("gx", "gz")) / entry_count
    chol_lower = jnp.linalg.cholesky(gram_matrix)
    identity = jnp.eye(vectors, dtype=jnp.float32)
    inverse = lax.linalg.triangular_solve(chol_lower, identity, left_side=True, lower=True)
    renormalized = jnp.dot(inverse, flattened, precision=lax.Precision.HIGHEST).reshape(
        advanced.shape
    )
    return (renormalized, jnp.transpose(chol_lower))


def solution(mesh):
    in_specs = (
        P(None, None, None, "gz", "gx"),
        P(None, "gz", "gx"),
        P(None, "gz", "gx"),
        P(None, "gz", "gx"),
    )
    out_specs = (P(None, None, None, "gz", "gx"), P())
    return jax.shard_map(
        per_device, mesh=mesh, in_specs=in_specs, out_specs=out_specs, check_vma=False
    )
```

profile of v0, /device:TPU:1, one launch (start us, length us, event | category | flops | bytes accessed | tf_op | source)
XLA Modules:
  0.0 268.2 jit_solution(8192287550584913324)
XLA Ops:
  0.6 0.9 multiply_multiply_fusion
  1.6 0.8 subtract_divide_fusion
  2.4 1.1 multiply_add_fusion.1
  3.5 1.6 fusion.2
  5.1 0.4 copy.106
  5.5 6.9 %collective-permute-start.1 = (f32[8,3,2,32,2]{3,0,4,2,1:T(8,128)S(1)}, f32[8,3,2,32,2]{3,0,4,2,1:T(8,128)S(1)}, u32[]{:S(2)}, u32[]{:S(2)}) collective-permute-start(f32[8,3,2,32,2]{3,0,4,2,1:T(8,128)S(1)} %copy.106), channel_id=1, source_target_pairs={{32,0},{64,32},{96,64},{128,96},{160,128},{192,160},{224,192},{256... | collective-permute-start | bytes 36872 | tf_op jit(solution)/shard_map/ppermute | solution.py:27
  12.3 0.3 copy.105
  12.7 1.9 collective-permute-start
  14.7 0.5 copy.84
  15.2 4.5 %collective-permute-done = f32[8,3,2,32,2]{3,0,4,2,1:T(8,128)S(1)} collective-permute-done((f32[8,3,2,32,2]{3,0,4,2,1:T(8,128)S(1)}, f32[8,3,2,32,2]{3,0,4,2,1:T(8,128)S(1)}, u32[]{:S(2)}, u32[]{:S(2)}) %collective-permute-start) | collective-permute-done | bytes 12320 | tf_op jit(solution)/shard_map/ppermute | solution.py:26
  19.6 0.4 copy.83
  20.0 0.4 copy.85
  20.4 0.1 pad_maximum_fusion.9
  20.6 6.3 %collective-permute-start.2 = (f32[8,3,2,2,132]{4,0,3,2,1:T(8,128)S(1)}, f32[8,3,2,2,132]{4,0,3,2,1:T(8,128)S(1)}, u32[]{:S(2)}, u32[]{:S(2)}) collective-permute-start(f32[8,3,2,2,132]{4,0,3,2,1:T(8,128)S(1)} %get-tuple-element.16), channel_id=1, source_target_pairs={{0,1},{1,2},{2,3},{3,4},{4,5},{5,6},{6,7},{7,8},{8,9},{9,10},{10,1... | collective-permute-start | bytes 152072 | tf_op jit(solution)/shard_map/ppermute | solution.py:26
  26.9 1.9 collective-permute-start.3
  28.9 0.6 multiply_reduce_fusion
  29.5 101.9 %psum.14 = f32[]{:T(128)} all-reduce(f32[]{:T(128)} %get-tuple-element.28), channel_id=1, replica_groups=mesh['gx'=16,'gz'=32] {'gx','gz'}, use_global_device_ids=true, to_apply=%region_1.2 | all-reduce | flops 1 | bytes 8 | tf_op jit(solution)/shard_map/psum | solution.py:138
  132.1 0.7 pad_maximum_fusion
  133.2 0.6 fusion.13
  133.8 0.7 fusion.20
  134.7 0.3 fusion
  135.0 0.4 copy.107
  135.4 0.4 copy.108
  135.8 4.7 %collective-permute-start.5 = (f32[8,3,2,32,2]{3,0,4,2,1:T(8,128)S(1)}, f32[8,3,2,32,2]{3,0,4,2,1:T(8,128)S(1)}, u32[]{:S(2)}, u32[]{:S(2)}) collective-permute-start(f32[8,3,2,32,2]{3,0,4,2,1:T(8,128)S(1)} %copy.108), channel_id=1, source_target_pairs={{32,0},{64,32},{96,64},{128,96},{160,128},{192,160},{224,192},{256... | collective-permute-start | bytes 36872 | tf_op jit(solution)/shard_map/ppermute | solution.py:27
  140.5 1.9 collective-permute-start.4
  142.5 0.5 copy.91
  142.9 4.5 %collective-permute-done.4 = f32[8,3,2,32,2]{3,0,4,2,1:T(8,128)S(1)} collective-permute-done((f32[8,3,2,32,2]{3,0,4,2,1:T(8,128)S(1)}, f32[8,3,2,32,2]{3,0,4,2,1:T(8,128)S(1)}, u32[]{:S(2)}, u32[]{:S(2)}) %collective-permute-start.4) | collective-permute-done | bytes 12320 | tf_op jit(solution)/shard_map/ppermute | solution.py:26
  147.4 0.4 copy.90
  147.8 0.4 copy.92
  148.2 0.8 pad_maximum_fusion.6
  148.9 5.1 %collective-permute-start.6 = (f32[8,3,2,2,132]{4,0,3,2,1:T(8,128)}, f32[8,3,2,2,132]{4,0,3,2,1:T(8,128)}, u32[]{:S(2)}, u32[]{:S(2)}) collective-permute-start(f32[8,3,2,2,132]{4,0,3,2,1:T(8,128)} %get-tuple-element.14), channel_id=1, source_target_pairs={{0,1},{1,2},{2,3},{3,4},{4,5},{5,6},{6,7},{7,8},{8,9},{9,10},{10,1... | collective-permute-start | bytes 152072 | tf_op jit(solution)/shard_map/ppermute | solution.py:26
  154.0 1.9 collective-permute-start.7
  156.0 5.6 %collective-permute-done.7 = f32[8,3,2,2,132]{4,0,3,2,1:T(8,128)} collective-permute-done((f32[8,3,2,2,132]{4,0,3,2,1:T(8,128)S(1)}, f32[8,3,2,2,132]{4,0,3,2,1:T(8,128)}, u32[]{:S(2)}, u32[]{:S(2)}) %collective-permute-start.7) | collective-permute-done | bytes 50720 | tf_op jit(solution)/shard_map/ppermute | solution.py:27
  161.6 1.6 pad_maximum_fusion.1
  163.4 0.6 fusion.27
  164.2 0.8 fusion.34
  165.0 0.2 fusion.5
  165.2 1.3 convolution_bitcast_fusion.1
  166.5 96.3 %psum.15 = f32[8,8]{0,1:T(8,128)S(1)} all-reduce(f32[8,8]{0,1:T(8,128)S(1)} %convolution_bitcast_fusion.1), channel_id=1, replica_groups=mesh['gx'=16,'gz'=32] {'gx','gz'}, use_global_device_ids=true, to_apply=%region_2.3 | all-reduce | flops 64 | bytes 512 | tf_op jit(solution)/shard_map/psum | solution.py:147
  262.9 0.7 cholesky.17
  263.7 0.6 compare_reduce_fusion
  264.3 0.6 fusion.68
  265.0 0.7 copy.101
  265.6 0.6 custom-call.6
  266.3 0.2 convolution_bitcast_fusion
  266.4 0.3 copy.115
  266.8 0.6 fusion.69
  267.3 0.9 copy.100
  (27 shorter events, 1.4 us)
Async XLA Ops:
  3.5 11.2 %copy-start = (f32[8,2,2,32,128]{4,3,2,1,0:T(8,128)S(1)}, f32[8,2,2,32,128]{4,3,2,1,0:T(8,128)}, u32[]{:S(2)}) copy-start(f32[8,2,2,32,128]{4,3,2,1,0:T(8,128)} %param.4) | copy-start | bytes 1572868
  5.5 14.6 %collective-permute-start.1 = (f32[8,3,2,32,2]{3,0,4,2,1:T(8,128)S(1)}, f32[8,3,2,32,2]{3,0,4,2,1:T(8,128)S(1)}, u32[]{:S(2)}, u32[]{:S(2)}) collective-permute-start(f32[8,3,2,32,2]{3,0,4,2,1:T(8,128)S(1)} %copy.106), channel_id=1, source_target_pairs={{32,0},{64,32},{96,64},{128,96},{160,128},{192,160},{224,192},{256... | collective-permute-start | bytes 36872 | tf_op jit(solution)/shard_map/ppermute | solution.py:27
  12.7 6.9 %collective-permute-start = (f32[8,3,2,32,2]{3,0,4,2,1:T(8,128)S(1)}, f32[8,3,2,32,2]{3,0,4,2,1:T(8,128)S(1)}, u32[]{:S(2)}, u32[]{:S(2)}) collective-permute-start(f32[8,3,2,32,2]{3,0,4,2,1:T(8,128)S(1)} %copy.105), channel_id=1, source_target_pairs={{0,32},{32,64},{64,96},{96,128},{128,160},{160,192},{192,224},{224... | collective-permute-start | bytes 36872 | tf_op jit(solution)/shard_map/ppermute | solution.py:26
  20.0 8.8 %copy-start.1 = (f32[2,32,128]{2,1,0:T(8,128)S(1)}, f32[2,32,128]{2,1,0:T(8,128)}, u32[]{:S(2)}) copy-start(f32[2,32,128]{2,1,0:T(8,128)} %param.7) | copy-start | bytes 98308
  20.6 111.5 %collective-permute-start.2 = (f32[8,3,2,2,132]{4,0,3,2,1:T(8,128)S(1)}, f32[8,3,2,2,132]{4,0,3,2,1:T(8,128)S(1)}, u32[]{:S(2)}, u32[]{:S(2)}) collective-permute-start(f32[8,3,2,2,132]{4,0,3,2,1:T(8,128)S(1)} %get-tuple-element.16), channel_id=1, source_target_pairs={{0,1},{1,2},{2,3},{3,4},{4,5},{5,6},{6,7},{7,8},{8,9},{9,10},{10,1... | collective-permute-start | bytes 152072 | tf_op jit(solution)/shard_map/ppermute | solution.py:26
  26.9 105.1 %collective-permute-start.3 = (f32[8,3,2,2,132]{4,0,3,2,1:T(8,128)S(1)}, f32[8,3,2,2,132]{4,0,3,2,1:T(8,128)S(1)}, u32[]{:S(2)}, u32[]{:S(2)}) collective-permute-start(f32[8,3,2,2,132]{4,0,3,2,1:T(8,128)S(1)} %get-tuple-element.17), channel_id=1, source_target_pairs={{1,0},{2,1},{3,2},{4,3},{5,4},{6,5},{7,6},{8,7},{9,8},{10,9},{11,1... | collective-permute-start | bytes 152072 | tf_op jit(solution)/shard_map/ppermute | solution.py:27
  135.8 12.0 %collective-permute-start.5 = (f32[8,3,2,32,2]{3,0,4,2,1:T(8,128)S(1)}, f32[8,3,2,32,2]{3,0,4,2,1:T(8,128)S(1)}, u32[]{:S(2)}, u32[]{:S(2)}) collective-permute-start(f32[8,3,2,32,2]{3,0,4,2,1:T(8,128)S(1)} %copy.108), channel_id=1, source_target_pairs={{32,0},{64,32},{96,64},{128,96},{160,128},{192,160},{224,192},{256... | collective-permute-start | bytes 36872 | tf_op jit(solution)/shard_map/ppermute | solution.py:27
  140.5 6.9 %collective-permute-start.4 = (f32[8,3,2,32,2]{3,0,4,2,1:T(8,128)S(1)}, f32[8,3,2,32,2]{3,0,4,2,1:T(8,128)S(1)}, u32[]{:S(2)}, u32[]{:S(2)}) collective-permute-start(f32[8,3,2,32,2]{3,0,4,2,1:T(8,128)S(1)} %copy.107), channel_id=1, source_target_pairs={{0,32},{32,64},{64,96},{96,128},{128,160},{160,192},{192,224},{224... | collective-permute-start | bytes 36872 | tf_op jit(solution)/shard_map/ppermute | solution.py:26
  148.9 7.0 %collective-permute-start.6 = (f32[8,3,2,2,132]{4,0,3,2,1:T(8,128)}, f32[8,3,2,2,132]{4,0,3,2,1:T(8,128)}, u32[]{:S(2)}, u32[]{:S(2)}) collective-permute-start(f32[8,3,2,2,132]{4,0,3,2,1:T(8,128)} %get-tuple-element.14), channel_id=1, source_target_pairs={{0,1},{1,2},{2,3},{3,4},{4,5},{5,6},{6,7},{7,8},{8,9},{9,10},{10,1... | collective-permute-start | bytes 152072 | tf_op jit(solution)/shard_map/ppermute | solution.py:26
  154.0 7.5 %collective-permute-start.7 = (f32[8,3,2,2,132]{4,0,3,2,1:T(8,128)S(1)}, f32[8,3,2,2,132]{4,0,3,2,1:T(8,128)}, u32[]{:S(2)}, u32[]{:S(2)}) collective-permute-start(f32[8,3,2,2,132]{4,0,3,2,1:T(8,128)S(1)} %get-tuple-element.15), channel_id=1, source_target_pairs={{1,0},{2,1},{3,2},{4,3},{5,4},{6,5},{7,6},{8,7},{9,8},{10,9},{11,1... | collective-permute-start | bytes 152072 | tf_op jit(solution)/shard_map/ppermute | solution.py:27
where the time goes:
time: 269 us; the launch traced here: 268 us
  blocking collectives  198 us (74%)
  starting transfers between devices  30.7 us (11%)
  waiting for transfers between devices  14.6 us (5%)
  other arithmetic  14.3 us (5%)
  local copies, waits for them, and re-layouts  6.75 us (3%)
    psum x1, blocking collectives, per_device(): speed_total = lax.psum(speed_local, ('gx', 'gz'))  102 us
    psum x1, blocking collectives, per_device(): gram_matrix = lax.psum(local_gram, ('gx', 'gz')) / entry_count  96.3 us
    ppermute x4, starting transfers between devices, with_halo(): after = lax.ppermute(initial, axis, down)  15.4 us
    ppermute x4, starting transfers between devices, with_halo(): before = lax.ppermute(last, axis, up)  15.3 us
    ppermute x4, waiting for transfers between devices, with_halo(): before = lax.ppermute(last, axis, up)  8.95 us
    ppermute x4, waiting for transfers between devices, with_halo(): after = lax.ppermute(initial, axis, down)  5.61 us
  transfers between devices with their start and end apart: 8, of which 3 were waited for; matrix products, arithmetic and copies ran while one was open for 1% of the time, Pallas kernels for 0%

commit v1 on v0

v1 whole, which is shorter than its diff:
```python
import functools

import jax
import jax.numpy as jnp
from jax import lax
from jax.experimental import pallas as pl
from jax.experimental.pallas import tpu as pltpu
from jax.sharding import Mesh, PartitionSpec as P

NEWTON = 4
isochoric_warmth_coefficient = 3.0
attraction = 0.5
acentric_coefficient_gradient = 0.6
covolume = 0.15
root_two = 1.4142135623730951
viscosity = 0.2
conductivity = 1.0
courant_number = 0.5

K = 8
NF = 4 * K
NC = 6
NA = NF + NC
Z = 32
X = 128
TOP = 8
ZE = Z + 16
GX = ("xh", "xl")
GZ = ("zh", "zl")
NEAR = ("xl", "zl")
FAR = ("xh", "zh")
WIRE = 168


def departure(cell_mass_concentration):
    low_term = 1.0 + (1.0 - root_two) * covolume * cell_mass_concentration
    high_term = 1.0 + (1.0 + root_two) * covolume * cell_mass_concentration
    factor = attraction * (1.0 + acentric_coefficient_gradient) / (2.0 * root_two * covolume)
    value = factor * (jnp.log(low_term) - jnp.log(high_term))
    slope = factor * (
        (1.0 - root_two) * covolume / low_term - (1.0 + root_two) * covolume / high_term
    )
    return (value, slope)


def slopes(mass, internal):
    deviation, departure_slope = departure(mass)
    warmth = internal / isochoric_warmth_coefficient
    for _ in range(NEWTON):
        root = jnp.sqrt(warmth)
        multiplier = 1.0 + acentric_coefficient_gradient * (1.0 - root)
        mismatch = isochoric_warmth_coefficient * warmth + deviation * multiplier - internal
        gradient = isochoric_warmth_coefficient - deviation * acentric_coefficient_gradient / (
            2.0 * root
        )
        warmth = warmth - mismatch / gradient
    root = jnp.sqrt(warmth)
    multiplier = 1.0 + acentric_coefficient_gradient * (1.0 - root)
    gradient = isochoric_warmth_coefficient - deviation * acentric_coefficient_gradient / (
        2.0 * root
    )
    energy = 1.0 / gradient
    return (-departure_slope * multiplier * energy, energy)


def lanes():
    return lax.broadcasted_iota(jnp.int32, (8, X), 1)


def prep_kernel(q_ref, mass_ref, internal_ref, velocity_ref, coef_ref, pack_ref):
    density, energy = slopes(mass_ref[...], internal_ref[...])
    coef_ref[0:2] = density
    coef_ref[2:4] = energy
    coef_ref[4:6] = velocity_ref[...]
    group = ((lanes() + 4) >> 3) & 15
    for b in range(3):
        for t in range(Z // 8):
            rows = slice(8 * t, 8 * t + 8)
            acc = jnp.zeros((8, X), jnp.float32)
            for i in range(16 if b < 2 else NC):
                field = q_ref[16 * b + i, rows, :] if b < 2 else coef_ref[i, rows, :]
                moved = pltpu.roll(field, 8 * i, 1) if i else field
                acc = jnp.where(group == i, moved, acc)
            pack_ref[b, rows, :] = acc


def wire_kernel(q_ref, coef_ref, left_ref, right_ref, side_ref, up_ref, down_ref):
    low = (lanes() & 7) < 4
    for b in range(3):
        for t in range(Z // 8):
            rows = slice(8 * t, 8 * t + 8)
            side_ref[b, rows, :] = jnp.where(low, right_ref[b, rows, :], left_ref[b, rows, :])
    for f in range(NA):
        ref, i = (q_ref, f) if f < NF else (coef_ref, f - NF)
        up_ref[4 * f : 4 * f + 4, :] = ref[i, 0:4, :]
        down_ref[4 * f : 4 * f + 4, :] = ref[i, Z - 4 : Z, :]
    for b in range(3):
        r = 4 * NA + 4 * b
        up_ref[r : r + 4, :] = side_ref[b, 0:4, :]
        down_ref[r : r + 4, :] = side_ref[b, Z - 4 : Z, :]
    r = 4 * NA + 12
    up_ref[r:WIRE, :] = jnp.zeros((WIRE - r, X), jnp.float32)
    down_ref[r:WIRE, :] = jnp.zeros((WIRE - r, X), jnp.float32)


def shifted(main, side, lane, both):
    out_main, out_side = [], []
    for d, edge in ((1, lane < 1), (X - 1, lane >= X - 1), (2, lane < 2), (X - 2, lane >= X - 2)):
        moved, turned = pltpu.roll(main, d, 1), pltpu.roll(side, d, 1)
        out_main.append(jnp.where(edge, turned, moved))
        if both:
            out_side.append(jnp.where(edge, moved, turned))
    return out_main, out_side


def stencil_kernel(
    q_ref, coef_ref, side_ref, above_ref, below_ref, a_ref, b_ref, sums_ref,
    em, eh, sm, wm, am, ah, red,
):
    f32 = jnp.float32
    lane = lanes()
    for f in range(NA):
        ref, i = (q_ref, f) if f < NF else (coef_ref, f - NF)
        em[f, TOP - 4 : TOP, :] = above_ref[4 * f : 4 * f + 4, :]
        for t in range(Z // 8):
            em[f, TOP + 8 * t : TOP + 8 * t + 8, :] = ref[i, 8 * t : 8 * t + 8, :]
        em[f, TOP + Z : TOP + Z + 4, :] = below_ref[4 * f : 4 * f + 4, :]
    for b in range(3):
        r = 4 * NA + 4 * b
        sm[b, TOP - 4 : TOP, :] = above_ref[r : r + 4, :]
        sm[b, TOP : TOP + Z, :] = side_ref[b]
        sm[b, TOP + Z : TOP + Z + 4, :] = below_ref[r : r + 4, :]
    for f in range(NA):
        b, i = f // 16, f % 16
        for t in range(5):
            rows = slice(4 + 8 * t, 12 + 8 * t)
            part = sm[b, rows, :]
            eh[f, rows, :] = pltpu.roll(part, X - 8 * i, 1) if i else part

    chunks_t = (4, 12, 20, 28, 36)
    chunks_a = (6, 14, 22, 30, 34)

    def temperature(dst_m, dst_h, src_m, src_h, base, slot, chunks):
        for y in range(2):
            for r in chunks:
                rows = pl.ds(r, 8)
                for dst, src, coef in ((dst_m, src_m, em), (dst_h, src_h, eh)):
                    dst[slot + y, rows, :] = (
                        coef[NF + y, rows, :] * src[base + y, rows, :]
                        + coef[NF + 2 + y, rows, :] * src[base + 2 + y, rows, :]
                    )

    def operate(src_m, src_h, tm, th, base, slot, y, r, both):
        rows = pl.ds(r, 8)
        other = 1 - y
        outs = []

        def loads(pair, i):
            return [p[i, rows, :] for p in pair]

        def along_z(p, i):
            one = p[i, pl.ds(r - 1, 8), :] + p[i, pl.ds(r + 1, 8), :]
            two = p[i, pl.ds(r - 2, 8), :] + p[i, pl.ds(r + 2, 8), :]
            return one, two

        def mix(ones, twos, center):
            return 16.0 * ones - twos - 90.0 * center

        rm, rh = loads((src_m, src_h), base + y)
        dm, dh = loads((src_m, src_h), base + 2 + y)
        cm, ch = loads((tm, th), slot + y)
        xr = shifted(rm, rh, lane, both)
        xe = shifted(dm, dh, lane, both)
        xt = shifted(cm, ch, lane, both)
        for s in range(2 if both else 1):
            src, tmp, coef = ((src_m, tm, em), (src_h, th, eh))[s]
            r1, r2, r3, r4 = xr[s]
            e1, e2, e3, e4 = xe[s]
            t1, t2, t3, t4 = xt[s]
            speed = coef[NF + 4 + y, rows, :] * (-1.0 / 12.0)
            z1, z2 = along_z(src, base + y)
            lap_r = mix(r1 + r2 + z1 + src[base + other, rows, :], r3 + r4 + z2, (rm, rh)[s])
            z1, z2 = along_z(tmp, slot + y)
            lap_t = mix(t1 + t2 + z1 + tmp[slot + other, rows, :], t3 + t4 + z2, (cm, ch)[s])
            rate_r = speed * (8.0 * (r2 - r1) - (r4 - r3)) + (viscosity / 12.0) * lap_r
            rate_e = speed * (8.0 * (e2 - e1) - (e4 - e3)) + (conductivity / 12.0) * lap_t
            outs.append((rate_r, rate_e))
        return outs

    def vector(k, carry):
        base = 4 * k
        temperature(wm.at[0], wm.at[1], em, eh, base, 0, chunks_t)
        for y in range(2):
            for r in chunks_a:
                rows = pl.ds(r, 8)
                (mr, me), (hr, he) = operate(em, eh, wm.at[0], wm.at[1], base, 0, y, r, True)
                am[base + y, rows, :] = mr
                am[base + 2 + y, rows, :] = me
                ah[base + y, rows, :] = hr
                ah[base + 2 + y, rows, :] = he
        temperature(wm.at[0], wm.at[1], am, ah, base, 2, chunks_a)
        for y in range(2):
            for t in range(Z // 8):
                out = operate(am, ah, wm.at[0], wm.at[1], base, 2, y, TOP + 8 * t, False)
                for c in range(2):
                    b_ref[base + 2 * c + y, 8 * t : 8 * t + 8, :] = out[0][c]
                    a_ref[base + 2 * c + y, 8 * t : 8 * t + 8, :] = am[
                        base + 2 * c + y, TOP + 8 * t : TOP + 8 * t + 8, :
                    ]
        return carry

    lax.fori_loop(0, K, vector, 0)

    result = jnp.zeros((8, X), f32)
    red[...] = jnp.zeros_like(red)
    for k in range(K):
        for m in range(5 if k < 4 else 4):
            l = (k + m) % K

            def tile(j, acc, k=k, l=l):
                p, t = j // 4, j % 4
                rows = pl.ds(pl.multiple_of(8 * t, 8), 8)
                qk, ak, bk = (v[4 * k + p, rows, :] for v in (q_ref, a_ref, b_ref))
                ql, al, bl = (v[4 * l + p, rows, :] for v in (q_ref, a_ref, b_ref))
                s0, s1, s2, s3, s4 = acc
                return (
                    s0 + qk * ql,
                    s1 + qk * al + ak * ql,
                    s2 + ak * al + 0.5 * (qk * bl + bk * ql),
                    s3 + 0.5 * (ak * bl + bk * al),
                    s4 + 0.25 * (bk * bl),
                )

            acc = (jnp.zeros((8, X), f32),) * 5
            acc = lax.fori_loop(0, 16, tile, acc, unroll=True)
            for n in range(5):
                red[8 * n + m, k : k + 1, :] = jnp.sum(acc[n], axis=0, keepdims=True)
    for n in range(5):
        for m in range(5):
            col = jnp.sum(red[8 * n + m], axis=1, keepdims=True)
            result = jnp.where(lane == 8 * n + m, col, result)
    speed = jnp.zeros((8, X), f32)
    for y in range(2):
        for t in range(Z // 8):
            v = coef_ref[4 + y, 8 * t : 8 * t + 8, :]
            speed = speed + v * v
    result = jnp.where(lane == 40, jnp.sum(speed, axis=1, keepdims=True), result)
    for n in range(sums_ref.shape[0]):
        sums_ref[n] = result


def finish_kernel(cells, q_ref, a_ref, b_ref, sums_ref, out_ref, growth_ref):
    f32 = jnp.float32
    lane = lanes()
    row = lax.broadcasted_iota(jnp.int32, (8, X), 0)
    total = sums_ref[0]
    for n in range(1, sums_ref.shape[0]):
        total = total + sums_ref[n]
    speed = jnp.broadcast_to(jnp.sum(total[:, 40:41], axis=0, keepdims=True), (8, X))
    step = courant_number / jnp.sqrt(speed * (1.0 / cells) + 1e-05)
    gram = total
    power = step
    for n in range(1, 5):
        gram = gram + power * pltpu.roll(total, X - 8 * n, 1)
        power = power * step
    gram = gram * (1.0 / (2.0 * cells))
    cols = [jnp.broadcast_to(gram[:, m : m + 1], (8, X)) for m in range(5)]

    def entry(i, j):
        k, m = (j, i - j) if i - j <= 4 else (i, j - i + K)
        if m == 4:
            k = min(i, j)
        return jnp.broadcast_to(cols[m][k : k + 1, :], (8, X))

    low = [[None] * K for _ in range(K)]
    inv_diag = []
    for j in range(K):
        d = entry(j, j)
        for p in range(j):
            d = d - low[j][p] * low[j][p]
        root = jnp.sqrt(d)
        low[j][j] = root
        inv_diag.append(1.0 / root)
        for i in range(j + 1, K):
            v = entry(i, j)
            for p in range(j):
                v = v - low[i][p] * low[j][p]
            low[i][j] = v * inv_diag[j]
    inverse = [[None] * K for _ in range(K)]
    for j in range(K):
        inverse[j][j] = inv_diag[j]
        for i in range(j + 1, K):
            v = low[i][j] * inverse[j][j]
            for p in range(j + 1, i):
                v = v + low[i][p] * inverse[p][j]
            inverse[i][j] = -v * inv_diag[i]
    growth = jnp.zeros((8, X), f32)
    for i in range(K):
        for j in range(i + 1):
            growth = jnp.where((row == j) & (lane == i), low[i][j], growth)
    growth_ref[...] = growth
    half = 0.5 * step * step
    for p in range(4):
        for t in range(Z // 8):
            rows = slice(8 * t, 8 * t + 8)
            adv = [
                q_ref[4 * k + p, rows, :]
                + step * a_ref[4 * k + p, rows, :]
                + half * b_ref[4 * k + p, rows, :]
                for k in range(K)
            ]
            for k in range(K):
                v = inverse[k][0] * adv[0]
                for j in range(1, k + 1):
                    v = v + inverse[k][j] * adv[j]
                out_ref[4 * k + p, rows, :] = v


def call(body, outs, scratch=(), flops=1000000):
    shapes = [jax.ShapeDtypeStruct(s, jnp.float32) for s in outs]
    return pl.pallas_call(
        body,
        out_shape=shapes,
        scratch_shapes=[pltpu.VMEM(s, jnp.float32) for s in scratch],
        compiler_params=pltpu.CompilerParams(vmem_limit_bytes=24 * 1024 * 1024),
        cost_estimate=pl.CostEstimate(flops=flops, bytes_accessed=1000000, transcendentals=0),
    )


def ring(array, axes, step):
    size = lax.axis_size(axes)
    return lax.ppermute(array, axes, [(i, (i + step) % size) for i in range(size)])


def gathered(array, axes):
    return lax.all_to_all(array, axes, 0, 0)


def per_device(tangents, mass, internal, velocity):
    cells = float(2 * Z * X * lax.axis_size(GX) * lax.axis_size(GZ))
    near, far = lax.axis_size(NEAR), lax.axis_size(FAR)
    q = tangents.reshape(NF, Z, X)
    coef, pack = call(prep_kernel, [(NC, Z, X), (3, Z, X)])(q, mass, internal, velocity)
    left = ring(pack, GX, 1)
    right = ring(pack, GX, -1)
    side, up, down = call(wire_kernel, [(3, Z, X), (WIRE, X), (WIRE, X)])(q, coef, left, right)
    above = ring(down, GZ, 1)
    below = ring(up, GZ, -1)
    ext = (NA, ZE, X)
    rate, second, sums = call(
        stencil_kernel,
        [(NF, Z, X), (NF, Z, X), (near, 8, X)],
        [ext, ext, (3, ZE, X), (2, 4, ZE, X), (NF, ZE, X), (NF, ZE, X), (40, 8, X)],
    )(q, coef, side, above, below)
    sums = jnp.sum(gathered(sums, NEAR), axis=0)
    sums = gathered(jnp.broadcast_to(sums, (far, 8, X)), FAR)
    out, growth = call(functools.partial(finish_kernel, cells), [(NF, Z, X), (8, X)])(
        q, rate, second, sums
    )
    return (out.reshape(tangents.shape), growth[:, :K])


def solution(mesh):
    gx, gz = mesh.devices.shape
    fine = Mesh(mesh.devices.reshape(gx // 4, 4, gz // 4, 4), GX + GZ)
    in_specs = (P(None, None, None, GZ, GX),) + (P(None, GZ, GX),) * 3
    out_specs = (P(None, None, None, GZ, GX), P())
    return jax.shard_map(
        per_device, mesh=fine, in_specs=in_specs, out_specs=out_specs, check_vma=False
    )
```

time: 269 us -> 74.2 us (0.28)
  blocking collectives: 198 us -> 33.5 us
  other arithmetic: 14.3 us -> 0.02 us
  starting transfers between devices: 30.7 us -> 17 us
  Pallas kernels: 0 us -> 8.36 us
  waiting for transfers between devices: 14.6 us -> 10.7 us
  local copies, waits for them, and re-layouts: 6.75 us -> 3.33 us
    psum x2 -> x0, blocking collectives: 198 us -> none  [the longest x1 102 us: per_device(): speed_total = lax.psum(speed_local, ('gx', 'gz'))]
    all_to_all x0 -> x2, blocking collectives: none -> 33.5 us  [gathered(): return lax.all_to_all(array, axes, 0, 0)]
    ppermute x8 -> x4, starting transfers between devices: 30.7 us -> 17 us  [ring(): lax.ppermute(array, axes, [(i, (i + step) % size) for i in range(size)])]
    pallas_call x0 -> x4, Pallas kernels: none -> 8.36 us  [the longest x1 6.77 us: per_device(): call(stencil_kernel, [(NF, Z, X), (NF, Z, X), (near, 8, X)], [ext, ext, (...]
    another operation x8 -> x0, other arithmetic: 4.63 us -> none  [the longest x4 2.61 us: section_rates(): return jnp.stack([rate_density, rate_energy], axis=1)]
    concatenate x6 -> x0, other arithmetic: 4.35 us -> none  [the longest x2 2.29 us: with_halo(): array = jnp.concatenate([before, array, after], axis=dim)]
    ppermute x8 -> x4, waiting for transfers between devices: 14.6 us -> 10.7 us  [ring(): lax.ppermute(array, axes, [(i, (i + step) % size) for i in range(size)])]
  transfers between devices with their start and end apart: 8 -> 4, of which waited for: 3 -> 2; matrix products, arithmetic and copies ran while one was open for 1% -> 0% of each run, Pallas kernels for 0% -> 0%
where the time goes in v1:
time: 74.2 us; the launch traced here: 73.7 us
  blocking collectives  33.5 us (45%)
  starting transfers between devices  17 us (23%)
  waiting for transfers between devices  10.7 us (14%)
  Pallas kernels  8.36 us (11%)
  local copies, waits for them, and re-layouts  3.33 us (4%)
    all_to_all x2, blocking collectives, gathered(): return lax.all_to_all(array, axes, 0, 0)  33.5 us
    ppermute x4, starting transfers between devices, ring(): lax.ppermute(array, axes, [(i, (i + step) % size) for i in range(size)])  17 us
    ppermute x4, waiting for transfers between devices, ring(): lax.ppermute(array, axes, [(i, (i + step) % size) for i in range(size)])  10.7 us
    pallas_call x1, Pallas kernels, per_device(): call(stencil_kernel, [(NF, Z, X), (NF, Z, X), (near, 8, X)], [ext, ext, (...  6.77 us
    unnamed x10, local copies, waits for them, and re-layouts  3.31 us
  transfers between devices with their start and end apart: 4, of which 2 were waited for; matrix products, arithmetic and copies ran while one was open for 0% of the time, Pallas kernels for 0%

profile of v1, /device:TPU:1, one launch (start us, length us, event | category | flops | bytes accessed | tf_op | source)
XLA Modules:
  0.0 73.7 jit_solution(1711953978622209256)
XLA Ops:
  0.6 0.0 copy-start
  0.6 1.0 %copy-done = f32[8,2,2,32,128]{4,3,2,1,0:T(8,128)S(1)} copy-done((f32[8,2,2,32,128]{4,3,2,1,0:T(8,128)S(1)}, f32[8,2,2,32,128]{4,3,2,1,0:T(8,128)}, u32[]{:S(2)}) %copy-start) | copy-done | bytes 524312
  1.7 0.0 copy-start.2
  1.7 0.8 %copy-done.2 = f32[2,32,128]{2,1,0:T(8,128)S(1)} copy-done((f32[2,32,128]{2,1,0:T(8,128)S(1)}, f32[2,32,128]{2,1,0:T(8,128)}, u32[]{:S(2)}) %copy-start.2) | copy-done | bytes 32792
  2.4 0.0 copy-start.3
  2.4 0.8 %copy-done.3 = f32[2,32,128]{2,1,0:T(8,128)S(1)} copy-done((f32[2,32,128]{2,1,0:T(8,128)S(1)}, f32[2,32,128]{2,1,0:T(8,128)}, u32[]{:S(2)}) %copy-start.3) | copy-done | bytes 32792
  3.2 0.0 copy-start.4
  3.2 0.8 %copy-done.4 = f32[2,32,128]{2,1,0:T(8,128)S(1)} copy-done((f32[2,32,128]{2,1,0:T(8,128)S(1)}, f32[2,32,128]{2,1,0:T(8,128)}, u32[]{:S(2)}) %copy-start.4) | copy-done | bytes 32792
  4.0 0.3 shard_map.59
  4.2 6.9 %collective-permute-start.1 = (f32[3,32,128]{2,1,0:T(8,128)S(1)}, f32[3,32,128]{2,1,0:T(8,128)S(1)}, u32[]{:S(2)}, u32[]{:S(2)}) collective-permute-start(f32[3,32,128]{2,1,0:T(8,128)S(1)} %get-tuple-element.13), channel_id=1, source_target_pairs={{0,480},{32,0},{64,32},{96,64},{128,96},{160,128},{192,160},{224,1... | collective-permute-start | bytes 147464 | tf_op jit(solution)/shard_map/ppermute | solution.py:332
  11.1 1.9 %collective-permute-start = (f32[3,32,128]{2,1,0:T(8,128)S(1)}, f32[3,32,128]{2,1,0:T(8,128)S(1)}, u32[]{:S(2)}, u32[]{:S(2)}) collective-permute-start(f32[3,32,128]{2,1,0:T(8,128)S(1)} %get-tuple-element.13), channel_id=1, source_target_pairs={{0,32},{32,64},{64,96},{96,128},{128,160},{160,192},{192,224},{224... | collective-permute-start | bytes 147464 | tf_op jit(solution)/shard_map/ppermute | solution.py:332
  13.0 0.0 collective-permute-done.1.right_ref
  13.0 5.0 %collective-permute-done.left_ref = f32[3,32,128]{2,1,0:T(8,128)S(1)} collective-permute-done((f32[3,32,128]{2,1,0:T(8,128)S(1)}, f32[3,32,128]{2,1,0:T(8,128)S(1)}, u32[]{:S(2)}, u32[]{:S(2)}) %collective-permute-start) | collective-permute-done | bytes 49184 | tf_op jit(solution)/shard_map/ppermute | solution.py:332
  18.1 6.3 %collective-permute-start.2 = (f32[168,128]{1,0:T(8,128)S(1)}, f32[168,128]{1,0:T(8,128)S(1)}, u32[]{:S(2)}, u32[]{:S(2)}) collective-permute-start(f32[168,128]{1,0:T(8,128)S(1)} %get-tuple-element.15), channel_id=1, source_target_pairs={{0,1},{1,2},{2,3},{3,4},{4,5},{5,6},{6,7},{7,8},{8,9},{9,10},{10,1... | collective-permute-start | bytes 258056 | tf_op jit(solution)/shard_map/ppermute | solution.py:332
  24.4 1.9 %collective-permute-start.3 = (f32[168,128]{1,0:T(8,128)S(1)}, f32[168,128]{1,0:T(8,128)S(1)}, u32[]{:S(2)}, u32[]{:S(2)}) collective-permute-start(f32[168,128]{1,0:T(8,128)S(1)} %get-tuple-element.16), channel_id=1, source_target_pairs={{0,31},{1,0},{2,1},{3,2},{4,3},{5,4},{6,5},{7,6},{8,7},{9,8},{10,9... | collective-permute-start | bytes 258056 | tf_op jit(solution)/shard_map/ppermute | solution.py:332
  26.4 0.0 collective-permute-done.2.above_ref
  26.4 5.7 %collective-permute-done.3.below_ref = f32[168,128]{1,0:T(8,128)S(1)} collective-permute-done((f32[168,128]{1,0:T(8,128)S(1)}, f32[168,128]{1,0:T(8,128)S(1)}, u32[]{:S(2)}, u32[]{:S(2)}) %collective-permute-start.3) | collective-permute-done | bytes 86048 | tf_op jit(solution)/shard_map/ppermute | solution.py:332
  32.0 0.0 copy-start.1
  32.0 6.8 %shard_map.61 = (f32[32,32,128]{2,1,0:T(8,128)S(1)}, f32[32,32,128]{2,1,0:T(8,128)S(1)}, f32[16,8,128]{2,1,0:T(8,128)S(1)}) custom-call(f32[32,32,128]{2,1,0:T(8,128)S(1)} %bitcast.5, f32[6,32,128]{2,1,0:T(8,128)S(1)} %get-tuple-element.12.coef_ref, f32[3,32,128]{2,1,0:T(8,128)S(1)} %get-tuple-element.14.side_ref, ...), custom_call_target="tpu_custom_call" | custom-call | flops 1000000 | bytes 1000000 | tf_op jit(solution)/shard_map/pallas_call | solution.py:350
  38.8 11.6 %all_to_all.10 = f32[16,8,128]{2,1,0:T(8,128)S(1)} all-to-all(f32[16,8,128]{2,1,0:T(8,128)S(1)} %get-tuple-element.19), channel_id=1, replica_groups=mesh['xh'=4,'xl'=4,'zh'=8,'zl'=4] {'xl','zl'}, dimensions={0} | all-to-all | bytes 131072 | tf_op jit(solution)/shard_map/all_to_all | solution.py:336
  50.4 22.0 %all_to_all.11.sums_ref = f32[32,8,128]{2,1,0:T(8,128)S(1)} all-to-all(f32[32,8,128]{2,1,0:T(8,128)S(1)} %broadcast_in_dim.3), channel_id=1, replica_groups=mesh['xh'=4,'xl'=4,'zh'=8,'zl'=4] {'xh','zh'}, dimensions={0} | all-to-all | bytes 262144 | tf_op jit(solution)/shard_map/all_to_all | solution.py:336
  72.4 0.0 copy-done.1
  72.4 1.3 %shard_map.62 = (f32[32,32,128]{2,1,0:T(8,128)}, f32[8,128]{1,0:T(8,128)}) custom-call(f32[32,32,128]{2,1,0:T(8,128)S(1)} %bitcast.6, f32[32,32,128]{2,1,0:T(8,128)S(1)} %get-tuple-element.17.a_ref, f32[32,32,128]{2,1,0:T(8,128)S(1)} %get-tuple-element.18.b_ref, f32[32,8,128]{2,1,0:T(8,128)S(1)} %all_to_all.11.sums_ref), custom_call_target="tpu_custom_call" | custom-call | flops 1000000 | bytes 1000000 | tf_op jit(solution)/shard_map/pallas_call | solution.py:357
  (3 shorter events, 0.1 us)
Async XLA Ops:
  0.6 1.0 %copy-start = (f32[8,2,2,32,128]{4,3,2,1,0:T(8,128)S(1)}, f32[8,2,2,32,128]{4,3,2,1,0:T(8,128)}, u32[]{:S(2)}) copy-start(f32[8,2,2,32,128]{4,3,2,1,0:T(8,128)} %param.4) | copy-start | bytes 1572868
  1.7 0.8 %copy-start.2 = (f32[2,32,128]{2,1,0:T(8,128)S(1)}, f32[2,32,128]{2,1,0:T(8,128)}, u32[]{:S(2)}) copy-start(f32[2,32,128]{2,1,0:T(8,128)} %mass_ref.1) | copy-start | bytes 98308
  2.4 0.8 %copy-start.3 = (f32[2,32,128]{2,1,0:T(8,128)S(1)}, f32[2,32,128]{2,1,0:T(8,128)}, u32[]{:S(2)}) copy-start(f32[2,32,128]{2,1,0:T(8,128)} %internal_ref.1) | copy-start | bytes 98308
  3.2 0.8 %copy-start.4 = (f32[2,32,128]{2,1,0:T(8,128)S(1)}, f32[2,32,128]{2,1,0:T(8,128)}, u32[]{:S(2)}) copy-start(f32[2,32,128]{2,1,0:T(8,128)} %velocity_ref.1) | copy-start | bytes 98308
  4.2 8.8 %collective-permute-start.1 = (f32[3,32,128]{2,1,0:T(8,128)S(1)}, f32[3,32,128]{2,1,0:T(8,128)S(1)}, u32[]{:S(2)}, u32[]{:S(2)}) collective-permute-start(f32[3,32,128]{2,1,0:T(8,128)S(1)} %get-tuple-element.13), channel_id=1, source_target_pairs={{0,480},{32,0},{64,32},{96,64},{128,96},{160,128},{192,160},{224,1... | collective-permute-start | bytes 147464 | tf_op jit(solution)/shard_map/ppermute | solution.py:332
  11.1 6.9 %collective-permute-start = (f32[3,32,128]{2,1,0:T(8,128)S(1)}, f32[3,32,128]{2,1,0:T(8,128)S(1)}, u32[]{:S(2)}, u32[]{:S(2)}) collective-permute-start(f32[3,32,128]{2,1,0:T(8,128)S(1)} %get-tuple-element.13), channel_id=1, source_target_pairs={{0,32},{32,64},{64,96},{96,128},{128,160},{160,192},{192,224},{224... | collective-permute-start | bytes 147464 | tf_op jit(solution)/shard_map/ppermute | solution.py:332
  18.1 8.3 %collective-permute-start.2 = (f32[168,128]{1,0:T(8,128)S(1)}, f32[168,128]{1,0:T(8,128)S(1)}, u32[]{:S(2)}, u32[]{:S(2)}) collective-permute-start(f32[168,128]{1,0:T(8,128)S(1)} %get-tuple-element.15), channel_id=1, source_target_pairs={{0,1},{1,2},{2,3},{3,4},{4,5},{5,6},{6,7},{7,8},{8,9},{9,10},{10,1... | collective-permute-start | bytes 258056 | tf_op jit(solution)/shard_map/ppermute | solution.py:332
  24.4 7.6 %collective-permute-start.3 = (f32[168,128]{1,0:T(8,128)S(1)}, f32[168,128]{1,0:T(8,128)S(1)}, u32[]{:S(2)}, u32[]{:S(2)}) collective-permute-start(f32[168,128]{1,0:T(8,128)S(1)} %get-tuple-element.16), channel_id=1, source_target_pairs={{0,31},{1,0},{2,1},{3,2},{4,3},{5,4},{6,5},{7,6},{8,7},{9,8},{10,9... | collective-permute-start | bytes 258056 | tf_op jit(solution)/shard_map/ppermute | solution.py:332
  32.0 40.3 %copy-start.1 = (f32[8,2,2,32,128]{4,3,2,1,0:T(8,128)S(1)}, f32[8,2,2,32,128]{4,3,2,1,0:T(8,128)}, u32[]{:S(2)}) copy-start(f32[8,2,2,32,128]{4,3,2,1,0:T(8,128)} %param.4) | copy-start | bytes 1572868

commit v2 on v1

v2 whole, which is shorter than its diff:
```python
import functools

import jax
import jax.numpy as jnp
from jax import lax
from jax.experimental import pallas as pl
from jax.experimental.pallas import tpu as pltpu
from jax.sharding import Mesh, PartitionSpec as P

NEWTON = 4
isochoric_warmth_coefficient = 3.0
attraction = 0.5
acentric_coefficient_gradient = 0.6
covolume = 0.15
root_two = 1.4142135623730951
viscosity = 0.2
conductivity = 1.0
courant_number = 0.5

K = 8
NF = 4 * K
NC = 6
NA = NF + NC
Z = 32
X = 128
GX = ("xh", "xl")
GZ = ("zh", "zl")
NEAR = ("xl", "zl")
FAR = ("xh", "zh")
F32 = jnp.float32


def departure(cell_mass_concentration):
    low_term = 1.0 + (1.0 - root_two) * covolume * cell_mass_concentration
    high_term = 1.0 + (1.0 + root_two) * covolume * cell_mass_concentration
    factor = attraction * (1.0 + acentric_coefficient_gradient) / (2.0 * root_two * covolume)
    value = factor * (jnp.log(low_term) - jnp.log(high_term))
    slope = factor * (
        (1.0 - root_two) * covolume / low_term - (1.0 + root_two) * covolume / high_term
    )
    return (value, slope)


def slopes(mass, internal):
    deviation, departure_slope = departure(mass)
    warmth = internal / isochoric_warmth_coefficient
    for _ in range(NEWTON):
        root = jnp.sqrt(warmth)
        multiplier = 1.0 + acentric_coefficient_gradient * (1.0 - root)
        mismatch = isochoric_warmth_coefficient * warmth + deviation * multiplier - internal
        gradient = isochoric_warmth_coefficient - deviation * acentric_coefficient_gradient / (
            2.0 * root
        )
        warmth = warmth - mismatch / gradient
    root = jnp.sqrt(warmth)
    multiplier = 1.0 + acentric_coefficient_gradient * (1.0 - root)
    gradient = isochoric_warmth_coefficient - deviation * acentric_coefficient_gradient / (
        2.0 * root
    )
    energy = 1.0 / gradient
    return (-departure_slope * multiplier * energy, energy)


def lanes():
    return lax.broadcasted_iota(jnp.int32, (8, X), 1)


def tile(t):
    return slice(8 * t, 8 * t + 8)


def prep_kernel(
    q_hbm, mass_hbm, internal_hbm, velocity_hbm, q_ref, coef_ref, pack_ref, mass, internal, sems
):
    copies = [
        pltpu.make_async_copy(src, dst, sems.at[i])
        for i, (src, dst) in enumerate(
            (
                (mass_hbm, mass),
                (internal_hbm, internal),
                (velocity_hbm, coef_ref.at[pl.ds(4, 2)]),
                (q_hbm, q_ref),
            )
        )
    ]
    for copy in copies:
        copy.start()
    copies[0].wait()
    copies[1].wait()
    density, energy = slopes(mass[...], internal[...])
    coef_ref[0:2] = density
    coef_ref[2:4] = energy
    copies[2].wait()
    copies[3].wait()
    group = lanes() >> 3
    for b in range(3):
        for t in range(Z // 8):
            acc = jnp.zeros((8, X), F32)
            for i in range(16 if b < 2 else NC):
                field = q_ref[16 * b + i, tile(t), :] if b < 2 else coef_ref[i, tile(t), :]
                moved = pltpu.roll(field, 8 * i, 1) if i else field
                acc = jnp.where(group == i, moved, acc)
            pack_ref[b, tile(t), :] = acc


def pairs():
    return [(k, m, (k + m) % K) for k in range(K) for m in range(5 if k < 4 else 4)]


def columns(result, lane, red, sets):
    for n in sets:
        for m in range(5):
            col = jnp.sum(red[8 * n + m], axis=1, keepdims=True)
            result = jnp.where(lane == 8 * n + m, col, result)
    return result


def own_kernel(q_ref, coef_ref, warm_ref, sums_ref, red):
    lane = lanes()
    red[...] = jnp.zeros_like(red)
    for k in range(K):
        for y in range(2):
            for t in range(Z // 8):
                warm_ref[2 * k + y, tile(t), :] = (
                    coef_ref[y, tile(t), :] * q_ref[4 * k + y, tile(t), :]
                    + coef_ref[2 + y, tile(t), :] * q_ref[4 * k + 2 + y, tile(t), :]
                )
    for k, m, l in pairs():
        acc = jnp.zeros((8, X), F32)
        for p in range(4):
            for t in range(Z // 8):
                acc = acc + q_ref[4 * k + p, tile(t), :] * q_ref[4 * l + p, tile(t), :]
        red[m, k : k + 1, :] = jnp.sum(acc, axis=0, keepdims=True)
    speed = jnp.zeros((8, X), F32)
    for y in range(2):
        for t in range(Z // 8):
            v = coef_ref[4 + y, tile(t), :]
            speed = speed + v * v
    result = jnp.where(lane == 40, jnp.sum(speed, axis=1, keepdims=True), 0.0)
    sums_ref[...] = columns(result, lane, red, range(1))


def wire_kernel(q_ref, coef_ref, side_ref, up_ref):
    for f in range(NA):
        ref, i = (q_ref, f) if f < NF else (coef_ref, f - NF)
        up_ref[f] = ref[i, 0:8, :]
    for b in range(3):
        up_ref[NA + b] = side_ref[b, 0:8, :]


def wide_shifts(main, side, lane):
    m = [pltpu.roll(main, d, 1) for d in (1, X - 1, 2, X - 2)]
    s = [pltpu.roll(side, d, 1) for d in (1, X - 1, 2, X - 2)]
    out_main = (
        m[0],
        jnp.where(lane >= X - 1, s[1], m[1]),
        m[2],
        jnp.where(lane >= X - 2, s[3], m[3]),
    )
    out_side = (jnp.where(lane < 1, m[0], s[0]), s[1], jnp.where(lane < 2, m[2], s[2]), s[3])
    return (out_main, out_side)


def block_shifts(main, side, lane):
    out = []
    for d, mask in (
        (1, (lane >= 1) & (lane < 4)),
        (X - 1, (lane < 4) | (lane >= X - 1)),
        (2, (lane >= 2) & (lane < 4)),
        (X - 2, (lane < 4) | (lane >= X - 2)),
    ):
        out.append(jnp.where(mask, pltpu.roll(side, d, 1), pltpu.roll(main, d, 1)))
    return out


def rate(speed, xr, xe, xt, r_at, t_at, r_other, t_other):
    def lap(x, at, other):
        ones = x[0] + x[1] + (at(-1) + at(1)) + other
        twos = x[2] + x[3] + (at(-2) + at(2))
        return 16.0 * ones - twos - 90.0 * at(0)

    def slope(x):
        return 8.0 * (x[1] - x[0]) - (x[3] - x[2])

    rate_r = speed * slope(xr) + (viscosity / 12.0) * lap(xr, r_at, r_other)
    rate_e = speed * slope(xe) + (conductivity / 12.0) * lap(xt, t_at, t_other)
    return (rate_r, rate_e)


def cross_sums(lane, red, qd, ad, bd, tiles):
    for k, m, l in pairs():
        acc = [jnp.zeros((8, X), F32)] * 4
        for p in range(4):
            for t in range(tiles):
                qk, ak, bk = (v[4 * k + p, tile(t), :] for v in (qd, ad, bd))
                ql, al, bl = (v[4 * l + p, tile(t), :] for v in (qd, ad, bd))
                acc[0] = acc[0] + (qk * al + ak * ql)
                acc[1] = acc[1] + (ak * al + (qk * bl + bk * ql))
                acc[2] = acc[2] + (ak * bl + bk * al)
                acc[3] = acc[3] + bk * bl
        for n in range(4):
            red[8 * n + 8 + m, k : k + 1, :] = jnp.sum(acc[n], axis=0, keepdims=True)


def inner_kernel(
    q_ref, coef_ref, warm_ref, side_ref, own_ref,
    ad_ref, bd_ref, tail_ref, sums_ref,
    eh, wh, am, ah, aw, tm, th, tw, qd, red,
):
    lane = lanes()
    block = lane < 4
    red[...] = jnp.zeros_like(red)
    for f in range(NA):
        b, i = f // 16, f % 16
        for t in range(Z // 8):
            part = side_ref[b, tile(t), :]
            eh[f, tile(t), :] = pltpu.roll(part, X - 8 * i, 1) if i else part
    for f in range(NF):
        for t in range(3):
            rows = slice(8 * t + 4, 8 * t + 12)
            qd[f, tile(t), :] = jnp.where(block, eh[f, rows, :], q_ref[f, rows, :])

    def vector(k, carry):
        base = 4 * k
        for y in range(2):
            for t in range(Z // 8):
                wh[y, tile(t), :] = (
                    eh[NF + y, tile(t), :] * eh[base + y, tile(t), :]
                    + eh[NF + 2 + y, tile(t), :] * eh[base + 2 + y, tile(t), :]
                )
        for y in range(2):
            for r in (2, 10, 18, 22):
                rows = pl.ds(r, 8)
                xr = wide_shifts(q_ref[base + y, rows, :], eh[base + y, rows, :], lane)
                xe = wide_shifts(q_ref[base + 2 + y, rows, :], eh[base + 2 + y, rows, :], lane)
                xt = wide_shifts(warm_ref[2 * k + y, rows, :], wh[y, rows, :], lane)
                out = []
                for s in range(2):
                    src, off = ((q_ref, 0), (eh, 0))[s]
                    speed = coef_ref[4 + y, rows, :] if s == 0 else eh[NF + 4 + y, rows, :]

                    def r_at(d, src=src):
                        return src[base + y, pl.ds(r + d, 8), :]

                    def t_at(d, s=s, plane=y):
                        if s == 0:
                            return warm_ref[2 * k + plane, pl.ds(r + d, 8), :]
                        return wh[plane, pl.ds(r + d, 8), :]

                    out.append(
                        rate(
                            speed * (-1.0 / 12.0), xr[s], xe[s], xt[s], r_at, t_at,
                            src[base + 1 - y, rows, :], t_at(0, plane=1 - y),
                        )
                    )
                for c in range(2):
                    i = base + 2 * c + y
                    am[i, rows, :] = out[0][c]
                    ah[i, rows, :] = out[1][c]
                    aw[i, rows, :] = jnp.where(block, out[1][c], out[0][c])
        for y in range(2):
            for r in (2, 10, 18, 22):
                rows = pl.ds(r, 8)
                main = coef_ref[y, rows, :] * am[base + y, rows, :] + (
                    coef_ref[2 + y, rows, :] * am[base + 2 + y, rows, :]
                )
                side = eh[NF + y, rows, :] * ah[base + y, rows, :] + (
                    eh[NF + 2 + y, rows, :] * ah[base + 2 + y, rows, :]
                )
                tm[y, rows, :] = main
                th[y, rows, :] = side
                tw[y, rows, :] = jnp.where(block, side, main)
        for y in range(2):
            for t in range(3):
                r = 8 * t + 4
                rows = pl.ds(r, 8)
                speed = jnp.where(block, eh[NF + 4 + y, rows, :], coef_ref[4 + y, rows, :])
                out = rate(
                    speed * (-1.0 / 12.0),
                    block_shifts(am[base + y, rows, :], ah[base + y, rows, :], lane),
                    block_shifts(am[base + 2 + y, rows, :], ah[base + 2 + y, rows, :], lane),
                    block_shifts(tm[y, rows, :], th[y, rows, :], lane),
                    lambda d: aw[base + y, pl.ds(r + d, 8), :],
                    lambda d: tw[y, pl.ds(r + d, 8), :],
                    aw[base + 1 - y, rows, :],
                    tw[1 - y, rows, :],
                )
                for c in range(2):
                    i = base + 2 * c + y
                    bd_ref[i, tile(t), :] = 0.5 * out[c]
                    ad_ref[i, tile(t), :] = aw[i, rows, :]
        for p in range(4):
            tail_ref[0, base + p] = am[base + p, 22:30, :]
            tail_ref[1, base + p] = ah[base + p, 22:30, :]
        return carry

    lax.fori_loop(0, K, vector, 0)
    cross_sums(lane, red, qd, ad_ref, bd_ref, 3)
    sums_ref[...] = columns(own_ref[...], lane, red, range(1, 5))


def edge_kernel(
    q_ref, coef_ref, side_ref, below_ref, tail_ref, inner_ref,
    ad_ref, bd_ref, sums_ref,
    em, eh, wm, wh, am, ah, aw, tm, th, tw, qd, red,
):
    lane = lanes()
    block = lane < 4
    red[...] = jnp.zeros_like(red)
    for f in range(NA):
        ref, i = (q_ref, f) if f < NF else (coef_ref, f - NF)
        em[f, 0:8, :] = ref[i, 24:32, :]
        em[f, 8:16, :] = below_ref[f]
        b, i = f // 16, f % 16
        for t, part in enumerate((side_ref[b, 24:32, :], below_ref[NA + b])):
            eh[f, tile(t), :] = pltpu.roll(part, X - 8 * i, 1) if i else part
    for f in range(NF):
        qd[f] = jnp.where(block, eh[f, 4:12, :], em[f, 4:12, :])

    def vector(k, carry):
        base = 4 * k
        for y in range(2):
            for t in range(2):
                for dst, src in ((wm, em), (wh, eh)):
                    dst[y, tile(t), :] = (
                        src[NF + y, tile(t), :] * src[base + y, tile(t), :]
                        + src[NF + 2 + y, tile(t), :] * src[base + 2 + y, tile(t), :]
                    )
        for p in range(4):
            am[base + p, 0:8, :] = tail_ref[0, base + p]
            ah[base + p, 0:8, :] = tail_ref[1, base + p]
            aw[base + p, 0:8, :] = jnp.where(block, tail_ref[1, base + p], tail_ref[0, base + p])
        for y in range(2):
            rows = pl.ds(6, 8)
            xr = wide_shifts(em[base + y, rows, :], eh[base + y, rows, :], lane)
            xe = wide_shifts(em[base + 2 + y, rows, :], eh[base + 2 + y, rows, :], lane)
            xt = wide_shifts(wm[y, rows, :], wh[y, rows, :], lane)
            out = []
            for s in range(2):
                src, warm = ((em, wm), (eh, wh))[s]
                out.append(
                    rate(
                        src[NF + 4 + y, rows, :] * (-1.0 / 12.0), xr[s], xe[s], xt[s],
                        lambda d: src[base + y, pl.ds(6 + d, 8), :],
                        lambda d: warm[y, pl.ds(6 + d, 8), :],
                        src[base + 1 - y, rows, :],
                        warm[1 - y, rows, :],
                    )
                )
            for c in range(2):
                i = base + 2 * c + y
                am[i, 8:16, :] = out[0][c]
                ah[i, 8:16, :] = out[1][c]
                aw[i, 8:16, :] = jnp.where(block, out[1][c], out[0][c])
        for y in range(2):
            for r in (4, 8):
                rows, here = pl.ds(r, 8), pl.ds(r - 2, 8)
                main = em[NF + y, here, :] * am[base + y, rows, :] + (
                    em[NF + 2 + y, here, :] * am[base + 2 + y, rows, :]
                )
                side = eh[NF + y, here, :] * ah[base + y, rows, :] + (
                    eh[NF + 2 + y, here, :] * ah[base + 2 + y, rows, :]
                )
                tm[y, rows, :] = main
                th[y, rows, :] = side
                tw[y, rows, :] = jnp.where(block, side, main)
        for y in range(2):
            rows = pl.ds(6, 8)
            speed = jnp.where(block, eh[NF + 4 + y, 4:12, :], em[NF + 4 + y, 4:12, :])
            out = rate(
                speed * (-1.0 / 12.0),
                block_shifts(am[base + y, rows, :], ah[base + y, rows, :], lane),
                block_shifts(am[base + 2 + y, rows, :], ah[base + 2 + y, rows, :], lane),
                block_shifts(tm[y, rows, :], th[y, rows, :], lane),
                lambda d: aw[base + y, pl.ds(6 + d, 8), :],
                lambda d: tw[y, pl.ds(6 + d, 8), :],
                aw[base + 1 - y, rows, :],
                tw[1 - y, rows, :],
            )
            for c in range(2):
                i = base + 2 * c + y
                bd_ref[i] = 0.5 * out[c]
                ad_ref[i] = aw[i, 6:14, :]
        return carry

    lax.fori_loop(0, K, vector, 0)
    cross_sums(lane, red, qd, ad_ref, bd_ref, 1)
    result = columns(jnp.zeros((8, X), F32), lane, red, range(1, 5)) + inner_ref[...]
    for n in range(sums_ref.shape[0]):
        sums_ref[n] = result


def give_kernel(ad_ref, bd_ref, ade_ref, bde_ref, out_ref):
    group = lanes() >> 2
    for n, (ref, edge) in enumerate(((ad_ref, ade_ref), (bd_ref, bde_ref))):
        for t in range(Z // 8):
            acc = jnp.zeros((8, X), F32)
            for f in range(NF):
                part = ref[f, tile(t), :] if t < 3 else edge[f]
                acc = jnp.where(group == f, pltpu.roll(part, 4 * f, 1) if f else part, acc)
            out_ref[n, tile(t), :] = acc


def place_kernel(ad_ref, bd_ref, ade_ref, bde_ref, got_ref, a_ref, b_ref, down_ref):
    block = lanes() < 4
    for n, (ref, edge, out) in enumerate(((ad_ref, ade_ref, a_ref), (bd_ref, bde_ref, b_ref))):
        for f in range(NF):
            for t in range(Z // 8):
                part = ref[f, tile(t), :] if t < 3 else edge[f]
                got = got_ref[n, tile(t), :]
                got = pltpu.roll(got, X - 4 * f, 1) if f else got
                part = jnp.where(block, got, part)
                if t < 3:
                    out[f, 8 * t + 4 : 8 * t + 12, :] = part
                else:
                    out[f, 28:32, :] = part[0:4, :]
                    out[f, 0:4, :] = jnp.zeros((4, X), F32)
                    r = 4 * (NF * n + f)
                    down_ref[r : r + 4, :] = part[4:8, :]


def finish_kernel(cells, q_ref, a_ref, b_ref, above_ref, sums_ref, out_ref, growth_ref, first):
    lane = lanes()
    row = lax.broadcasted_iota(jnp.int32, (8, X), 0)
    for n, ref in enumerate((a_ref, b_ref)):
        for f in range(NF):
            r = 4 * (NF * n + f)
            first[n, f, 0:4, :] = above_ref[r : r + 4, :]
            first[n, f, 4:8, :] = ref[f, 4:8, :]
    total = sums_ref[0]
    for n in range(1, sums_ref.shape[0]):
        total = total + sums_ref[n]
    speed = jnp.broadcast_to(jnp.sum(total[:, 40:41], axis=0, keepdims=True), (8, X))
    step = courant_number / jnp.sqrt(speed * (1.0 / cells) + 1e-05)
    gram = total
    power = step
    for n in range(1, 5):
        gram = gram + power * pltpu.roll(total, X - 8 * n, 1)
        power = power * step
    gram = gram * (1.0 / (2.0 * cells))
    cols = [jnp.broadcast_to(gram[:, m : m + 1], (8, X)) for m in range(5)]

    def entry(i, j):
        k, m = (j, i - j) if i - j <= 4 else (i, j - i + K)
        if m == 4:
            k = min(i, j)
        return jnp.broadcast_to(cols[m][k : k + 1, :], (8, X))

    low = [[None] * K for _ in range(K)]
    inv_diag = []
    for j in range(K):
        d = entry(j, j)
        for p in range(j):
            d = d - low[j][p] * low[j][p]
        root = jnp.sqrt(d)
        low[j][j] = root
        inv_diag.append(1.0 / root)
        for i in range(j + 1, K):
            v = entry(i, j)
            for p in range(j):
                v = v - low[i][p] * low[j][p]
            low[i][j] = v * inv_diag[j]
    inverse = [[None] * K for _ in range(K)]
    for j in range(K):
        inverse[j][j] = inv_diag[j]
        for i in range(j + 1, K):
            v = low[i][j] * inverse[j][j]
            for p in range(j + 1, i):
                v = v + low[i][p] * inverse[p][j]
            inverse[i][j] = -v * inv_diag[i]
    growth = jnp.zeros((8, X), F32)
    for i in range(K):
        for j in range(i + 1):
            growth = jnp.where((row == j) & (lane == i), low[i][j], growth)
    growth_ref[...] = growth
    square = step * step
    for p in range(4):
        for t in range(Z // 8):
            adv = []
            for k in range(K):
                f = 4 * k + p
                a, b = (
                    (first[0, f], first[1, f])
                    if t == 0
                    else (a_ref[f, tile(t), :], b_ref[f, tile(t), :])
                )
                adv.append(q_ref[f, tile(t), :] + step * a + square * b)
            for k in range(K):
                v = inverse[k][0] * adv[0]
                for j in range(1, k + 1):
                    v = v + inverse[k][j] * adv[j]
                out_ref[4 * k + p, tile(t), :] = v


def call(body, outs, scratch=(), cost=2000000, limit=24, **more):
    shapes = [jax.ShapeDtypeStruct(s, F32) for s in outs]
    return pl.pallas_call(
        body,
        out_shape=shapes,
        scratch_shapes=[pltpu.VMEM(s, F32) if isinstance(s, tuple) else s for s in scratch],
        compiler_params=pltpu.CompilerParams(vmem_limit_bytes=limit * 1024 * 1024),
        cost_estimate=pl.CostEstimate(flops=cost, bytes_accessed=cost, transcendentals=0),
        **more,
    )


def ring(array, axes, step):
    size = lax.axis_size(axes)
    return lax.ppermute(array, axes, [(i, (i + step) % size) for i in range(size)])


def gathered(array, axes):
    return lax.all_to_all(array, axes, 0, 0)


def per_device(tangents, mass, internal, velocity):
    cells = float(2 * Z * X * lax.axis_size(GX) * lax.axis_size(GZ))
    near, far = lax.axis_size(NEAR), lax.axis_size(FAR)
    whole, inner, edge, tall = (NF, Z, X), (NF, 24, X), (NF, 8, X), (NA, 16, X)
    q, coef, pack = call(
        prep_kernel,
        [whole, (NC, Z, X), (3, Z, X)],
        [(2, Z, X), (2, Z, X), pltpu.SemaphoreType.DMA((4,))],
        limit=60,
        in_specs=[pl.BlockSpec(memory_space=pl.ANY)] * 4,
    )(tangents.reshape(whole), mass, internal, velocity)
    side = ring(pack, GX, -1)
    warm, own = call(own_kernel, [(2 * K, Z, X), (8, X)], [(8, 8, X)])(q, coef)
    side, warm, own = lax.optimization_barrier((side, warm, own))
    (up,) = call(wire_kernel, [(NA + 3, 8, X)])(q, coef, side)
    below = ring(up, GZ, -1)
    ad, bd, tail, part = call(
        inner_kernel,
        [inner, inner, (2, NF, 8, X), (8, X)],
        [(NA, Z, X), (2, Z, X), whole, whole, whole, (2, Z, X), (2, Z, X), (2, Z, X), inner, (40, 8, X)],
    )(q, coef, warm, side, own)
    low = (NF, 16, X)
    ade, bde, sums = call(
        edge_kernel,
        [edge, edge, (near, 8, X)],
        [tall, tall, (2, 16, X), (2, 16, X), low, low, low]
        + [(2, 16, X)] * 3
        + [edge, (40, 8, X)],
    )(q, coef, side, below, tail, part)
    sums = jnp.sum(gathered(sums, NEAR), axis=0)
    (give,) = call(give_kernel, [(2, Z, X)])(ad, bd, ade, bde)
    got = ring(give, GX, 1)
    sums, got = lax.optimization_barrier((sums, got))
    sums = gathered(jnp.broadcast_to(sums, (far, 8, X)), FAR)
    a, b, down = call(place_kernel, [whole, whole, (8 * NF, X)])(ad, bd, ade, bde, got)
    above = ring(down, GZ, 1)
    out, growth = call(
        functools.partial(finish_kernel, cells), [whole, (8, X)], [(2, NF, 8, X)]
    )(q, a, b, above, sums)
    return (out.reshape(tangents.shape), growth[:, :K])


def solution(mesh):
    gx, gz = mesh.devices.shape
    fine = Mesh(mesh.devices.reshape(gx // 4, 4, gz // 4, 4), GX + GZ)
    in_specs = (P(None, None, None, GZ, GX),) + (P(None, GZ, GX),) * 3
    out_specs = (P(None, None, None, GZ, GX), P())
    return jax.shard_map(
        per_device, mesh=fine, in_specs=in_specs, out_specs=out_specs, check_vma=False
    )
```

time: 74.2 us -> 65.6 us (0.88)
  the two profiles are of different devices: /device:TPU:1 before, /device:TPU:4 now
where the time goes in v2:
time: 65.6 us; the launch traced here: 65.1 us
  starting transfers between devices  34.1 us (52%)
  waiting for transfers between devices  15.1 us (23%)
  Pallas kernels  12.6 us (19%)
  local copies, waits for them, and re-layouts  2.59 us (4%)
  between operations  0.71 us (1%)
    all_to_all x2, starting transfers between devices, gathered(): return lax.all_to_all(array, axes, 0, 0)  21.2 us
    ppermute x4, starting transfers between devices, ring(): lax.ppermute(array, axes, [(i, (i + step) % size) for i in range(size)])  13 us
    ppermute x4, waiting for transfers between devices, ring(): lax.ppermute(array, axes, [(i, (i + step) % size) for i in range(size)])  10.2 us
    pallas_call x1, Pallas kernels, per_device(): call(inner_kernel, [inner, inner, (2, NF, 8, X), (8, X)], [(NA, Z, X), (2...  5.14 us
    all_to_all x2, waiting for transfers between devices, gathered(): return lax.all_to_all(array, axes, 0, 0)  4.94 us
    pallas_call x1, Pallas kernels, per_device(): call(edge_kernel, [edge, edge, (near, 8, X)], [tall, tall, (2, 16, X), (2...  3.24 us
    pallas_call x1, Pallas kernels, per_device(): call(prep_kernel, [whole, (NC, Z, X), (3, Z, X)], [(2, Z, X), (2, Z, X),...  1.97 us
    unnamed x6, local copies, waits for them, and re-layouts  1.94 us
  transfers between devices with their start and end apart: 6, of which 4 were waited for; matrix products, arithmetic and copies ran while one was open for 0% of the time, Pallas kernels for 9%

profile of v2, /device:TPU:4, one launch (start us, length us, event | category | flops | bytes accessed | tf_op | source)
XLA Modules:
  0.0 65.1 jit_solution(10286846474689873703)
XLA Ops:
  0.6 2.0 %shard_map.59 = (f32[32,32,128]{2,1,0:T(8,128)}, f32[6,32,128]{2,1,0:T(8,128)}, f32[3,32,128]{2,1,0:T(8,128)}) custom-call(f32[32,32,128]{2,1,0:T(8,128)} %bitcast.3, f32[2,32,128]{2,1,0:T(8,128)} %mass_hbm.1, f32[2,32,128]{2,1,0:T(8,128)} %internal_hbm.1, f32[2,32,128]{2,1,0:T(8,128)} %velocity_hbm.1), custom_call_target="tpu_custom_call" | custom-call | flops 2000000 | bytes 2000000 | tf_op jit(solution)/shard_map/pallas_call | solution.py:520
  2.6 6.0 %collective-permute-start = (f32[3,32,128]{2,1,0:T(8,128)}, f32[3,32,128]{2,1,0:T(8,128)S(1)}, u32[]{:S(2)}, u32[]{:S(2)}) collective-permute-start(f32[3,32,128]{2,1,0:T(8,128)} %get-tuple-element.26), channel_id=1, source_target_pairs={{0,480},{32,0},{64,32},{96,64},{128,96},{160,128},{192,160},{224,1... | collective-permute-start | bytes 147464 | tf_op jit(solution)/shard_map/ppermute | solution.py:509
  8.6 0.0 copy-start
  8.6 1.0 %copy-done = f32[32,32,128]{2,1,0:T(8,128)S(1)} copy-done((f32[32,32,128]{2,1,0:T(8,128)S(1)}, f32[32,32,128]{2,1,0:T(8,128)}, u32[]{:S(2)}) %copy-start) | copy-done | bytes 524312
  9.7 0.0 copy-start.2
  9.7 0.9 %copy-done.2 = f32[6,32,128]{2,1,0:T(8,128)S(1)} copy-done((f32[6,32,128]{2,1,0:T(8,128)S(1)}, f32[6,32,128]{2,1,0:T(8,128)}, u32[]{:S(2)}) %copy-start.2) | copy-done | bytes 98328
  10.6 0.3 shard_map.60
  10.9 0.0 collective-permute-done.side_ref
  10.9 1.9 %collective-permute-start.1 = (f32[41,8,128]{2,1,0:T(8,128)S(1)}, f32[41,8,128]{2,1,0:T(8,128)S(1)}, u32[]{:S(2)}, u32[]{:S(2)}) collective-permute-start(f32[41,8,128]{2,1,0:T(8,128)S(1)} %shard_map.62), channel_id=1, source_target_pairs={{0,31},{1,0},{2,1},{3,2},{4,3},{5,4},{6,5},{7,6},{8,7},{9,8},{10,9... | collective-permute-start | bytes 503816 | tf_op jit(solution)/shard_map/ppermute | solution.py:509
  12.8 5.1 %shard_map.61 = (f32[32,24,128]{2,1,0:T(8,128)S(1)}, f32[32,24,128]{2,1,0:T(8,128)S(1)}, f32[2,32,8,128]{3,2,1,0:T(8,128)S(1)}, f32[8,128]{1,0:T(8,128)S(1)}) custom-call(f32[32,32,128]{2,1,0:T(8,128)S(1)} %copy-done, f32[6,32,128]{2,1,0:T(8,128)S(1)} %copy-done.2, f32[16,32,128]{2,1,0:T(8,128)S(1)} %get-tuple-element.29.warm_ref, ...), custom_call_target="tpu_custom_call" | custom-call | flops 2000000 | bytes 2000000 | tf_op jit(solution)/shard_map/pallas_call | solution.py:532
  18.0 0.0 collective-permute-done.1.below_ref
  18.0 3.2 %shard_map.63 = (f32[32,8,128]{2,1,0:T(8,128)S(1)}, f32[32,8,128]{2,1,0:T(8,128)S(1)}, f32[16,8,128]{2,1,0:T(8,128)}) custom-call(f32[32,32,128]{2,1,0:T(8,128)S(1)} %copy-done, f32[6,32,128]{2,1,0:T(8,128)S(1)} %copy-done.2, f32[3,32,128]{2,1,0:T(8,128)S(1)} %collective-permute-done.side_ref, f32[41,8,128]{2,1,0:T(8,128)S(1)} %collective-permute-done.1.below_ref, ...), custom_call_target="tpu_custom_call" | custom-call | flops 2000000 | bytes 2000000 | tf_op jit(solution)/shard_map/pallas_call | solution.py:538
  21.2 14.4 %all-to-all-start = ((f32[16,8,128]{2,1,0:T(8,128)}), f32[16,8,128]{2,1,0:T(8,128)S(1)}, u32[]{:S(2)}, u32[]{:S(2)}) async-start(f32[16,8,128]{2,1,0:T(8,128)} %get-tuple-element.38), calls=%async_computation | async-start | bytes 131072 | tf_op jit(solution)/shard_map/all_to_all | solution.py:513
  35.6 0.3 shard_map.64
  36.0 3.1 %collective-permute-start.2 = (f32[2,32,128]{2,1,0:T(8,128)S(1)}, f32[2,32,128]{2,1,0:T(8,128)S(1)}, u32[]{:S(2)}, u32[]{:S(2)}) collective-permute-start(f32[2,32,128]{2,1,0:T(8,128)S(1)} %shard_map.64), channel_id=1, source_target_pairs={{0,32},{32,64},{64,96},{96,128},{128,160},{160,192},{192,224},{224... | collective-permute-start | bytes 98312 | tf_op jit(solution)/shard_map/ppermute | solution.py:509
  39.1 0.5 all-to-all-done
  39.6 4.3 %collective-permute-done.2.got_ref = f32[2,32,128]{2,1,0:T(8,128)S(1)} collective-permute-done((f32[2,32,128]{2,1,0:T(8,128)S(1)}, f32[2,32,128]{2,1,0:T(8,128)S(1)}, u32[]{:S(2)}, u32[]{:S(2)}) %collective-permute-start.2) | collective-permute-done | bytes 32800 | tf_op jit(solution)/shard_map/ppermute | solution.py:509
  43.9 0.7 %broadcast_in_dim.3 = f32[32,8,128]{2,1,0:T(8,128)} broadcast(f32[8,128]{1,0:T(8,128)S(1)} %reduce_sum.9), dimensions={1,2} | broadcast | bytes 135168 | tf_op jit(solution)/shard_map/broadcast_in_dim | solution.py:549
  44.5 6.7 %all-to-all-start.1 = ((f32[32,8,128]{2,1,0:T(8,128)}), f32[32,8,128]{2,1,0:T(8,128)S(1)}, u32[]{:S(2)}, u32[]{:S(2)}) async-start(f32[32,8,128]{2,1,0:T(8,128)} %broadcast_in_dim.3), calls=%async_computation.1 | async-start | bytes 262144 | tf_op jit(solution)/shard_map/all_to_all | solution.py:513
  51.3 0.0 copy-start.1
  51.3 0.3 shard_map.65
  51.6 1.9 %collective-permute-start.3 = (f32[256,128]{1,0:T(8,128)S(1)}, f32[256,128]{1,0:T(8,128)S(1)}, u32[]{:S(2)}, u32[]{:S(2)}) collective-permute-start(f32[256,128]{1,0:T(8,128)S(1)} %get-tuple-element.42), channel_id=1, source_target_pairs={{0,1},{1,2},{2,3},{3,4},{4,5},{5,6},{6,7},{7,8},{8,9},{9,10},{10,1... | collective-permute-start | bytes 393224 | tf_op jit(solution)/shard_map/ppermute | solution.py:509
  53.6 5.9 %collective-permute-done.3.above_ref = f32[256,128]{1,0:T(8,128)S(1)} collective-permute-done((f32[256,128]{1,0:T(8,128)S(1)}, f32[256,128]{1,0:T(8,128)S(1)}, u32[]{:S(2)}, u32[]{:S(2)}) %collective-permute-start.3) | collective-permute-done | bytes 131104 | tf_op jit(solution)/shard_map/ppermute | solution.py:509
  59.4 4.4 %all-to-all-done.1.sums_ref = f32[32,8,128]{2,1,0:T(8,128)S(1)} async-done(((f32[32,8,128]{2,1,0:T(8,128)}), f32[32,8,128]{2,1,0:T(8,128)S(1)}, u32[]{:S(2)}, u32[]{:S(2)}) %all-to-all-start.1) | async-done | bytes 131104 | tf_op jit(solution)/shard_map/all_to_all | solution.py:513
  63.9 0.0 copy-done.1
  63.9 1.3 %shard_map.66 = (f32[32,32,128]{2,1,0:T(8,128)}, f32[8,128]{1,0:T(8,128)}) custom-call(f32[32,32,128]{2,1,0:T(8,128)S(1)} %copy-done.1, f32[32,32,128]{2,1,0:T(8,128)S(1)} %get-tuple-element.40.a_ref, f32[32,32,128]{2,1,0:T(8,128)S(1)} %get-tuple-element.41.b_ref, f32[256,128]{1,0:T(8,128)S(1)} %collective-permute-done.3.above_ref, ...), custom_call_target="tpu_custom_call" | custom-call | flops 2000000 | bytes 2000000 | tf_op jit(solution)/shard_map/pallas_call | solution.py:552
  (2 shorter events, 0.0 us)
Async XLA Ops:
  2.6 8.2 %collective-permute-start = (f32[3,32,128]{2,1,0:T(8,128)}, f32[3,32,128]{2,1,0:T(8,128)S(1)}, u32[]{:S(2)}, u32[]{:S(2)}) collective-permute-start(f32[3,32,128]{2,1,0:T(8,128)} %get-tuple-element.26), channel_id=1, source_target_pairs={{0,480},{32,0},{64,32},{96,64},{128,96},{160,128},{192,160},{224,1... | collective-permute-start | bytes 147464 | tf_op jit(solution)/shard_map/ppermute | solution.py:509
  8.6 1.0 %copy-start = (f32[32,32,128]{2,1,0:T(8,128)S(1)}, f32[32,32,128]{2,1,0:T(8,128)}, u32[]{:S(2)}) copy-start(f32[32,32,128]{2,1,0:T(8,128)} %get-tuple-element.24.q_ref) | copy-start | bytes 1572868
  9.7 0.9 %copy-start.2 = (f32[6,32,128]{2,1,0:T(8,128)S(1)}, f32[6,32,128]{2,1,0:T(8,128)}, u32[]{:S(2)}) copy-start(f32[6,32,128]{2,1,0:T(8,128)} %get-tuple-element.25.coef_ref) | copy-start | bytes 294916
  10.9 7.1 %collective-permute-start.1 = (f32[41,8,128]{2,1,0:T(8,128)S(1)}, f32[41,8,128]{2,1,0:T(8,128)S(1)}, u32[]{:S(2)}, u32[]{:S(2)}) collective-permute-start(f32[41,8,128]{2,1,0:T(8,128)S(1)} %shard_map.62), channel_id=1, source_target_pairs={{0,31},{1,0},{2,1},{3,2},{4,3},{5,4},{6,5},{7,6},{8,7},{9,8},{10,9... | collective-permute-start | bytes 503816 | tf_op jit(solution)/shard_map/ppermute | solution.py:509
  21.2 18.4 %all-to-all-start = ((f32[16,8,128]{2,1,0:T(8,128)}), f32[16,8,128]{2,1,0:T(8,128)S(1)}, u32[]{:S(2)}, u32[]{:S(2)}) async-start(f32[16,8,128]{2,1,0:T(8,128)} %get-tuple-element.38), calls=%async_computation | async-start | bytes 131072 | tf_op jit(solution)/shard_map/all_to_all | solution.py:513
  36.0 7.9 %collective-permute-start.2 = (f32[2,32,128]{2,1,0:T(8,128)S(1)}, f32[2,32,128]{2,1,0:T(8,128)S(1)}, u32[]{:S(2)}, u32[]{:S(2)}) collective-permute-start(f32[2,32,128]{2,1,0:T(8,128)S(1)} %shard_map.64), channel_id=1, source_target_pairs={{0,32},{32,64},{64,96},{96,128},{128,160},{160,192},{192,224},{224... | collective-permute-start | bytes 98312 | tf_op jit(solution)/shard_map/ppermute | solution.py:509
  44.5 19.3 %all-to-all-start.1 = ((f32[32,8,128]{2,1,0:T(8,128)}), f32[32,8,128]{2,1,0:T(8,128)S(1)}, u32[]{:S(2)}, u32[]{:S(2)}) async-start(f32[32,8,128]{2,1,0:T(8,128)} %broadcast_in_dim.3), calls=%async_computation.1 | async-start | bytes 262144 | tf_op jit(solution)/shard_map/all_to_all | solution.py:513
  51.3 12.6 %copy-start.1 = (f32[32,32,128]{2,1,0:T(8,128)S(1)}, f32[32,32,128]{2,1,0:T(8,128)}, u32[]{:S(2)}) copy-start(f32[32,32,128]{2,1,0:T(8,128)} %get-tuple-element.24.q_ref) | copy-start | bytes 1572868
  51.6 7.8 %collective-permute-start.3 = (f32[256,128]{1,0:T(8,128)S(1)}, f32[256,128]{1,0:T(8,128)S(1)}, u32[]{:S(2)}, u32[]{:S(2)}) collective-permute-start(f32[256,128]{1,0:T(8,128)S(1)} %get-tuple-element.42), channel_id=1, source_target_pairs={{0,1},{1,2},{2,3},{3,4},{4,5},{5,6},{6,7},{7,8},{8,9},{9,10},{10,1... | collective-permute-start | bytes 393224 | tf_op jit(solution)/shard_map/ppermute | solution.py:509

commit v3 on v2

v3 whole, which is shorter than its diff:
```python
import functools

import jax
import jax.numpy as jnp
from jax import lax
from jax.experimental import pallas as pl
from jax.experimental.pallas import tpu as pltpu
from jax.sharding import Mesh, PartitionSpec as P

NEWTON = 4
isochoric_warmth_coefficient = 3.0
attraction = 0.5
acentric_coefficient_gradient = 0.6
covolume = 0.15
root_two = 1.4142135623730951
viscosity = 0.2
conductivity = 1.0
courant_number = 0.5

K = 8
NF = 4 * K
NC = 6
NA = NF + NC
Z = 32
X = 128
GX = ("xh", "xl")
GZ = ("zh", "zl")
NEAR = ("xl", "zl")
FAR = ("xh", "zh")
F32 = jnp.float32


def departure(cell_mass_concentration):
    low_term = 1.0 + (1.0 - root_two) * covolume * cell_mass_concentration
    high_term = 1.0 + (1.0 + root_two) * covolume * cell_mass_concentration
    factor = attraction * (1.0 + acentric_coefficient_gradient) / (2.0 * root_two * covolume)
    value = factor * (jnp.log(low_term) - jnp.log(high_term))
    slope = factor * (
        (1.0 - root_two) * covolume / low_term - (1.0 + root_two) * covolume / high_term
    )
    return (value, slope)


def slopes(mass, internal):
    deviation, departure_slope = departure(mass)
    warmth = internal / isochoric_warmth_coefficient
    for _ in range(NEWTON):
        root = jnp.sqrt(warmth)
        multiplier = 1.0 + acentric_coefficient_gradient * (1.0 - root)
        mismatch = isochoric_warmth_coefficient * warmth + deviation * multiplier - internal
        gradient = isochoric_warmth_coefficient - deviation * acentric_coefficient_gradient / (
            2.0 * root
        )
        warmth = warmth - mismatch / gradient
    root = jnp.sqrt(warmth)
    multiplier = 1.0 + acentric_coefficient_gradient * (1.0 - root)
    gradient = isochoric_warmth_coefficient - deviation * acentric_coefficient_gradient / (
        2.0 * root
    )
    energy = 1.0 / gradient
    return (-departure_slope * multiplier * energy, energy)


def lanes():
    return lax.broadcasted_iota(jnp.int32, (8, X), 1)


def tile(t):
    return slice(8 * t, 8 * t + 8)


def prep_kernel(
    q_hbm, mass_hbm, internal_hbm, velocity_hbm, coef_ref, pack_ref, rows_ref, q, mass, internal, sems
):
    copies = [
        pltpu.make_async_copy(src, dst, sems.at[i])
        for i, (src, dst) in enumerate(
            (
                (mass_hbm, mass),
                (internal_hbm, internal),
                (velocity_hbm, coef_ref.at[pl.ds(4, 2)]),
                (q_hbm, q),
            )
        )
    ]
    for copy in copies:
        copy.start()
    copies[0].wait()
    copies[1].wait()
    density, energy = slopes(mass[...], internal[...])
    coef_ref[0:2] = density
    coef_ref[2:4] = energy
    copies[2].wait()
    copies[3].wait()
    group = lanes() >> 3
    for t in range(Z // 8):
        for c in range(2):
            acc = q[2 * c, tile(t), :]
            for y in range(2):
                for k in range(K):
                    i = 8 * y + k
                    if i:
                        part = pltpu.roll(q[4 * k + 2 * c + y, tile(t), :], 8 * i, 1)
                        acc = jnp.where(group == i, part, acc)
            pack_ref[c, tile(t), :] = acc
        acc = jnp.where(group == 0, coef_ref[0, tile(t), :], 0.0)
        for i in range(1, NC):
            acc = jnp.where(group == i, pltpu.roll(coef_ref[i, tile(t), :], 8 * i, 1), acc)
        pack_ref[2, tile(t), :] = acc
    for f in range(NA):
        rows_ref[f] = q[f, 0:8, :] if f < NF else coef_ref[f - NF, 0:8, :]


def pairs():
    return [(k, m, (k + m) % K) for k in range(K) for m in range(5 if k < 4 else 4)]


def clear(red, sets):
    for n in range(sets):
        for k in range(4, K):
            red[5 * n + 4, 8 * k : 8 * k + 8, :] = jnp.zeros((8, X), F32)


def columns(result, lane, red, sets):
    for n, place in enumerate(sets):
        for m in range(5):
            acc = red[5 * n + m, pl.ds(0, 8, stride=8), :]
            for s in range(1, 8):
                acc = acc + red[5 * n + m, pl.ds(s, 8, stride=8), :]
            col = jnp.sum(acc, axis=1, keepdims=True)
            result = jnp.where(lane == 8 * place + m, col, result)
    return result


def own_kernel(q_ref, coef_ref, warm_ref, last_ref, sums_ref, red):
    lane = lanes()
    clear(red, 1)
    group = lane >> 3
    for t in range(Z // 8):
        last = [None] * 3
        for y in range(2):
            for k in range(K):
                i = 8 * y + k
                fields = [q_ref[4 * k + 2 * c + y, tile(t), :] for c in range(2)]
                fields.append(
                    coef_ref[y, tile(t), :] * fields[0] + coef_ref[2 + y, tile(t), :] * fields[1]
                )
                warm_ref[2 * k + y, tile(t), :] = fields[2]
                for n in range(3):
                    part = pltpu.roll(fields[n], (8 * i + 8) % X, 1) if i < 15 else fields[n]
                    last[n] = part if i == 0 else jnp.where(group == i, part, last[n])
        for n in range(3):
            last_ref[n, tile(t), :] = last[n]
    for k, m, l in pairs():
        acc = jnp.zeros((8, X), F32)
        for p in range(4):
            for t in range(Z // 8):
                acc = acc + q_ref[4 * k + p, tile(t), :] * q_ref[4 * l + p, tile(t), :]
        red[m, 8 * k : 8 * k + 8, :] = acc
    speed = jnp.zeros((8, X), F32)
    for y in range(2):
        for t in range(Z // 8):
            v = coef_ref[4 + y, tile(t), :]
            speed = speed + v * v
    result = jnp.where(lane == 40, jnp.sum(speed, axis=1, keepdims=True), 0.0)
    sums_ref[...] = columns(result, lane, red, (0,))


def corner_kernel(side_ref, corner_ref):
    for b in range(3):
        corner_ref[b] = side_ref[b, 0:8, :]


def side_of(packed, i):
    return pltpu.roll(packed, X - 8 * i, 1) if i else packed


def spread(packed, lane, n):
    out = jnp.where(lane < 8, side_of(packed, 2 * n), 0.0)
    out = jnp.where((lane >= 64) & (lane < 72), pltpu.roll(packed, 56 - 16 * n, 1), out)
    for d in (8, 16, 32):
        out = out + pltpu.roll(out, d, 1)
    return out


def packed_shifts(side, last, lane):
    col = lane & 7
    return (
        jnp.where(col < 1, pltpu.roll(last, 121, 1), pltpu.roll(side, 1, 1)),
        pltpu.roll(side, X - 1, 1),
        jnp.where(col < 2, pltpu.roll(last, 122, 1), pltpu.roll(side, 2, 1)),
        pltpu.roll(side, X - 2, 1),
    )


def wide_shifts(main, side, lane):
    ahead = jnp.where(lane < 2, side, main)
    return (
        pltpu.roll(main, 1, 1),
        pltpu.roll(ahead, X - 1, 1),
        pltpu.roll(main, 2, 1),
        pltpu.roll(ahead, X - 2, 1),
    )


def block_shifts(main, side, lane):
    return [
        pltpu.roll(jnp.where(lane < n, side, main), d, 1)
        for n, d in ((3, 1), (5, X - 1), (2, 2), (6, X - 2))
    ]


def rate(speed, xr, xe, xt, r_at, t_at, r_other, t_other):
    def lap(x, at, other):
        ones = x[0] + x[1] + (at(-1) + at(1)) + other
        twos = x[2] + x[3] + (at(-2) + at(2))
        return 16.0 * ones - twos - 90.0 * at(0)

    def slope(x):
        return 8.0 * (x[1] - x[0]) - (x[3] - x[2])

    rate_r = speed * slope(xr) + (viscosity / 12.0) * lap(xr, r_at, r_other)
    rate_e = speed * slope(xe) + (conductivity / 12.0) * lap(xt, t_at, t_other)
    return (rate_r, rate_e)


def cross_sums(red, qd, ad, bd, tiles):
    for k, m, l in pairs():
        acc = [jnp.zeros((8, X), F32)] * 4
        for p in range(4):
            for t in range(tiles):
                qk, ak, bk = (v[4 * k + p, tile(t), :] for v in (qd, ad, bd))
                ql, al, bl = (v[4 * l + p, tile(t), :] for v in (qd, ad, bd))
                acc[0] = acc[0] + (qk * al + ak * ql)
                acc[1] = acc[1] + (ak * al + (qk * bl + bk * ql))
                acc[2] = acc[2] + (ak * bl + bk * al)
                acc[3] = acc[3] + bk * bl
        for n in range(4):
            red[5 * n + m, 8 * k : 8 * k + 8, :] = acc[n]


def packed_rate(side, last, warm, pc, out, r, to, lane):
    rows = slice(r, r + 8)
    got = rate(
        pc[2, rows, :] * (-1.0 / 12.0),
        packed_shifts(side[0, rows, :], last[0, rows, :], lane),
        packed_shifts(side[1, rows, :], last[1, rows, :], lane),
        packed_shifts(warm[rows, :], last[2, rows, :], lane),
        lambda d: side[0, r + d : r + d + 8, :],
        lambda d: warm[r + d : r + d + 8, :],
        pltpu.roll(side[0, rows, :], 64, 1),
        pltpu.roll(warm[rows, :], 64, 1),
    )
    dest = slice(to, to + 8)
    out[0, dest, :] = got[0]
    out[1, dest, :] = got[1]
    out[2, dest, :] = pc[0, rows, :] * got[0] + pc[1, rows, :] * got[1]


def first_rate(field, coef, warm, side, side_warm, am, k, y, r, to, lane):
    i, rows = 8 * y + k, slice(r, r + 8)
    got = rate(
        coef(4 + y, r) * (-1.0 / 12.0),
        wide_shifts(field(4 * k + y, r), side_of(side[0, rows, :], i), lane),
        wide_shifts(field(4 * k + 2 + y, r), side_of(side[1, rows, :], i), lane),
        wide_shifts(warm(2 * k + y, r), side_of(side_warm[rows, :], i), lane),
        lambda d: field(4 * k + y, r + d),
        lambda d: warm(2 * k + y, r + d),
        field(4 * k + 1 - y, r),
        warm(2 * k + 1 - y, r),
    )
    for c in range(2):
        am[4 * k + 2 * c + y, to : to + 8, :] = got[c]


def middle(coef, am, pa, aw, tm, tw, k, y, r, here, lane):
    i, rows = 8 * y + k, slice(r, r + 8)
    main = [am[4 * k + 2 * c + y, rows, :] for c in range(2)]
    main.append(coef(y, here) * main[0] + coef(2 + y, here) * main[1])
    tm[2 * k + y, rows, :] = main[2]
    block = lane < 4
    aw[2 * k + y, rows, :] = jnp.where(block, side_of(pa[0, rows, :], i), main[0])
    tw[2 * k + y, rows, :] = jnp.where(block, side_of(pa[2, rows, :], i), main[2])


def second_rate(speed, am, pa, aw, tm, tw, ad, bd, k, y, r, to, lane):
    i, rows, dest = 8 * y + k, slice(r, r + 8), slice(to, to + 8)
    main = [am[4 * k + y, rows, :], am[4 * k + 2 + y, rows, :], tm[2 * k + y, rows, :]]
    side = [side_of(pa[n, rows, :], i) for n in range(3)]
    got = rate(
        speed * (-1.0 / 12.0),
        *(block_shifts(main[n], side[n], lane) for n in range(3)),
        lambda d: aw[2 * k + y, r + d : r + d + 8, :],
        lambda d: tw[2 * k + y, r + d : r + d + 8, :],
        aw[2 * k + 1 - y, rows, :],
        tw[2 * k + 1 - y, rows, :],
    )
    for c in range(2):
        bd[4 * k + 2 * c + y, dest, :] = 0.5 * got[c]
    ad[4 * k + y, dest, :] = aw[2 * k + y, rows, :]
    ad[4 * k + 2 + y, dest, :] = jnp.where(lane < 4, side[1], main[1])


def each():
    return [(k, y) for k in range(K) for y in range(2)]


def inner_kernel(
    q_ref, coef_ref, warm_ref, side_ref, last_ref, own_ref,
    ad_ref, bd_ref, tail_ref, packed_ref, sums_ref,
    pc, pt, pa, am, aw, tm, tw, qd, red,
):
    lane = lanes()
    block = lane < 4
    clear(red, 4)
    for t in range(Z // 8):
        for n in range(3):
            pc[n, tile(t), :] = spread(side_ref[2, tile(t), :], lane, n)
        pt[tile(t), :] = (
            pc[0, tile(t), :] * side_ref[0, tile(t), :] + pc[1, tile(t), :] * side_ref[1, tile(t), :]
        )
    for k, y in each():
        for c in range(2):
            for t in range(3):
                rows = slice(8 * t + 4, 8 * t + 12)
                f = 4 * k + 2 * c + y
                part = side_of(side_ref[c, rows, :], 8 * y + k)
                qd[f, tile(t), :] = jnp.where(block, part, q_ref[f, rows, :])

    def field(f, r):
        return q_ref[f, r : r + 8, :]

    def coef(f, r):
        return coef_ref[f, r : r + 8, :]

    def warm(f, r):
        return warm_ref[f, r : r + 8, :]

    starts = (2, 10, 18, 22)
    for r in starts:
        packed_rate(side_ref, last_ref, pt, pc, pa, r, r, lane)
    for k, y in each():
        for r in starts:
            first_rate(field, coef, warm, side_ref, pt, am, k, y, r, r, lane)
    for k, y in each():
        for r in starts:
            middle(coef, am, pa, aw, tm, tw, k, y, r, r, lane)
    for y in range(2):
        for t in range(3):
            r = 8 * t + 4
            side = side_of(side_ref[2, r : r + 8, :], 4 + y)
            speed = jnp.where(block, side, coef(4 + y, r))
            for k in range(K):
                second_rate(
                    speed, am, pa, aw, tm, tw, ad_ref, bd_ref, k, y, r, 8 * t, lane
                )
    for f in range(NF):
        tail_ref[f] = am[f, 22:30, :]
    for n in range(3):
        packed_ref[n] = pa[n, 22:30, :]
        packed_ref[3 + n] = pc[n, 24:32, :]
    cross_sums(red, qd, ad_ref, bd_ref, 3)
    sums_ref[...] = columns(own_ref[...], lane, red, range(1, 5))


def edge_kernel(
    q_ref, coef_ref, warm_ref, side_ref, last_ref, below_ref, corner_ref, tail_ref, packed_ref,
    inner_ref, ad_ref, bd_ref, sums_ref,
    em, wm, sm, lm, pc, pt, pa, am, aw, tm, tw, qd, red,
):
    lane = lanes()
    block = lane < 4
    group = lane >> 3
    clear(red, 4)
    for f in range(NA):
        em[f, 0:8, :] = q_ref[f, 24:32, :] if f < NF else coef_ref[f - NF, 24:32, :]
        em[f, 8:16, :] = below_ref[f]
    for n in range(3):
        sm[n, 0:8, :] = side_ref[n, 24:32, :]
        sm[n, 8:16, :] = corner_ref[n]
        lm[n, 0:8, :] = last_ref[n, 24:32, :]
        pc[n, 0:8, :] = packed_ref[3 + n]
        pc[n, 8:16, :] = spread(corner_ref[2], lane, n)
        pa[n, 0:8, :] = packed_ref[n]
    last = [None] * 3
    for y in range(2):
        for k in range(K):
            i = 8 * y + k
            fields = [below_ref[4 * k + 2 * c + y] for c in range(2)]
            fields.append(
                below_ref[NF + y] * fields[0] + below_ref[NF + 2 + y] * fields[1]
            )
            wm[2 * k + y, 0:8, :] = warm_ref[2 * k + y, 24:32, :]
            wm[2 * k + y, 8:16, :] = fields[2]
            for n in range(3):
                part = pltpu.roll(fields[n], (8 * i + 8) % X, 1) if i < 15 else fields[n]
                last[n] = part if i == 0 else jnp.where(group == i, part, last[n])
    for n in range(3):
        lm[n, 8:16, :] = last[n]
    for t in range(2):
        pt[tile(t), :] = pc[0, tile(t), :] * sm[0, tile(t), :] + pc[1, tile(t), :] * sm[1, tile(t), :]
    for f in range(NF):
        am[f, 0:8, :] = tail_ref[f]

    def field(f, r):
        return em[f, r : r + 8, :]

    def coef(f, r):
        return em[NF + f, r : r + 8, :]

    def warm(f, r):
        return wm[f, r : r + 8, :]

    packed_rate(sm, lm, pt, pc, pa, 6, 8, lane)
    for k, y in each():
        for c in range(2):
            f = 4 * k + 2 * c + y
            part = side_of(sm[c, 4:12, :], 8 * y + k)
            qd[f] = jnp.where(block, part, em[f, 4:12, :])
        first_rate(field, coef, warm, sm, pt, am, k, y, 6, 8, lane)
    for k, y in each():
        for r in (4, 8):
            middle(coef, am, pa, aw, tm, tw, k, y, r, r - 2, lane)
    for y in range(2):
        speed = jnp.where(block, side_of(sm[2, 4:12, :], 4 + y), coef(4 + y, 4))
        for k in range(K):
            second_rate(speed, am, pa, aw, tm, tw, ad_ref, bd_ref, k, y, 6, 0, lane)
    cross_sums(red, qd, ad_ref, bd_ref, 1)
    result = columns(jnp.zeros((8, X), F32), lane, red, range(1, 5)) + inner_ref[...]
    for n in range(sums_ref.shape[0]):
        sums_ref[n] = result


def give_kernel(ad_ref, bd_ref, ade_ref, bde_ref, out_ref):
    group = lanes() >> 2
    for n, (ref, edge) in enumerate(((ad_ref, ade_ref), (bd_ref, bde_ref))):
        for t in range(Z // 8):
            acc = jnp.zeros((8, X), F32)
            for f in range(NF):
                part = ref[f, tile(t), :] if t < 3 else edge[f]
                acc = jnp.where(group == f, pltpu.roll(part, 4 * f, 1) if f else part, acc)
            out_ref[n, tile(t), :] = acc


def place_kernel(ad_ref, bd_ref, ade_ref, bde_ref, got_ref, a_ref, b_ref, down_ref):
    block = lanes() < 4
    for n, (ref, edge, out) in enumerate(((ad_ref, ade_ref, a_ref), (bd_ref, bde_ref, b_ref))):
        for f in range(NF):
            for t in range(Z // 8):
                part = ref[f, tile(t), :] if t < 3 else edge[f]
                got = got_ref[n, tile(t), :]
                got = pltpu.roll(got, X - 4 * f, 1) if f else got
                part = jnp.where(block, got, part)
                if t < 3:
                    out[f, 8 * t + 4 : 8 * t + 12, :] = part
                else:
                    out[f, 28:32, :] = part[0:4, :]
                    out[f, 0:4, :] = jnp.zeros((4, X), F32)
                    r = 4 * (NF * n + f)
                    down_ref[r : r + 4, :] = part[4:8, :]


def finish_kernel(cells, q_ref, a_ref, b_ref, above_ref, sums_ref, out_ref, growth_ref, first):
    lane = lanes()
    row = lax.broadcasted_iota(jnp.int32, (8, X), 0)
    for n, ref in enumerate((a_ref, b_ref)):
        for f in range(NF):
            r = 4 * (NF * n + f)
            first[n, f, 0:4, :] = above_ref[r : r + 4, :]
            first[n, f, 4:8, :] = ref[f, 4:8, :]
    total = sums_ref[0]
    for n in range(1, sums_ref.shape[0]):
        total = total + sums_ref[n]
    speed = jnp.broadcast_to(jnp.sum(total[:, 40:41], axis=0, keepdims=True), (8, X))
    step = courant_number / jnp.sqrt(speed * (1.0 / cells) + 1e-05)
    gram = total
    power = step
    for n in range(1, 5):
        gram = gram + power * pltpu.roll(total, X - 8 * n, 1)
        power = power * step
    gram = gram * (1.0 / (2.0 * cells))
    cols = [jnp.broadcast_to(gram[:, m : m + 1], (8, X)) for m in range(5)]

    def entry(i, j):
        k, m = (j, i - j) if i - j <= 4 else (i, j - i + K)
        if m == 4:
            k = min(i, j)
        return jnp.broadcast_to(cols[m][k : k + 1, :], (8, X))

    low = [[None] * K for _ in range(K)]
    inv_diag = []
    for j in range(K):
        d = entry(j, j)
        for p in range(j):
            d = d - low[j][p] * low[j][p]
        root = jnp.sqrt(d)
        low[j][j] = root
        inv_diag.append(1.0 / root)
        for i in range(j + 1, K):
            v = entry(i, j)
            for p in range(j):
                v = v - low[i][p] * low[j][p]
            low[i][j] = v * inv_diag[j]
    inverse = [[None] * K for _ in range(K)]
    for j in range(K):
        inverse[j][j] = inv_diag[j]
        for i in range(j + 1, K):
            v = low[i][j] * inverse[j][j]
            for p in range(j + 1, i):
                v = v + low[i][p] * inverse[p][j]
            inverse[i][j] = -v * inv_diag[i]
    growth = jnp.zeros((8, X), F32)
    for i in range(K):
        for j in range(i + 1):
            growth = jnp.where((row == j) & (lane == i), low[i][j], growth)
    growth_ref[...] = growth
    square = step * step
    for p in range(4):
        for t in range(Z // 8):
            adv = []
            for k in range(K):
                f = 4 * k + p
                a, b = (
                    (first[0, f], first[1, f])
                    if t == 0
                    else (a_ref[f, tile(t), :], b_ref[f, tile(t), :])
                )
                adv.append(q_ref[f, tile(t), :] + step * a + square * b)
            for k in range(K):
                v = inverse[k][0] * adv[0]
                for j in range(1, k + 1):
                    v = v + inverse[k][j] * adv[j]
                out_ref[4 * k + p, tile(t), :] = v


def call(body, outs, scratch=(), cost=2000000, limit=24, **more):
    shapes = [jax.ShapeDtypeStruct(s, F32) for s in outs]
    return pl.pallas_call(
        body,
        out_shape=shapes,
        scratch_shapes=[pltpu.VMEM(s, F32) if isinstance(s, tuple) else s for s in scratch],
        compiler_params=pltpu.CompilerParams(vmem_limit_bytes=limit * 1024 * 1024),
        cost_estimate=pl.CostEstimate(flops=cost, bytes_accessed=cost, transcendentals=0),
        **more,
    )


def ring(array, axes, step):
    size = lax.axis_size(axes)
    return lax.ppermute(array, axes, [(i, (i + step) % size) for i in range(size)])


def gathered(array, axes):
    return lax.all_to_all(array, axes, 0, 0)


def per_device(tangents, mass, internal, velocity):
    cells = float(2 * Z * X * lax.axis_size(GX) * lax.axis_size(GZ))
    near, far = lax.axis_size(NEAR), lax.axis_size(FAR)
    whole, inner, edge = (NF, Z, X), (NF, 24, X), (NF, 8, X)
    half, small, red = (2 * K, Z, X), (3, Z, X), (20, 64, X)
    q = tangents.reshape(whole)
    coef, pack, rows = call(
        prep_kernel,
        [(NC, Z, X), small, (NA, 8, X)],
        [whole, (2, Z, X), (2, Z, X), pltpu.SemaphoreType.DMA((4,))],
        limit=60,
        in_specs=[pl.BlockSpec(memory_space=pl.ANY)] * 4,
    )(q, mass, internal, velocity)
    side = ring(pack, GX, -1)
    below = ring(rows, GZ, -1)
    warm, last, own = call(own_kernel, [half, small, (8, X)], [(5, 64, X)])(q, coef)
    side, warm, last, own = lax.optimization_barrier((side, warm, last, own))
    (corner,) = call(corner_kernel, [(3, 8, X)], cost=1000)(side)
    corner = ring(corner, GZ, -1)
    ad, bd, tail, packed, part = call(
        inner_kernel,
        [inner, inner, edge, (6, 8, X), (8, X)],
        [small, (Z, X), small, whole, half, half, half, inner, red],
    )(q, coef, warm, side, last, own)
    low, slim = (2 * K, 16, X), (3, 16, X)
    ade, bde, sums = call(
        edge_kernel,
        [edge, edge, (far, 8, X)],
        [(NA, 16, X), low, slim, slim, slim, (16, X), slim, (NF, 16, X), low, low, low, edge, red],
    )(q, coef, warm, side, last, below, corner, tail, packed, part)
    sums = jnp.sum(gathered(sums, FAR), axis=0)
    (give,) = call(give_kernel, [(2, Z, X)])(ad, bd, ade, bde)
    got = ring(give, GX, 1)
    a, b, down = call(place_kernel, [whole, whole, (8 * NF, X)])(ad, bd, ade, bde, got)
    above = ring(down, GZ, 1)
    sums = gathered(jnp.broadcast_to(sums, (near, 8, X)), NEAR)
    out, growth = call(
        functools.partial(finish_kernel, cells), [whole, (8, X)], [(2, NF, 8, X)]
    )(q, a, b, above, sums)
    return (out.reshape(tangents.shape), growth[:, :K])


def solution(mesh):
    gx, gz = mesh.devices.shape
    fine = Mesh(mesh.devices.reshape(gx // 4, 4, gz // 4, 4), GX + GZ)
    in_specs = (P(None, None, None, GZ, GX),) + (P(None, GZ, GX),) * 3
    out_specs = (P(None, None, None, GZ, GX), P())
    return jax.shard_map(
        per_device, mesh=fine, in_specs=in_specs, out_specs=out_specs, check_vma=False
    )
```

time: 65.6 us -> 72.4 us (1.10)
  the two profiles are of different devices: /device:TPU:4 before, /device:TPU:1 now
where the time goes in v3:
time: 72.4 us; the launch traced here: 72 us
  starting transfers between devices  38.3 us (53%)
  Pallas kernels  19.1 us (26%)
  waiting for transfers between devices  12.2 us (17%)
  local copies, waits for them, and re-layouts  1.53 us (2%)
  between operations  0.76 us (1%)
    ppermute x5, starting transfers between devices, ring(): lax.ppermute(array, axes, [(i, (i + step) % size) for i in range(size)])  27.5 us
    pallas_call x1, Pallas kernels, per_device(): call(inner_kernel, [inner, inner, edge, (6, 8, X), (8, X)], [small, (Z, X...  11.3 us
    all_to_all x2, starting transfers between devices, gathered(): return lax.all_to_all(array, axes, 0, 0)  10.8 us
    ppermute x5, waiting for transfers between devices, ring(): lax.ppermute(array, axes, [(i, (i + step) % size) for i in range(size)])  6.42 us
    all_to_all x2, waiting for transfers between devices, gathered(): return lax.all_to_all(array, axes, 0, 0)  5.82 us
    pallas_call x1, Pallas kernels, per_device(): call(edge_kernel, [edge, edge, (far, 8, X)], [(NA, 16, X), low, slim, sli...  3.44 us
    pallas_call x1, Pallas kernels, per_device(): call(prep_kernel, [(NC, Z, X), small, (NA, 8, X)], [whole, (2, Z, X), (2,...  2.09 us
  transfers between devices with their start and end apart: 7, of which 3 were waited for; matrix products, arithmetic and copies ran while one was open for 1% of the time, Pallas kernels for 17%

profile of v3, /device:TPU:1, one launch (start us, length us, event | category | flops | bytes accessed | tf_op | source)
XLA Modules:
  0.0 72.0 jit_solution(8064162237005906689)
XLA Ops:
  0.6 0.0 copy-start
  0.6 2.1 %shard_map.59 = (f32[6,32,128]{2,1,0:T(8,128)}, f32[3,32,128]{2,1,0:T(8,128)}, f32[38,8,128]{2,1,0:T(8,128)}) custom-call(f32[32,32,128]{2,1,0:T(8,128)} %bitcast.3, f32[2,32,128]{2,1,0:T(8,128)} %mass_hbm.1, f32[2,32,128]{2,1,0:T(8,128)} %internal_hbm.1, f32[2,32,128]{2,1,0:T(8,128)} %velocity_hbm.1), custom_call_target="tpu_custom_call" | custom-call | flops 2000000 | bytes 2000000 | tf_op jit(solution)/shard_map/pallas_call | solution.py:563
  2.7 8.8 %collective-permute-start.1 = (f32[38,8,128]{2,1,0:T(8,128)}, f32[38,8,128]{2,1,0:T(8,128)S(1)}, u32[]{:S(2)}, u32[]{:S(2)}) collective-permute-start(f32[38,8,128]{2,1,0:T(8,128)} %get-tuple-element.36), channel_id=1, source_target_pairs={{0,31},{1,0},{2,1},{3,2},{4,3},{5,4},{6,5},{7,6},{8,7},{9,8},{10,9... | collective-permute-start | bytes 466952 | tf_op jit(solution)/shard_map/ppermute | solution.py:550
  11.5 1.9 %collective-permute-start = (f32[3,32,128]{2,1,0:T(8,128)}, f32[3,32,128]{2,1,0:T(8,128)S(1)}, u32[]{:S(2)}, u32[]{:S(2)}) collective-permute-start(f32[3,32,128]{2,1,0:T(8,128)} %get-tuple-element.26), channel_id=1, source_target_pairs={{0,480},{32,0},{64,32},{96,64},{128,96},{160,128},{192,160},{224,1... | collective-permute-start | bytes 147464 | tf_op jit(solution)/shard_map/ppermute | solution.py:550
  13.5 0.0 copy-done
  13.5 0.0 copy-start.1
  13.5 0.9 %copy-done.1 = f32[6,32,128]{2,1,0:T(8,128)S(1)} copy-done((f32[6,32,128]{2,1,0:T(8,128)S(1)}, f32[6,32,128]{2,1,0:T(8,128)}, u32[]{:S(2)}) %copy-start.1) | copy-done | bytes 98328
  14.4 0.4 shard_map.60
  14.8 1.8 %collective-permute-done.side_ref = f32[3,32,128]{2,1,0:T(8,128)S(1)} collective-permute-done((f32[3,32,128]{2,1,0:T(8,128)}, f32[3,32,128]{2,1,0:T(8,128)S(1)}, u32[]{:S(2)}, u32[]{:S(2)}) %collective-permute-start) | collective-permute-done | bytes 49184 | tf_op jit(solution)/shard_map/ppermute | solution.py:550
  16.6 9.9 %collective-permute-start.2 = (f32[3,8,128]{2,1,0:T(8,128)S(1)}, f32[3,8,128]{2,1,0:T(8,128)S(1)}, u32[]{:S(2)}, u32[]{:S(2)}) collective-permute-start(f32[3,8,128]{2,1,0:T(8,128)S(1)} %shard_map.62), channel_id=1, source_target_pairs={{0,31},{1,0},{2,1},{3,2},{4,3},{5,4},{6,5},{7,6},{8,7},{9,8},{10,9... | collective-permute-start | bytes 36872 | tf_op jit(solution)/shard_map/ppermute | solution.py:550
  26.5 11.3 %shard_map.61 = (f32[32,24,128]{2,1,0:T(8,128)S(1)}, f32[32,24,128]{2,1,0:T(8,128)S(1)}, f32[32,8,128]{2,1,0:T(8,128)S(1)}, f32[6,8,128]{2,1,0:T(8,128)S(1)}, f32[8,128]{1,0:T(8,128)S(1)}) custom-call(f32[32,32,128]{2,1,0:T(8,128)S(1)} %bitcast.5, f32[6,32,128]{2,1,0:T(8,128)S(1)} %copy-done.1, f32[16,32,128]{2,1,0:T(8,128)S(1)} %get-tuple-element.30.warm_ref, ...), custom_call_target="tpu_custom_call" | custom-call | flops 2000000 | bytes 2000000 | tf_op jit(solution)/shard_map/pallas_call | solution.py:576
  37.7 0.0 collective-permute-done.2.corner_ref
  37.7 0.0 collective-permute-done.1.below_ref
  37.8 3.4 %shard_map.63 = (f32[32,8,128]{2,1,0:T(8,128)S(1)}, f32[32,8,128]{2,1,0:T(8,128)S(1)}, f32[32,8,128]{2,1,0:T(8,128)}) custom-call(f32[32,32,128]{2,1,0:T(8,128)S(1)} %bitcast.6, f32[6,32,128]{2,1,0:T(8,128)S(1)} %copy-done.1, f32[16,32,128]{2,1,0:T(8,128)S(1)} %get-tuple-element.30.warm_ref, f32[3,32,128]{2,1,0:T(8,128)S(1)} %collective-permute-done.side_ref, ...), custom_call_target="tpu_custom_call" | custom-call | flops 2000000 | bytes 2000000 | tf_op jit(solution)/shard_map/pallas_call | solution.py:582
  41.2 6.4 %all-to-all-start = ((f32[32,8,128]{2,1,0:T(8,128)}), f32[32,8,128]{2,1,0:T(8,128)S(1)}, u32[]{:S(2)}, u32[]{:S(2)}) async-start(f32[32,8,128]{2,1,0:T(8,128)} %get-tuple-element.45), calls=%async_computation | async-start | bytes 262144 | tf_op jit(solution)/shard_map/all_to_all | solution.py:554
  47.6 0.3 shard_map.64
  47.9 3.1 %collective-permute-start.3 = (f32[2,32,128]{2,1,0:T(8,128)S(1)}, f32[2,32,128]{2,1,0:T(8,128)S(1)}, u32[]{:S(2)}, u32[]{:S(2)}) collective-permute-start(f32[2,32,128]{2,1,0:T(8,128)S(1)} %shard_map.64), channel_id=1, source_target_pairs={{0,32},{32,64},{64,96},{96,128},{128,160},{160,192},{192,224},{224... | collective-permute-start | bytes 98312 | tf_op jit(solution)/shard_map/ppermute | solution.py:550
  51.0 4.6 %collective-permute-done.3.got_ref = f32[2,32,128]{2,1,0:T(8,128)S(1)} collective-permute-done((f32[2,32,128]{2,1,0:T(8,128)S(1)}, f32[2,32,128]{2,1,0:T(8,128)S(1)}, u32[]{:S(2)}, u32[]{:S(2)}) %collective-permute-start.3) | collective-permute-done | bytes 32800 | tf_op jit(solution)/shard_map/ppermute | solution.py:550
  55.6 0.3 shard_map.65
  55.9 3.9 %collective-permute-start.4 = (f32[256,128]{1,0:T(8,128)S(1)}, f32[256,128]{1,0:T(8,128)S(1)}, u32[]{:S(2)}, u32[]{:S(2)}) collective-permute-start(f32[256,128]{1,0:T(8,128)S(1)} %get-tuple-element.44), channel_id=1, source_target_pairs={{0,1},{1,2},{2,3},{3,4},{4,5},{5,6},{6,7},{7,8},{8,9},{9,10},{10,1... | collective-permute-start | bytes 393224 | tf_op jit(solution)/shard_map/ppermute | solution.py:550
  59.8 0.0 all-to-all-done
  59.9 0.6 broadcast_in_dim.3
  60.5 4.4 %all-to-all-start.1 = ((f32[16,8,128]{2,1,0:T(8,128)}), f32[16,8,128]{2,1,0:T(8,128)S(1)}, u32[]{:S(2)}, u32[]{:S(2)}) async-start(f32[16,8,128]{2,1,0:T(8,128)} %broadcast_in_dim.3), calls=%async_computation.1 | async-start | bytes 131072 | tf_op jit(solution)/shard_map/all_to_all | solution.py:554
  64.9 0.0 collective-permute-done.4.above_ref
  64.9 5.8 %all-to-all-done.1.sums_ref = f32[16,8,128]{2,1,0:T(8,128)S(1)} async-done(((f32[16,8,128]{2,1,0:T(8,128)}), f32[16,8,128]{2,1,0:T(8,128)S(1)}, u32[]{:S(2)}, u32[]{:S(2)}) %all-to-all-start.1) | async-done | bytes 65568 | tf_op jit(solution)/shard_map/all_to_all | solution.py:554
  70.7 1.3 %shard_map.66 = (f32[32,32,128]{2,1,0:T(8,128)}, f32[8,128]{1,0:T(8,128)}) custom-call(f32[32,32,128]{2,1,0:T(8,128)S(1)} %bitcast.7, f32[32,32,128]{2,1,0:T(8,128)S(1)} %get-tuple-element.42.a_ref, f32[32,32,128]{2,1,0:T(8,128)S(1)} %get-tuple-element.43.b_ref, f32[256,128]{1,0:T(8,128)S(1)} %collective-permute-done.4.above_ref, ...), custom_call_target="tpu_custom_call" | custom-call | flops 2000000 | bytes 2000000 | tf_op jit(solution)/shard_map/pallas_call | solution.py:593
  (2 shorter events, 0.0 us)
Async XLA Ops:
  0.6 12.8 %copy-start = (f32[8,2,2,32,128]{4,3,2,1,0:T(8,128)S(1)}, f32[8,2,2,32,128]{4,3,2,1,0:T(8,128)}, u32[]{:S(2)}) copy-start(f32[8,2,2,32,128]{4,3,2,1,0:T(8,128)} %param.4) | copy-start | bytes 1572868
  2.7 35.0 %collective-permute-start.1 = (f32[38,8,128]{2,1,0:T(8,128)}, f32[38,8,128]{2,1,0:T(8,128)S(1)}, u32[]{:S(2)}, u32[]{:S(2)}) collective-permute-start(f32[38,8,128]{2,1,0:T(8,128)} %get-tuple-element.36), channel_id=1, source_target_pairs={{0,31},{1,0},{2,1},{3,2},{4,3},{5,4},{6,5},{7,6},{8,7},{9,8},{10,9... | collective-permute-start | bytes 466952 | tf_op jit(solution)/shard_map/ppermute | solution.py:550
  11.5 5.0 %collective-permute-start = (f32[3,32,128]{2,1,0:T(8,128)}, f32[3,32,128]{2,1,0:T(8,128)S(1)}, u32[]{:S(2)}, u32[]{:S(2)}) collective-permute-start(f32[3,32,128]{2,1,0:T(8,128)} %get-tuple-element.26), channel_id=1, source_target_pairs={{0,480},{32,0},{64,32},{96,64},{128,96},{160,128},{192,160},{224,1... | collective-permute-start | bytes 147464 | tf_op jit(solution)/shard_map/ppermute | solution.py:550
  13.5 0.9 %copy-start.1 = (f32[6,32,128]{2,1,0:T(8,128)S(1)}, f32[6,32,128]{2,1,0:T(8,128)}, u32[]{:S(2)}) copy-start(f32[6,32,128]{2,1,0:T(8,128)} %get-tuple-element.25.coef_ref) | copy-start | bytes 294916
  16.6 21.2 %collective-permute-start.2 = (f32[3,8,128]{2,1,0:T(8,128)S(1)}, f32[3,8,128]{2,1,0:T(8,128)S(1)}, u32[]{:S(2)}, u32[]{:S(2)}) collective-permute-start(f32[3,8,128]{2,1,0:T(8,128)S(1)} %shard_map.62), channel_id=1, source_target_pairs={{0,31},{1,0},{2,1},{3,2},{4,3},{5,4},{6,5},{7,6},{8,7},{9,8},{10,9... | collective-permute-start | bytes 36872 | tf_op jit(solution)/shard_map/ppermute | solution.py:550
  41.2 18.6 %all-to-all-start = ((f32[32,8,128]{2,1,0:T(8,128)}), f32[32,8,128]{2,1,0:T(8,128)S(1)}, u32[]{:S(2)}, u32[]{:S(2)}) async-start(f32[32,8,128]{2,1,0:T(8,128)} %get-tuple-element.45), calls=%async_computation | async-start | bytes 262144 | tf_op jit(solution)/shard_map/all_to_all | solution.py:554
  47.9 7.7 %collective-permute-start.3 = (f32[2,32,128]{2,1,0:T(8,128)S(1)}, f32[2,32,128]{2,1,0:T(8,128)S(1)}, u32[]{:S(2)}, u32[]{:S(2)}) collective-permute-start(f32[2,32,128]{2,1,0:T(8,128)S(1)} %shard_map.64), channel_id=1, source_target_pairs={{0,32},{32,64},{64,96},{96,128},{128,160},{160,192},{192,224},{224... | collective-permute-start | bytes 98312 | tf_op jit(solution)/shard_map/ppermute | solution.py:550
  55.9 9.0 %collective-permute-start.4 = (f32[256,128]{1,0:T(8,128)S(1)}, f32[256,128]{1,0:T(8,128)S(1)}, u32[]{:S(2)}, u32[]{:S(2)}) collective-permute-start(f32[256,128]{1,0:T(8,128)S(1)} %get-tuple-element.44), channel_id=1, source_target_pairs={{0,1},{1,2},{2,3},{3,4},{4,5},{5,6},{6,7},{7,8},{8,9},{9,10},{10,1... | collective-permute-start | bytes 393224 | tf_op jit(solution)/shard_map/ppermute | solution.py:550
  60.5 10.2 %all-to-all-start.1 = ((f32[16,8,128]{2,1,0:T(8,128)}), f32[16,8,128]{2,1,0:T(8,128)S(1)}, u32[]{:S(2)}, u32[]{:S(2)}) async-start(f32[16,8,128]{2,1,0:T(8,128)} %broadcast_in_dim.3), calls=%async_computation.1 | async-start | bytes 131072 | tf_op jit(solution)/shard_map/all_to_all | solution.py:554

commit v4 on v3

v4 whole, which is shorter than its diff:
```python
import functools

import jax
import jax.numpy as jnp
import numpy as np
from jax import lax
from jax.experimental import pallas as pl
from jax.experimental.pallas import tpu as pltpu
from jax.sharding import Mesh, PartitionSpec as P

NEWTON = 4
isochoric_warmth_coefficient = 3.0
attraction = 0.5
acentric_coefficient_gradient = 0.6
covolume = 0.15
root_two = 1.4142135623730951
viscosity = 0.2
conductivity = 1.0
courant_number = 0.5

K = 8
NF = 4 * K
NC = 6
NA = NF + NC
Z = 32
X = 128
GX = ("xh", "xl")
GZ = ("zh", "zl")
NEAR = ("xl", "zl")
FAR = ("xh", "zh")
F32 = jnp.float32


def bands():
    first = {-2: 1.0, -1: -8.0, 1: 8.0, 2: -1.0}
    second = {-2: -1.0, -1: 16.0, 0: -30.0, 1: 16.0, 2: -1.0}
    main, packed = [], []
    for band in (first, second):
        w, v = np.zeros((X, X), np.float32), np.zeros((2 * X, 2 * X), np.float32)
        for d, value in band.items():
            for j in range(X):
                if 0 <= j + d < X:
                    w[j + d, j] = value
            for g in range(16):
                for j in range(16):
                    if 0 <= j + d < 16:
                        at = [X * (c // 8) + 8 * g + c % 8 for c in (j + d, j)]
                        v[at[0], at[1]] = value
        main.append(np.concatenate([w, w]))
        packed.append(v)
    return [
        np.concatenate(main, axis=1).astype(jnp.bfloat16),
        np.stack(packed).astype(jnp.bfloat16),
    ]


def departure(cell_mass_concentration):
    low_term = 1.0 + (1.0 - root_two) * covolume * cell_mass_concentration
    high_term = 1.0 + (1.0 + root_two) * covolume * cell_mass_concentration
    factor = attraction * (1.0 + acentric_coefficient_gradient) / (2.0 * root_two * covolume)
    value = factor * (jnp.log(low_term) - jnp.log(high_term))
    slope = factor * (
        (1.0 - root_two) * covolume / low_term - (1.0 + root_two) * covolume / high_term
    )
    return (value, slope)


def slopes(mass, internal):
    deviation, departure_slope = departure(mass)
    warmth = internal / isochoric_warmth_coefficient
    for _ in range(NEWTON):
        root = jnp.sqrt(warmth)
        multiplier = 1.0 + acentric_coefficient_gradient * (1.0 - root)
        mismatch = isochoric_warmth_coefficient * warmth + deviation * multiplier - internal
        gradient = isochoric_warmth_coefficient - deviation * acentric_coefficient_gradient / (
            2.0 * root
        )
        warmth = warmth - mismatch / gradient
    root = jnp.sqrt(warmth)
    multiplier = 1.0 + acentric_coefficient_gradient * (1.0 - root)
    gradient = isochoric_warmth_coefficient - deviation * acentric_coefficient_gradient / (
        2.0 * root
    )
    energy = 1.0 / gradient
    return (-departure_slope * multiplier * energy, energy)


def lanes():
    return lax.broadcasted_iota(jnp.int32, (8, X), 1)


def tile(t):
    return slice(8 * t, 8 * t + 8)


def prep_kernel(
    q_hbm, mass_hbm, internal_hbm, velocity_hbm, coef_ref, pack_ref, q, mass, internal, sems
):
    copies = [
        pltpu.make_async_copy(src, dst, sems.at[i])
        for i, (src, dst) in enumerate(
            (
                (mass_hbm, mass),
                (internal_hbm, internal),
                (velocity_hbm, coef_ref.at[pl.ds(4, 2)]),
                (q_hbm, q),
            )
        )
    ]
    for copy in copies:
        copy.start()
    copies[0].wait()
    copies[1].wait()
    density, energy = slopes(mass[...], internal[...])
    coef_ref[0:2] = density
    coef_ref[2:4] = energy
    copies[2].wait()
    copies[3].wait()
    group = lanes() >> 3
    for t in range(Z // 8):
        for c in range(2):
            acc = q[2 * c, tile(t), :]
            for y in range(2):
                for k in range(K):
                    i = 8 * y + k
                    if i:
                        part = pltpu.roll(q[4 * k + 2 * c + y, tile(t), :], 8 * i, 1)
                        acc = jnp.where(group == i, part, acc)
            pack_ref[c, tile(t), :] = acc
        acc = jnp.where(group == 0, coef_ref[0, tile(t), :], 0.0)
        for i in range(1, NC):
            acc = jnp.where(group == i, pltpu.roll(coef_ref[i, tile(t), :], 8 * i, 1), acc)
        pack_ref[2, tile(t), :] = acc


def rows_kernel(q_ref, rows_ref):
    for f in range(NF):
        rows_ref[f] = q_ref[f, 0:8, :]


def pairs():
    return [(k, m, (k + m) % K) for k in range(K) for m in range(5 if k < 4 else 4)]


def columns(result, lane, red, extra, sets):
    row = lax.broadcasted_iota(jnp.int32, (8, X), 0)
    mine = ((lane >> 3) & 7) == row
    for n, place in enumerate(sets):
        for m in range(5):
            acc = red[5 * n + m]
            if extra is not None:
                part = extra[5 * n + m]
                for d in (4, 2, 1):
                    part = part + pltpu.roll(part, d, 0)
                if m == 4:
                    acc = jnp.where(row < 4, acc + jnp.where(mine, part, 0.0), 0.0)
                else:
                    acc = acc + jnp.where(mine, part, 0.0)
            col = jnp.sum(acc, axis=1, keepdims=True)
            result = jnp.where(lane == 8 * place + m, col, result)
    return result


def put(red, n, k, acc):
    red[n, k : k + 1, :] = jnp.sum(acc, axis=0, keepdims=True)


def side_of(packed, i):
    return pltpu.roll(packed, X - 8 * i, 1) if i else packed


def fill(pair, lane):
    out = jnp.where(lane < 8, pair[0], 0.0)
    out = jnp.where((lane >= 64) & (lane < 72), pltpu.roll(pair[1], 64, 1), out)
    for d in (8, 16, 32):
        out = out + pltpu.roll(out, d, 1)
    return out


def own_kernel(q_ref, coef_ref, warm_ref, last_ref, sums_ref, red):
    lane = lanes()
    red[...] = jnp.zeros_like(red)
    group = lane >> 3
    for t in range(Z // 8):
        last = [None] * 3
        for y in range(2):
            for k in range(K):
                i = 8 * y + k
                fields = [q_ref[4 * k + 2 * c + y, tile(t), :] for c in range(2)]
                fields.append(
                    coef_ref[y, tile(t), :] * fields[0] + coef_ref[2 + y, tile(t), :] * fields[1]
                )
                warm_ref[2 * k + y, tile(t), :] = fields[2]
                for n in range(2):
                    part = pltpu.roll(fields[n], (8 * i + 8) % X, 1) if i < 15 else fields[n]
                    last[n] = part if i == 0 else jnp.where(group == i, part, last[n])
        full = [
            fill([pltpu.roll(coef_ref[2 * n + y, tile(t), :], 8, 1) for y in range(2)], lane)
            for n in range(3)
        ]
        last[2] = full[0] * last[0] + full[1] * last[1]
        for n in range(3):
            last_ref[n, tile(t), :] = last[n]
            last_ref[3 + n, tile(t), :] = full[n]
    for k, m, l in pairs():
        acc = jnp.zeros((8, X), F32)
        for p in range(4):
            for t in range(Z // 8):
                acc = acc + q_ref[4 * k + p, tile(t), :] * q_ref[4 * l + p, tile(t), :]
        put(red, m, k, acc)
    speed = jnp.zeros((8, X), F32)
    for y in range(2):
        for t in range(Z // 8):
            v = coef_ref[4 + y, tile(t), :]
            speed = speed + v * v
    result = jnp.where(lane == 40, jnp.sum(speed, axis=1, keepdims=True), 0.0)
    sums_ref[...] = columns(result, lane, red, None, (0,))


def join(side_ref, last_ref, packed, t, at, lane):
    rows = slice(at, at + 8)
    got = [side_ref[c, tile(t), :] for c in range(2)]
    third = side_ref[2, tile(t), :]
    full = [fill([side_of(third, 2 * n + y) for y in range(2)], lane) for n in range(3)]
    got.append(full[0] * got[0] + full[1] * got[1])
    for n, part in enumerate(got + full):
        packed[n, rows, 0:X] = last_ref[n, tile(t), :]
        packed[n, rows, X : 2 * X] = part


def corner_kernel(side_ref, last_ref, coef_ref, corner_ref, packed):
    join(side_ref, last_ref, packed, 0, 0, lanes())
    for n in range(6):
        corner_ref[n] = packed[n, :, 0:X]
        corner_ref[6 + n] = packed[n, :, X : 2 * X]
        corner_ref[12 + n] = coef_ref[n, 0:8, :]


def split(x):
    high = x.astype(jnp.bfloat16)
    return high, (x - high.astype(F32)).astype(jnp.bfloat16)


def product(x, w):
    return jnp.dot(x, w, preferred_element_type=F32)


def rest(at, other):
    return 16.0 * (at(-1) + at(1) + other) - (at(-2) + at(2)) - 60.0 * at(0)


def main_rate(speed, weights, r_at, e_at, t_at, r_other, t_other):
    both = product(jnp.concatenate(split(r_at(0)), axis=1), weights[...])
    slope = product(jnp.concatenate(split(e_at(0)), axis=1), weights[:, 0:X])
    bend = product(jnp.concatenate(split(t_at(0)), axis=1), weights[:, X : 2 * X])
    rate_r = speed * both[:, 0:X] + (viscosity / 12.0) * (both[:, X:] + rest(r_at, r_other))
    rate_e = speed * slope + (conductivity / 12.0) * (bend + rest(t_at, t_other))
    return rate_r, rate_e


def turned(x):
    return jnp.concatenate([pltpu.roll(x[:, 0:X], 64, 1), pltpu.roll(x[:, X:], 64, 1)], axis=1)


def packed_rate(speed, weights, at):
    def along(n, w):
        high, low = split(at(n, 0))
        return product(high, weights[w]) + product(low, weights[w])

    rate_r = speed * along(0, 0) + (viscosity / 12.0) * (
        along(0, 1) + rest(lambda d: at(0, d), turned(at(0, 0)))
    )
    rate_e = speed * along(1, 0) + (conductivity / 12.0) * (
        along(2, 1) + rest(lambda d: at(2, d), turned(at(2, 0)))
    )
    return rate_r, rate_e


def packed_steps(packed, wp, pa, blocks, first, second, count, lane):
    src, dst, height = first
    rows = slice(src, src + height)
    got = packed_rate(
        packed[5, rows, :] * (-1.0 / 12.0), wp, lambda n, d: packed[n, src + d : src + d + height, :]
    )
    out = slice(dst, dst + height)
    pa[0, out, :] = got[0]
    pa[1, out, :] = got[1]
    pa[2, out, :] = packed[3, rows, :] * got[0] + packed[4, rows, :] * got[1]
    here, there = second
    rows = slice(here, here + count)
    got = packed_rate(
        packed[5, rows, :] * (-1.0 / 12.0),
        wp,
        lambda n, d: pa[n, there + d : there + d + count, :],
    )
    qp, ap, bp = blocks
    low = (lax.broadcasted_iota(jnp.int32, (count, X), 1) & 7) < 4
    for c in range(2):
        for dest, value in (
            (qp, packed[c, rows, :]),
            (ap, pa[c, there : there + count, :]),
            (bp, 0.5 * got[c]),
        ):
            dest[c] = jnp.where(low, value[:, X:], value[:, 0:X])


def main_sums(red, q_at, ad, bd, tiles):
    for k, m, l in pairs():
        acc = [jnp.zeros((8, X), F32)] * 4
        for p in range(4):
            for t in range(tiles):
                qk, ql = q_at(4 * k + p, t), q_at(4 * l + p, t)
                ak, bk = (v[4 * k + p, tile(t), :] for v in (ad, bd))
                al, bl = (v[4 * l + p, tile(t), :] for v in (ad, bd))
                acc[0] = acc[0] + (qk * al + ak * ql)
                acc[1] = acc[1] + (ak * al + (qk * bl + bk * ql))
                acc[2] = acc[2] + (ak * bl + bk * al)
                acc[3] = acc[3] + bk * bl
        for n in range(4):
            put(red, 5 * n + m, k, acc[n])


def packed_sums(extra, blocks, tiles, lane):
    acc = [jnp.zeros((8, X), F32) for _ in range(20)]
    for c in range(2):
        for t in range(tiles):
            q, a, b = (ref[c, tile(t), :] for ref in blocks)
            for m in range(5):

                def other(v, m=m):
                    if m == 0:
                        return v
                    near = pltpu.roll(v, X - 8 * m, 1)
                    return jnp.where((lane & 63) < 64 - 8 * m, near, pltpu.roll(v, 64 - 8 * m, 1))

                ql, al, bl = other(q), other(a), other(b)
                acc[m] = acc[m] + (q * al + a * ql)
                acc[5 + m] = acc[5 + m] + (a * al + (q * bl + b * ql))
                acc[10 + m] = acc[10 + m] + (a * bl + b * al)
                acc[15 + m] = acc[15 + m] + b * bl
    for n in range(20):
        extra[n] = acc[n]


def inside(rows):
    lane = lax.broadcasted_iota(jnp.int32, (rows, X), 1)
    return (lane >= 4) & (lane < 124)


def inner_kernel(
    q_ref, coef_ref, warm_ref, side_ref, last_ref, own_ref, wm_ref, wp_ref,
    ad_ref, bd_ref, ap_ref, bp_ref, tail_ref, packed_ref, sums_ref,
    packed, pa, qp, am, tm, red, extra,
):
    lane = lanes()
    red[...] = jnp.zeros_like(red)
    for t in range(Z // 8):
        join(side_ref, last_ref, packed, t, 8 * t, lane)
    packed_steps(packed, wp_ref, pa, (qp, ap_ref, bp_ref), (2, 2, 28), (4, 4), 24, lane)
    packed_sums(extra, (qp, ap_ref, bp_ref), 3, lane)
    for n in range(3):
        packed_ref[n] = pa[n, 22:30, :]
    for n in range(6):
        packed_ref[3 + n] = packed[n, 24:32, :]
    keep = inside(24)

    def vector(k, carry):
        base = 4 * k
        for y in range(2):
            got = main_rate(
                coef_ref[4 + y, 2:30, :] * (-1.0 / 12.0),
                wm_ref,
                lambda d: q_ref[base + y, 2 + d : 30 + d, :],
                lambda d: q_ref[base + 2 + y, 2 + d : 30 + d, :],
                lambda d: warm_ref[2 * k + y, 2 + d : 30 + d, :],
                q_ref[base + 1 - y, 2:30, :],
                warm_ref[2 * k + 1 - y, 2:30, :],
            )
            for c in range(2):
                am[k, 2 * c + y, 2:30, :] = got[c]
            tm[k, y, 2:30, :] = coef_ref[y, 2:30, :] * got[0] + coef_ref[2 + y, 2:30, :] * got[1]
        for y in range(2):
            got = main_rate(
                coef_ref[4 + y, 4:28, :] * (-1.0 / 12.0),
                wm_ref,
                lambda d: am[k, y, 4 + d : 28 + d, :],
                lambda d: am[k, 2 + y, 4 + d : 28 + d, :],
                lambda d: tm[k, y, 4 + d : 28 + d, :],
                am[k, 1 - y, 4:28, :],
                tm[k, 1 - y, 4:28, :],
            )
            for c in range(2):
                i = base + 2 * c + y
                bd_ref[i] = jnp.where(keep, 0.5 * got[c], 0.0)
                ad_ref[i] = jnp.where(keep, am[k, 2 * c + y, 4:28, :], 0.0)
        for p in range(4):
            tail_ref[base + p] = am[k, p, 22:30, :]
        return carry

    lax.fori_loop(0, K, vector, 0)
    main_sums(red, lambda f, t: q_ref[f, 8 * t + 4 : 8 * t + 12, :], ad_ref, bd_ref, 3)
    sums_ref[...] = columns(own_ref[...], lane, red, extra, range(1, 5))


def edge_kernel(
    q_ref, coef_ref, warm_ref, below_ref, corner_ref, tail_ref, packed_ref, inner_ref, wm_ref, wp_ref,
    ad_ref, bd_ref, ap_ref, bp_ref, sums_ref,
    em, ec, wm, packed, pa, qp, am, tm, red, extra,
):
    lane = lanes()
    red[...] = jnp.zeros_like(red)
    for n in range(NC):
        ec[n, 0:8, :] = coef_ref[n, 24:32, :]
        ec[n, 8:16, :] = corner_ref[12 + n]
        packed[n, 0:8, :] = packed_ref[3 + n]
        packed[n, 8:16, 0:X] = corner_ref[n]
        packed[n, 8:16, X : 2 * X] = corner_ref[6 + n]
    for n in range(3):
        pa[n, 0:8, :] = packed_ref[n]
    packed_steps(packed, wp_ref, pa, (qp, ap_ref, bp_ref), (6, 8, 8), (4, 6), 8, lane)
    packed_sums(extra, (qp, ap_ref, bp_ref), 1, lane)
    keep = inside(8)

    def vector(k, carry):
        base = 4 * k
        for p in range(4):
            em[base + p, 0:8, :] = q_ref[base + p, 24:32, :]
            em[base + p, 8:16, :] = below_ref[base + p]
            am[k, p, 0:8, :] = tail_ref[base + p]
        for y in range(2):
            wm[k, y, 0:8, :] = warm_ref[2 * k + y, 24:32, :]
            wm[k, y, 8:16, :] = (
                ec[y, 8:16, :] * below_ref[base + y] + ec[2 + y, 8:16, :] * below_ref[base + 2 + y]
            )
        for y in range(2):
            got = main_rate(
                ec[4 + y, 6:14, :] * (-1.0 / 12.0),
                wm_ref,
                lambda d: em[base + y, 6 + d : 14 + d, :],
                lambda d: em[base + 2 + y, 6 + d : 14 + d, :],
                lambda d: wm[k, y, 6 + d : 14 + d, :],
                em[base + 1 - y, 6:14, :],
                wm[k, 1 - y, 6:14, :],
            )
            for c in range(2):
                am[k, 2 * c + y, 8:16, :] = got[c]
            tm[k, y, 8:16, :] = ec[y, 6:14, :] * got[0] + ec[2 + y, 6:14, :] * got[1]
            tm[k, y, 4:8, :] = (
                ec[y, 2:6, :] * am[k, y, 4:8, :] + ec[2 + y, 2:6, :] * am[k, 2 + y, 4:8, :]
            )
        for y in range(2):
            got = main_rate(
                ec[4 + y, 4:12, :] * (-1.0 / 12.0),
                wm_ref,
                lambda d: am[k, y, 6 + d : 14 + d, :],
                lambda d: am[k, 2 + y, 6 + d : 14 + d, :],
                lambda d: tm[k, y, 6 + d : 14 + d, :],
                am[k, 1 - y, 6:14, :],
                tm[k, 1 - y, 6:14, :],
            )
            for c in range(2):
                i = base + 2 * c + y
                bd_ref[i] = jnp.where(keep, 0.5 * got[c], 0.0)
                ad_ref[i] = jnp.where(keep, am[k, 2 * c + y, 6:14, :], 0.0)
        return carry

    lax.fori_loop(0, K, vector, 0)
    main_sums(red, lambda f, t: em[f, 4:12, :], ad_ref, bd_ref, 1)
    result = columns(jnp.zeros((8, X), F32), lane, red, extra, range(1, 5)) + inner_ref[...]
    for n in range(sums_ref.shape[0]):
        sums_ref[n] = result


def give_kernel(ap_ref, bp_ref, ape_ref, bpe_ref, out_ref):
    for n, (ref, edge) in enumerate(((ap_ref, ape_ref), (bp_ref, bpe_ref))):
        for c in range(2):
            out_ref[n, c, 0:24, :] = ref[c]
            out_ref[n, c, 24:32, :] = edge[c]


def place_kernel(ad_ref, bd_ref, ade_ref, bde_ref, mine_ref, got_ref, a_ref, b_ref, down_ref):
    lane = lanes()
    strip = (lane < 4) | (lane >= 124)
    low = (lane & 7) < 4
    for n, (ref, edge, out) in enumerate(((ad_ref, ade_ref, a_ref), (bd_ref, bde_ref, b_ref))):
        for c in range(2):
            for t in range(Z // 8):
                mine = pltpu.roll(mine_ref[n, c, tile(t), :], X - 8, 1)
                both = jnp.where(low, got_ref[n, c, tile(t), :], mine)
                for y in range(2):
                    for k in range(K):
                        f = 4 * k + 2 * c + y
                        part = ref[f, tile(t), :] if t < 3 else edge[f]
                        part = jnp.where(strip, side_of(both, 8 * y + k), part)
                        if t < 3:
                            out[f, 8 * t + 4 : 8 * t + 12, :] = part
                        else:
                            out[f, 28:32, :] = part[0:4, :]
                            out[f, 0:4, :] = jnp.zeros((4, X), F32)
                            r = 4 * (NF * n + f)
                            down_ref[r : r + 4, :] = part[4:8, :]


def finish_kernel(cells, q_ref, a_ref, b_ref, above_ref, sums_ref, out_ref, growth_ref, first):
    lane = lanes()
    row = lax.broadcasted_iota(jnp.int32, (8, X), 0)
    for n, ref in enumerate((a_ref, b_ref)):
        for f in range(NF):
            r = 4 * (NF * n + f)
            first[n, f, 0:4, :] = above_ref[r : r + 4, :]
            first[n, f, 4:8, :] = ref[f, 4:8, :]
    total = sums_ref[0]
    for n in range(1, sums_ref.shape[0]):
        total = total + sums_ref[n]
    speed = jnp.broadcast_to(jnp.sum(total[:, 40:41], axis=0, keepdims=True), (8, X))
    step = courant_number / jnp.sqrt(speed * (1.0 / cells) + 1e-05)
    gram = total
    power = step
    for n in range(1, 5):
        gram = gram + power * pltpu.roll(total, X - 8 * n, 1)
        power = power * step
    gram = gram * (1.0 / (2.0 * cells))
    cols = [jnp.broadcast_to(gram[:, m : m + 1], (8, X)) for m in range(5)]

    def entry(i, j):
        k, m = (j, i - j) if i - j <= 4 else (i, j - i + K)
        if m == 4:
            k = min(i, j)
        return jnp.broadcast_to(cols[m][k : k + 1, :], (8, X))

    low = [[None] * K for _ in range(K)]
    inv_diag = []
    for j in range(K):
        d = entry(j, j)
        for p in range(j):
            d = d - low[j][p] * low[j][p]
        root = jnp.sqrt(d)
        low[j][j] = root
        inv_diag.append(1.0 / root)
        for i in range(j + 1, K):
            v = entry(i, j)
            for p in range(j):
                v = v - low[i][p] * low[j][p]
            low[i][j] = v * inv_diag[j]
    inverse = [[None] * K for _ in range(K)]
    for j in range(K):
        inverse[j][j] = inv_diag[j]
        for i in range(j + 1, K):
            v = low[i][j] * inverse[j][j]
            for p in range(j + 1, i):
                v = v + low[i][p] * inverse[p][j]
            inverse[i][j] = -v * inv_diag[i]
    growth = jnp.zeros((8, X), F32)
    for i in range(K):
        for j in range(i + 1):
            growth = jnp.where((row == j) & (lane == i), low[i][j], growth)
    growth_ref[...] = growth
    square = step * step
    for p in range(4):
        for t in range(Z // 8):
            adv = []
            for k in range(K):
                f = 4 * k + p
                a, b = (
                    (first[0, f], first[1, f])
                    if t == 0
                    else (a_ref[f, tile(t), :], b_ref[f, tile(t), :])
                )
                adv.append(q_ref[f, tile(t), :] + step * a + square * b)
            for k in range(K):
                v = inverse[k][0] * adv[0]
                for j in range(1, k + 1):
                    v = v + inverse[k][j] * adv[j]
                out_ref[4 * k + p, tile(t), :] = v


def call(body, outs, scratch=(), cost=2000000, limit=24, **more):
    shapes = [jax.ShapeDtypeStruct(s, F32) for s in outs]
    return pl.pallas_call(
        body,
        out_shape=shapes,
        scratch_shapes=[pltpu.VMEM(s, F32) if isinstance(s, tuple) else s for s in scratch],
        compiler_params=pltpu.CompilerParams(vmem_limit_bytes=limit * 1024 * 1024),
        cost_estimate=pl.CostEstimate(flops=cost, bytes_accessed=cost, transcendentals=0),
        **more,
    )


def ring(array, axes, step):
    size = lax.axis_size(axes)
    return lax.ppermute(array, axes, [(i, (i + step) % size) for i in range(size)])


def gathered(array, axes):
    return lax.all_to_all(array, axes, 0, 0)


def per_device(tangents, mass, internal, velocity):
    cells = float(2 * Z * X * lax.axis_size(GX) * lax.axis_size(GZ))
    near, far = lax.axis_size(NEAR), lax.axis_size(FAR)
    whole, inner, edge = (NF, Z, X), (NF, 24, X), (NF, 8, X)
    half, small, red = (2 * K, Z, X), (3, Z, X), (20, 8, X)
    wm, wp = (jnp.asarray(w) for w in bands())
    q = tangents.reshape(whole)
    coef, pack = call(
        prep_kernel,
        [(NC, Z, X), small],
        [whole, (2, Z, X), (2, Z, X), pltpu.SemaphoreType.DMA((4,))],
        limit=60,
        in_specs=[pl.BlockSpec(memory_space=pl.ANY)] * 4,
    )(q, mass, internal, velocity)
    side = ring(pack, GX, -1)
    later, _ = lax.optimization_barrier((q, pack))
    (rows,) = call(rows_kernel, [edge], cost=1000)(later)
    below = ring(rows, GZ, -1)
    warm, last, own = call(own_kernel, [half, (6, Z, X), (8, X)], [(5, 8, X)])(q, coef)
    side, warm, last, own = lax.optimization_barrier((side, warm, last, own))
    (corner,) = call(corner_kernel, [(18, 8, X)], [(6, 8, 2 * X)], cost=1000)(side, last, coef)
    corner = ring(corner, GZ, -1)
    ad, bd, ap, bp, tail, packed, part = call(
        inner_kernel,
        [inner, inner, (2, 24, X), (2, 24, X), edge, (9, 8, 2 * X), (8, X)],
        [(6, Z, 2 * X), (3, Z, 2 * X), (2, 24, X), (K, 4, Z, X), (K, 2, Z, X), red, red],
    )(q, coef, warm, side, last, own, wm, wp)
    ade, bde, ape, bpe, sums = call(
        edge_kernel,
        [edge, edge, (2, 8, X), (2, 8, X), (far, 8, X)],
        [(NF, 16, X), (NC, 16, X), (K, 2, 16, X), (6, 16, 2 * X), (3, 16, 2 * X), (2, 8, X)]
        + [(K, 4, 16, X), (K, 2, 16, X), red, red],
    )(q, coef, warm, below, corner, tail, packed, part, wm, wp)
    sums = jnp.sum(gathered(sums, FAR), axis=0)
    (give,) = call(give_kernel, [(2, 2, Z, X)])(ap, bp, ape, bpe)
    got = ring(give, GX, 1)
    a, b, down = call(place_kernel, [whole, whole, (8 * NF, X)])(ad, bd, ade, bde, give, got)
    above = ring(down, GZ, 1)
    sums = gathered(jnp.broadcast_to(sums, (near, 8, X)), NEAR)
    out, growth = call(
        functools.partial(finish_kernel, cells), [whole, (8, X)], [(2, NF, 8, X)]
    )(q, a, b, above, sums)
    return (out.reshape(tangents.shape), growth[:, :K])


def solution(mesh):
    gx, gz = mesh.devices.shape
    fine = Mesh(mesh.devices.reshape(gx // 4, 4, gz // 4, 4), GX + GZ)
    in_specs = (P(None, None, None, GZ, GX),) + (P(None, GZ, GX),) * 3
    out_specs = (P(None, None, None, GZ, GX), P())
    return jax.shard_map(
        per_device, mesh=fine, in_specs=in_specs, out_specs=out_specs, check_vma=False
    )
```

time: 72.4 us -> 68.6 us (0.948)
  Pallas kernels: 19.1 us -> 14.6 us
  waiting for transfers between devices: 12.2 us -> 14.2 us
  local copies, waits for them, and re-layouts: 1.53 us -> 0.67 us
    pallas_call x7 -> x8, Pallas kernels: 17.9 us -> 13.3 us  [the longest x1 5.03 us: per_device(): call(inner_kernel, [inner, inner, (2, 24, X), (2, 24, X), edge, (9, 8, 2...]
    ppermute x5, waiting for transfers between devices: 6.42 us -> 8.36 us  [ring(): lax.ppermute(array, axes, [(i, (i + step) % size) for i in range(size)])]
    all_to_all x2, starting transfers between devices: 10.8 us -> 9.78 us  [gathered(): return lax.all_to_all(array, axes, 0, 0)]
    unnamed x4 -> x10, local copies, waits for them, and re-layouts: 0.89 us -> 0.03 us
  transfers between devices with their start and end apart: 7 -> 7, of which waited for: 3 -> 3; matrix products, arithmetic and copies ran while one was open for 1% -> 1% of each run, Pallas kernels for 17% -> 10%
where the time goes in v4:
time: 68.6 us; the launch traced here: 68.2 us
  starting transfers between devices  37.9 us (55%)
  Pallas kernels  14.6 us (21%)
  waiting for transfers between devices  14.2 us (21%)
  between operations  0.81 us (1%)
    ppermute x5, starting transfers between devices, ring(): lax.ppermute(array, axes, [(i, (i + step) % size) for i in range(size)])  28.1 us
    all_to_all x2, starting transfers between devices, gathered(): return lax.all_to_all(array, axes, 0, 0)  9.78 us
    ppermute x5, waiting for transfers between devices, ring(): lax.ppermute(array, axes, [(i, (i + step) % size) for i in range(size)])  8.36 us
    all_to_all x2, waiting for transfers between devices, gathered(): return lax.all_to_all(array, axes, 0, 0)  5.82 us
    pallas_call x1, Pallas kernels, per_device(): call(inner_kernel, [inner, inner, (2, 24, X), (2, 24, X), edge, (9, 8, 2...  5.03 us
    pallas_call x1, Pallas kernels, per_device(): call(edge_kernel, [edge, edge, (2, 8, X), (2, 8, X), (far, 8, X)], [(NF,...  4.52 us
    pallas_call x1, Pallas kernels, per_device(): call(prep_kernel, [(NC, Z, X), small], [whole, (2, Z, X), (2, Z, X), pltp...  2.02 us
  transfers between devices with their start and end apart: 7, of which 3 were waited for; matrix products, arithmetic and copies ran while one was open for 1% of the time, Pallas kernels for 10%

profile of v4, /device:TPU:1, one launch (start us, length us, event | category | flops | bytes accessed | tf_op | source)
XLA Modules:
  0.0 68.2 jit_solution(13149735318988809063)
XLA Ops:
  0.6 0.0 copy-start
  0.6 2.0 %shard_map.77 = (f32[6,32,128]{2,1,0:T(8,128)}, f32[3,32,128]{2,1,0:T(8,128)}) custom-call(f32[32,32,128]{2,1,0:T(8,128)} %bitcast.3, f32[2,32,128]{2,1,0:T(8,128)} %mass_hbm.1, f32[2,32,128]{2,1,0:T(8,128)} %internal_hbm.1, f32[2,32,128]{2,1,0:T(8,128)} %velocity_hbm.1), custom_call_target="tpu_custom_call" | custom-call | flops 2000000 | bytes 2000000 | tf_op jit(solution)/shard_map/pallas_call | solution.py:605
  2.7 0.0 copy-done
  2.7 0.0 copy-start.4
  2.7 0.0 copy-start.1
  2.7 8.9 %collective-permute-start.1 = (f32[32,8,128]{2,1,0:T(8,128)S(1)}, f32[32,8,128]{2,1,0:T(8,128)S(1)}, u32[]{:S(2)}, u32[]{:S(2)}) collective-permute-start(f32[32,8,128]{2,1,0:T(8,128)S(1)} %shard_map.80), channel_id=1, source_target_pairs={{0,31},{1,0},{2,1},{3,2},{4,3},{5,4},{6,5},{7,6},{8,7},{9,8},{10,9... | collective-permute-start | bytes 393224 | tf_op jit(solution)/shard_map/ppermute | solution.py:591
  11.7 0.0 copy-done.4
  11.7 1.9 %collective-permute-start = (f32[3,32,128]{2,1,0:T(8,128)S(1)}, f32[3,32,128]{2,1,0:T(8,128)S(1)}, u32[]{:S(2)}, u32[]{:S(2)}) collective-permute-start(f32[3,32,128]{2,1,0:T(8,128)S(1)} %copy-done.4), channel_id=1, source_target_pairs={{0,480},{32,0},{64,32},{96,64},{128,96},{160,128},{192,160},{224,1... | collective-permute-start | bytes 147464 | tf_op jit(solution)/shard_map/ppermute | solution.py:591
  13.6 0.0 copy-done.1
  13.6 0.0 copy-start.3
  13.6 0.5 shard_map.78
  14.1 0.0 copy-start.2
  14.1 2.4 %collective-permute-done.side_ref = f32[3,32,128]{2,1,0:T(8,128)S(1)} collective-permute-done((f32[3,32,128]{2,1,0:T(8,128)S(1)}, f32[3,32,128]{2,1,0:T(8,128)S(1)}, u32[]{:S(2)}, u32[]{:S(2)}) %collective-permute-start) | collective-permute-done | bytes 49184 | tf_op jit(solution)/shard_map/ppermute | solution.py:591
  16.5 0.3 shard_map.81
  16.8 9.8 %collective-permute-start.2 = (f32[18,8,128]{2,1,0:T(8,128)S(1)}, f32[18,8,128]{2,1,0:T(8,128)S(1)}, u32[]{:S(2)}, u32[]{:S(2)}) collective-permute-start(f32[18,8,128]{2,1,0:T(8,128)S(1)} %shard_map.81), channel_id=1, source_target_pairs={{0,31},{1,0},{2,1},{3,2},{4,3},{5,4},{6,5},{7,6},{8,7},{9,8},{10,9... | collective-permute-start | bytes 221192 | tf_op jit(solution)/shard_map/ppermute | solution.py:591
  26.6 0.0 copy-done.3
  26.6 0.0 copy-done.2
  26.6 5.0 %shard_map.79 = (f32[32,24,128]{2,1,0:T(8,128)S(1)}, f32[32,24,128]{2,1,0:T(8,128)S(1)}, f32[2,24,128]{2,1,0:T(8,128)S(1)}, f32[2,24,128]{2,1,0:T(8,128)S(1)}, f...) custom-call(f32[32,32,128]{2,1,0:T(8,128)S(1)} %bitcast.6, f32[6,32,128]{2,1,0:T(8,128)S(1)} %copy-done.1, ...), custom_call_target="tpu_custom_call" | custom-call | flops 2000000 | bytes 2000000 | tf_op jit(solution)/shard_map/pallas_call | solution.py:620
  31.7 0.0 collective-permute-done.2.corner_ref
  31.7 0.0 collective-permute-done.1.below_ref
  31.7 4.5 %shard_map.82 = (f32[32,8,128]{2,1,0:T(8,128)S(1)}, f32[32,8,128]{2,1,0:T(8,128)S(1)}, f32[2,8,128]{2,1,0:T(8,128)S(1)}, f32[2,8,128]{2,1,0:T(8,128)S(1)}, f32[32,8,128]{2,1,0:T(8,128)}) custom-call(f32[32,32,128]{2,1,0:T(8,128)S(1)} %bitcast.7, f32[6,32,128]{2,1,0:T(8,128)S(1)} %copy-done.1, f32[16,32,128]{2,1,0:T(8,128)S(1)} %get-tuple-element.34.warm_ref, ...), custom_call_target="tpu_custom_call" | custom-call | flops 2000000 | bytes 2000000 | tf_op jit(solution)/shard_map/pallas_call | solution.py:625
  36.2 6.2 %all-to-all-start = ((f32[32,8,128]{2,1,0:T(8,128)}), f32[32,8,128]{2,1,0:T(8,128)S(1)}, u32[]{:S(2)}, u32[]{:S(2)}) async-start(f32[32,8,128]{2,1,0:T(8,128)} %get-tuple-element.53), calls=%async_computation | async-start | bytes 262144 | tf_op jit(solution)/shard_map/all_to_all | solution.py:595
  42.4 3.1 %collective-permute-start.3 = (f32[2,2,32,128]{3,2,1,0:T(8,128)S(1)}, f32[2,2,32,128]{3,2,1,0:T(8,128)S(1)}, u32[]{:S(2)}, u32[]{:S(2)}) collective-permute-start(f32[2,2,32,128]{3,2,1,0:T(8,128)S(1)} %shard_map.83.mine_ref), channel_id=1, source_target_pairs={{0,32},{32,64},{64,96},{96,128},{128,160},{160,192},{192,224},{224... | collective-permute-start | bytes 196616 | tf_op jit(solution)/shard_map/ppermute | solution.py:591
  45.5 6.0 %collective-permute-done.3.got_ref = f32[2,2,32,128]{3,2,1,0:T(8,128)S(1)} collective-permute-done((f32[2,2,32,128]{3,2,1,0:T(8,128)S(1)}, f32[2,2,32,128]{3,2,1,0:T(8,128)S(1)}, u32[]{:S(2)}, u32[]{:S(2)}) %collective-permute-start.3) | collective-permute-done | bytes 65568 | tf_op jit(solution)/shard_map/ppermute | solution.py:591
  51.5 0.9 %shard_map.84 = (f32[32,32,128]{2,1,0:T(8,128)S(1)}, f32[32,32,128]{2,1,0:T(8,128)S(1)}, f32[256,128]{1,0:T(8,128)S(1)}) custom-call(f32[32,24,128]{2,1,0:T(8,128)S(1)} %get-tuple-element.38.ad_ref, f32[32,24,128]{2,1,0:T(8,128)S(1)} %get-tuple-element.39.bd_ref, f32[32,8,128]{2,1,0:T(8,128)S(1)} %get-tuple-element.44.ade_ref, ...), custom_call_target="tpu_custom_call" | custom-call | flops 2000000 | bytes 2000000 | tf_op jit(solution)/shard_map/pallas_call | solution.py:634
  52.4 4.5 %collective-permute-start.4 = (f32[256,128]{1,0:T(8,128)S(1)}, f32[256,128]{1,0:T(8,128)S(1)}, u32[]{:S(2)}, u32[]{:S(2)}) collective-permute-start(f32[256,128]{1,0:T(8,128)S(1)} %get-tuple-element.52), channel_id=1, source_target_pairs={{0,1},{1,2},{2,3},{3,4},{4,5},{5,6},{6,7},{7,8},{8,9},{9,10},{10,1... | collective-permute-start | bytes 393224 | tf_op jit(solution)/shard_map/ppermute | solution.py:591
  56.9 0.0 all-to-all-done
  56.9 0.6 broadcast_in_dim.3
  57.6 3.6 %all-to-all-start.1 = ((f32[16,8,128]{2,1,0:T(8,128)}), f32[16,8,128]{2,1,0:T(8,128)S(1)}, u32[]{:S(2)}, u32[]{:S(2)}) async-start(f32[16,8,128]{2,1,0:T(8,128)} %broadcast_in_dim.3), calls=%async_computation.1 | async-start | bytes 131072 | tf_op jit(solution)/shard_map/all_to_all | solution.py:595
  61.1 0.0 collective-permute-done.4.above_ref
  61.1 5.8 %all-to-all-done.1.sums_ref = f32[16,8,128]{2,1,0:T(8,128)S(1)} async-done(((f32[16,8,128]{2,1,0:T(8,128)}), f32[16,8,128]{2,1,0:T(8,128)S(1)}, u32[]{:S(2)}, u32[]{:S(2)}) %all-to-all-start.1) | async-done | bytes 65568 | tf_op jit(solution)/shard_map/all_to_all | solution.py:595
  67.0 1.3 %shard_map.85 = (f32[32,32,128]{2,1,0:T(8,128)}, f32[8,128]{1,0:T(8,128)}) custom-call(f32[32,32,128]{2,1,0:T(8,128)S(1)} %bitcast.8, f32[32,32,128]{2,1,0:T(8,128)S(1)} %get-tuple-element.50.a_ref, f32[32,32,128]{2,1,0:T(8,128)S(1)} %get-tuple-element.51.b_ref, f32[256,128]{1,0:T(8,128)S(1)} %collective-permute-done.4.above_ref, ...), custom_call_target="tpu_custom_call" | custom-call | flops 2000000 | bytes 2000000 | tf_op jit(solution)/shard_map/pallas_call | solution.py:637
  (3 shorter events, 0.1 us)
Async XLA Ops:
  0.6 2.0 %copy-start = (f32[8,2,2,32,128]{4,3,2,1,0:T(8,128)S(1)}, f32[8,2,2,32,128]{4,3,2,1,0:T(8,128)}, u32[]{:S(2)}) copy-start(f32[8,2,2,32,128]{4,3,2,1,0:T(8,128)} %param.6) | copy-start | bytes 1572868
  2.7 9.0 %copy-start.4 = (f32[3,32,128]{2,1,0:T(8,128)S(1)}, f32[3,32,128]{2,1,0:T(8,128)}, u32[]{:S(2)}) copy-start(f32[3,32,128]{2,1,0:T(8,128)} %get-tuple-element.30) | copy-start | bytes 147460
  2.7 10.9 %copy-start.1 = (f32[6,32,128]{2,1,0:T(8,128)S(1)}, f32[6,32,128]{2,1,0:T(8,128)}, u32[]{:S(2)}) copy-start(f32[6,32,128]{2,1,0:T(8,128)} %get-tuple-element.29.coef_ref) | copy-start | bytes 294916
  2.7 29.0 %collective-permute-start.1 = (f32[32,8,128]{2,1,0:T(8,128)S(1)}, f32[32,8,128]{2,1,0:T(8,128)S(1)}, u32[]{:S(2)}, u32[]{:S(2)}) collective-permute-start(f32[32,8,128]{2,1,0:T(8,128)S(1)} %shard_map.80), channel_id=1, source_target_pairs={{0,31},{1,0},{2,1},{3,2},{4,3},{5,4},{6,5},{7,6},{8,7},{9,8},{10,9... | collective-permute-start | bytes 393224 | tf_op jit(solution)/shard_map/ppermute | solution.py:591
  11.7 4.8 %collective-permute-start = (f32[3,32,128]{2,1,0:T(8,128)S(1)}, f32[3,32,128]{2,1,0:T(8,128)S(1)}, u32[]{:S(2)}, u32[]{:S(2)}) collective-permute-start(f32[3,32,128]{2,1,0:T(8,128)S(1)} %copy-done.4), channel_id=1, source_target_pairs={{0,480},{32,0},{64,32},{96,64},{128,96},{160,128},{192,160},{224,1... | collective-permute-start | bytes 147464 | tf_op jit(solution)/shard_map/ppermute | solution.py:591
  13.6 13.0 %copy-start.3 = (bf16[256,256]{1,0:T(8,128)(2,1)S(1)}, bf16[256,256]{1,0:T(8,128)(2,1)}, u32[]{:S(2)}) copy-start(bf16[256,256]{1,0:T(8,128)(2,1)} %constant.6.clone.wm_ref) | copy-start | bytes 393220
  14.1 12.5 %copy-start.2 = (bf16[2,256,256]{2,1,0:T(8,128)(2,1)S(1)}, bf16[2,256,256]{2,1,0:T(8,128)(2,1)}, u32[]{:S(2)}) copy-start(bf16[2,256,256]{2,1,0:T(8,128)(2,1)} %constant.7.clone.wp_ref) | copy-start | bytes 786436
  16.8 14.8 %collective-permute-start.2 = (f32[18,8,128]{2,1,0:T(8,128)S(1)}, f32[18,8,128]{2,1,0:T(8,128)S(1)}, u32[]{:S(2)}, u32[]{:S(2)}) collective-permute-start(f32[18,8,128]{2,1,0:T(8,128)S(1)} %shard_map.81), channel_id=1, source_target_pairs={{0,31},{1,0},{2,1},{3,2},{4,3},{5,4},{6,5},{7,6},{8,7},{9,8},{10,9... | collective-permute-start | bytes 221192 | tf_op jit(solution)/shard_map/ppermute | solution.py:591
  36.2 20.7 %all-to-all-start = ((f32[32,8,128]{2,1,0:T(8,128)}), f32[32,8,128]{2,1,0:T(8,128)S(1)}, u32[]{:S(2)}, u32[]{:S(2)}) async-start(f32[32,8,128]{2,1,0:T(8,128)} %get-tuple-element.53), calls=%async_computation | async-start | bytes 262144 | tf_op jit(solution)/shard_map/all_to_all | solution.py:595
  42.4 9.0 %collective-permute-start.3 = (f32[2,2,32,128]{3,2,1,0:T(8,128)S(1)}, f32[2,2,32,128]{3,2,1,0:T(8,128)S(1)}, u32[]{:S(2)}, u32[]{:S(2)}) collective-permute-start(f32[2,2,32,128]{3,2,1,0:T(8,128)S(1)} %shard_map.83.mine_ref), channel_id=1, source_target_pairs={{0,32},{32,64},{64,96},{96,128},{128,160},{160,192},{192,224},{224... | collective-permute-start | bytes 196616 | tf_op jit(solution)/shard_map/ppermute | solution.py:591
  52.4 8.7 %collective-permute-start.4 = (f32[256,128]{1,0:T(8,128)S(1)}, f32[256,128]{1,0:T(8,128)S(1)}, u32[]{:S(2)}, u32[]{:S(2)}) collective-permute-start(f32[256,128]{1,0:T(8,128)S(1)} %get-tuple-element.52), channel_id=1, source_target_pairs={{0,1},{1,2},{2,3},{3,4},{4,5},{5,6},{6,7},{7,8},{8,9},{9,10},{10,1... | collective-permute-start | bytes 393224 | tf_op jit(solution)/shard_map/ppermute | solution.py:591
  57.6 9.4 %all-to-all-start.1 = ((f32[16,8,128]{2,1,0:T(8,128)}), f32[16,8,128]{2,1,0:T(8,128)S(1)}, u32[]{:S(2)}, u32[]{:S(2)}) async-start(f32[16,8,128]{2,1,0:T(8,128)} %broadcast_in_dim.3), calls=%async_computation.1 | async-start | bytes 131072 | tf_op jit(solution)/shard_map/all_to_all | solution.py:595

commit v5 on v4

--- a/solution.py
+++ b/solution.py
@@ -29,6 +29,7 @@
 NEAR = ("xl", "zl")
 FAR = ("xh", "zh")
 F32 = jnp.float32
+STEP = 4
 
 
 def bands():
@@ -145,19 +146,28 @@
 def columns(result, lane, red, extra, sets):
     row = lax.broadcasted_iota(jnp.int32, (8, X), 0)
     mine = ((lane >> 3) & 7) == row
-    for n, place in enumerate(sets):
+    rows = []
+    for n in range(len(sets)):
         for m in range(5):
             acc = red[5 * n + m]
             if extra is not None:
                 part = extra[5 * n + m]
                 for d in (4, 2, 1):
                     part = part + pltpu.roll(part, d, 0)
-                if m == 4:
-                    acc = jnp.where(row < 4, acc + jnp.where(mine, part, 0.0), 0.0)
-                else:
-                    acc = acc + jnp.where(mine, part, 0.0)
-            col = jnp.sum(acc, axis=1, keepdims=True)
-            result = jnp.where(lane == 8 * place + m, col, result)
+                acc = acc + jnp.where(mine, part, 0.0)
+            rows.append(jnp.where(row < 4, acc, 0.0) if m == 4 else acc)
+    if len(rows) % 2:
+        rows.append(rows[-1])
+    rows = jnp.concatenate(rows, axis=0)
+    high, low = split(rows)
+    last = (rows - high.astype(F32) - low.astype(F32)).astype(jnp.bfloat16)
+    total = product(
+        jnp.concatenate([high, low, last], axis=1), jnp.ones((3 * X, X), jnp.bfloat16)
+    )
+    for n, place in enumerate(sets):
+        for m in range(5):
+            at = 8 * (5 * n + m)
+            result = jnp.where(lane == 8 * place + m, total[at : at + 8, :], result)
     return result
 
 
@@ -249,12 +259,29 @@
     return 16.0 * (at(-1) + at(1) + other) - (at(-2) + at(2)) - 60.0 * at(0)
 
 
-def main_rate(speed, weights, r_at, e_at, t_at, r_other, t_other):
-    both = product(jnp.concatenate(split(r_at(0)), axis=1), weights[...])
-    slope = product(jnp.concatenate(split(e_at(0)), axis=1), weights[:, 0:X])
-    bend = product(jnp.concatenate(split(t_at(0)), axis=1), weights[:, X : 2 * X])
-    rate_r = speed * both[:, 0:X] + (viscosity / 12.0) * (both[:, X:] + rest(r_at, r_other))
-    rate_e = speed * slope + (conductivity / 12.0) * (bend + rest(t_at, t_other))
+def each():
+    return [(k, y) for k in range(K) for y in range(2)]
+
+
+def main_rates(count, weights, r_at, e_at, t_at):
+    def stack(at):
+        rows = jnp.concatenate([at(i) for i in range(count)], axis=0)
+        return jnp.concatenate(split(rows), axis=1)
+
+    both = product(stack(r_at), weights[...])
+    slope = product(stack(e_at), weights[:, 0:X])
+    bend = product(stack(t_at), weights[:, X : 2 * X])
+    out = []
+    for i in range(count):
+        rows = slice(8 * i, 8 * i + 8)
+        out.append((both[rows, 0:X], both[rows, X:], slope[rows], bend[rows]))
+    return out
+
+
+def main_rate(speed, parts, r_at, t_at, r_other, t_other):
+    slope_r, bend_r, slope_e, bend_t = parts
+    rate_r = speed * slope_r + (viscosity / 12.0) * (bend_r + rest(r_at, r_other))
+    rate_e = speed * slope_e + (conductivity / 12.0) * (bend_t + rest(t_at, t_other))
     return rate_r, rate_e
 
 
@@ -362,42 +389,59 @@
         packed_ref[n] = pa[n, 22:30, :]
     for n in range(6):
         packed_ref[3 + n] = packed[n, 24:32, :]
-    keep = inside(24)
-
-    def vector(k, carry):
-        base = 4 * k
-        for y in range(2):
+    keep = inside(8)
+
+    def vectors(j, carry):
+        planes = [(STEP * j + i, y) for i in range(STEP) for y in range(2)]
+        order = [(k, y, r) for k, y in planes for r in (2, 10, 18, 22)]
+        parts = main_rates(
+            len(order),
+            wm_ref,
+            lambda i: q_ref[4 * order[i][0] + order[i][1], order[i][2] : order[i][2] + 8, :],
+            lambda i: q_ref[4 * order[i][0] + 2 + order[i][1], order[i][2] : order[i][2] + 8, :],
+            lambda i: warm_ref[2 * order[i][0] + order[i][1], order[i][2] : order[i][2] + 8, :],
+        )
+        for i, (k, y, r) in enumerate(order):
+            rows = slice(r, r + 8)
             got = main_rate(
-                coef_ref[4 + y, 2:30, :] * (-1.0 / 12.0),
-                wm_ref,
-                lambda d: q_ref[base + y, 2 + d : 30 + d, :],
-                lambda d: q_ref[base + 2 + y, 2 + d : 30 + d, :],
-                lambda d: warm_ref[2 * k + y, 2 + d : 30 + d, :],
-                q_ref[base + 1 - y, 2:30, :],
-                warm_ref[2 * k + 1 - y, 2:30, :],
+                coef_ref[4 + y, rows, :] * (-1.0 / 12.0),
+                parts[i],
+                lambda d: q_ref[4 * k + y, r + d : r + d + 8, :],
+                lambda d: warm_ref[2 * k + y, r + d : r + d + 8, :],
+                q_ref[4 * k + 1 - y, rows, :],
+                warm_ref[2 * k + 1 - y, rows, :],
             )
             for c in range(2):
-                am[k, 2 * c + y, 2:30, :] = got[c]
-            tm[k, y, 2:30, :] = coef_ref[y, 2:30, :] * got[0] + coef_ref[2 + y, 2:30, :] * got[1]
-        for y in range(2):
+                am[k, 2 * c + y, rows, :] = got[c]
+            tm[k, y, rows, :] = coef_ref[y, rows, :] * got[0] + coef_ref[2 + y, rows, :] * got[1]
+        order = [(k, y, r) for k, y in planes for r in (4, 12, 20)]
+        parts = main_rates(
+            len(order),
+            wm_ref,
+            lambda i: am[order[i][0], order[i][1], order[i][2] : order[i][2] + 8, :],
+            lambda i: am[order[i][0], 2 + order[i][1], order[i][2] : order[i][2] + 8, :],
+            lambda i: tm[order[i][0], order[i][1], order[i][2] : order[i][2] + 8, :],
+        )
+        for i, (k, y, r) in enumerate(order):
+            rows = slice(r, r + 8)
             got = main_rate(
-                coef_ref[4 + y, 4:28, :] * (-1.0 / 12.0),
-                wm_ref,
-                lambda d: am[k, y, 4 + d : 28 + d, :],
-                lambda d: am[k, 2 + y, 4 + d : 28 + d, :],
-                lambda d: tm[k, y, 4 + d : 28 + d, :],
-                am[k, 1 - y, 4:28, :],
-                tm[k, 1 - y, 4:28, :],
+                coef_ref[4 + y, rows, :] * (-1.0 / 12.0),
+                parts[i],
+                lambda d: am[k, y, r + d : r + d + 8, :],
+                lambda d: tm[k, y, r + d : r + d + 8, :],
+                am[k, 1 - y, rows, :],
+                tm[k, 1 - y, rows, :],
             )
             for c in range(2):
-                i = base + 2 * c + y
-                bd_ref[i] = jnp.where(keep, 0.5 * got[c], 0.0)
-                ad_ref[i] = jnp.where(keep, am[k, 2 * c + y, 4:28, :], 0.0)
-        for p in range(4):
-            tail_ref[base + p] = am[k, p, 22:30, :]
+                f = 4 * k + 2 * c + y
+                bd_ref[f, r - 4 : r + 4, :] = jnp.where(keep, 0.5 * got[c], 0.0)
+                ad_ref[f, r - 4 : r + 4, :] = jnp.where(keep, am[k, 2 * c + y, rows, :], 0.0)
+        for k in [STEP * j + i for i in range(STEP)]:
+            for p in range(4):
+                tail_ref[4 * k + p] = am[k, p, 22:30, :]
         return carry
 
-    lax.fori_loop(0, K, vector, 0)
+    lax.fori_loop(0, K // STEP, vectors, 0)
     main_sums(red, lambda f, t: q_ref[f, 8 * t + 4 : 8 * t + 12, :], ad_ref, bd_ref, 3)
     sums_ref[...] = columns(own_ref[...], lane, red, extra, range(1, 5))
 
@@ -420,8 +464,7 @@
     packed_steps(packed, wp_ref, pa, (qp, ap_ref, bp_ref), (6, 8, 8), (4, 6), 8, lane)
     packed_sums(extra, (qp, ap_ref, bp_ref), 1, lane)
     keep = inside(8)
-
-    def vector(k, carry):
+    for k in range(K):
         base = 4 * k
         for p in range(4):
             em[base + p, 0:8, :] = q_ref[base + p, 24:32, :]
@@ -432,39 +475,49 @@
             wm[k, y, 8:16, :] = (
                 ec[y, 8:16, :] * below_ref[base + y] + ec[2 + y, 8:16, :] * below_ref[base + 2 + y]
             )
-        for y in range(2):
-            got = main_rate(
-                ec[4 + y, 6:14, :] * (-1.0 / 12.0),
-                wm_ref,
-                lambda d: em[base + y, 6 + d : 14 + d, :],
-                lambda d: em[base + 2 + y, 6 + d : 14 + d, :],
-                lambda d: wm[k, y, 6 + d : 14 + d, :],
-                em[base + 1 - y, 6:14, :],
-                wm[k, 1 - y, 6:14, :],
-            )
-            for c in range(2):
-                am[k, 2 * c + y, 8:16, :] = got[c]
-            tm[k, y, 8:16, :] = ec[y, 6:14, :] * got[0] + ec[2 + y, 6:14, :] * got[1]
-            tm[k, y, 4:8, :] = (
-                ec[y, 2:6, :] * am[k, y, 4:8, :] + ec[2 + y, 2:6, :] * am[k, 2 + y, 4:8, :]
-            )
-        for y in range(2):
-            got = main_rate(
-                ec[4 + y, 4:12, :] * (-1.0 / 12.0),
-                wm_ref,
-                lambda d: am[k, y, 6 + d : 14 + d, :],
-                lambda d: am[k, 2 + y, 6 + d : 14 + d, :],
-                lambda d: tm[k, y, 6 + d : 14 + d, :],
-                am[k, 1 - y, 6:14, :],
-                tm[k, 1 - y, 6:14, :],
-            )
-            for c in range(2):
-                i = base + 2 * c + y
-                bd_ref[i] = jnp.where(keep, 0.5 * got[c], 0.0)
-                ad_ref[i] = jnp.where(keep, am[k, 2 * c + y, 6:14, :], 0.0)
-        return carry
-
-    lax.fori_loop(0, K, vector, 0)
+    order = each()
+    parts = main_rates(
+        16,
+        wm_ref,
+        lambda i: em[4 * order[i][0] + order[i][1], 6:14, :],
+        lambda i: em[4 * order[i][0] + 2 + order[i][1], 6:14, :],
+        lambda i: wm[order[i][0], order[i][1], 6:14, :],
+    )
+    for i, (k, y) in enumerate(order):
+        got = main_rate(
+            ec[4 + y, 6:14, :] * (-1.0 / 12.0),
+            parts[i],
+            lambda d: em[4 * k + y, 6 + d : 14 + d, :],
+            lambda d: wm[k, y, 6 + d : 14 + d, :],
+            em[4 * k + 1 - y, 6:14, :],
+            wm[k, 1 - y, 6:14, :],
+        )
+        for c in range(2):
+            am[k, 2 * c + y, 8:16, :] = got[c]
+        tm[k, y, 8:16, :] = ec[y, 6:14, :] * got[0] + ec[2 + y, 6:14, :] * got[1]
+        tm[k, y, 4:8, :] = (
+            ec[y, 2:6, :] * am[k, y, 4:8, :] + ec[2 + y, 2:6, :] * am[k, 2 + y, 4:8, :]
+        )
+    parts = main_rates(
+        16,
+        wm_ref,
+        lambda i: am[order[i][0], order[i][1], 6:14, :],
+        lambda i: am[order[i][0], 2 + order[i][1], 6:14, :],
+        lambda i: tm[order[i][0], order[i][1], 6:14, :],
+    )
+    for i, (k, y) in enumerate(order):
+        got = main_rate(
+            ec[4 + y, 4:12, :] * (-1.0 / 12.0),
+            parts[i],
+            lambda d: am[k, y, 6 + d : 14 + d, :],
+            lambda d: tm[k, y, 6 + d : 14 + d, :],
+            am[k, 1 - y, 6:14, :],
+            tm[k, 1 - y, 6:14, :],
+        )
+        for c in range(2):
+            f = 4 * k + 2 * c + y
+            bd_ref[f] = jnp.where(keep, 0.5 * got[c], 0.0)
+            ad_ref[f] = jnp.where(keep, am[k, 2 * c + y, 6:14, :], 0.0)
     main_sums(red, lambda f, t: em[f, 4:12, :], ad_ref, bd_ref, 1)
     result = columns(jnp.zeros((8, X), F32), lane, red, extra, range(1, 5)) + inner_ref[...]
     for n in range(sums_ref.shape[0]):
@@ -624,16 +677,17 @@
     )(q, coef, warm, side, last, own, wm, wp)
     ade, bde, ape, bpe, sums = call(
         edge_kernel,
-        [edge, edge, (2, 8, X), (2, 8, X), (far, 8, X)],
+        [edge, edge, (2, 8, X), (2, 8, X), (near, 8, X)],
         [(NF, 16, X), (NC, 16, X), (K, 2, 16, X), (6, 16, 2 * X), (3, 16, 2 * X), (2, 8, X)]
         + [(K, 4, 16, X), (K, 2, 16, X), red, red],
     )(q, coef, warm, below, corner, tail, packed, part, wm, wp)
-    sums = jnp.sum(gathered(sums, FAR), axis=0)
+    sums = jnp.sum(gathered(sums, NEAR), axis=0)
     (give,) = call(give_kernel, [(2, 2, Z, X)])(ap, bp, ape, bpe)
     got = ring(give, GX, 1)
+    sums, got = lax.optimization_barrier((sums, got))
+    sums = gathered(jnp.broadcast_to(sums, (far, 8, X)), FAR)
     a, b, down = call(place_kernel, [whole, whole, (8 * NF, X)])(ad, bd, ade, bde, give, got)
     above = ring(down, GZ, 1)
-    sums = gathered(jnp.broadcast_to(sums, (near, 8, X)), NEAR)
     out, growth = call(
         functools.partial(finish_kernel, cells), [whole, (8, X)], [(2, NF, 8, X)]
     )(q, a, b, above, sums)

time: 68.6 us -> 66.5 us (0.969)
  the two profiles are of different devices: /device:TPU:1 before, /device:TPU:4 now
where the time goes in v5:
time: 66.5 us; the launch traced here: 66.1 us
  starting transfers between devices  38.2 us (57%)
  waiting for transfers between devices  16.3 us (25%)
  Pallas kernels  10.1 us (15%)
  between operations  0.81 us (1%)
  local copies, waits for them, and re-layouts  0.69 us (1%)
    all_to_all x2, starting transfers between devices, gathered(): return lax.all_to_all(array, axes, 0, 0)  20.1 us
    ppermute x5, starting transfers between devices, ring(): lax.ppermute(array, axes, [(i, (i + step) % size) for i in range(size)])  18.1 us
    ppermute x5, waiting for transfers between devices, ring(): lax.ppermute(array, axes, [(i, (i + step) % size) for i in range(size)])  11.6 us
    all_to_all x2, waiting for transfers between devices, gathered(): return lax.all_to_all(array, axes, 0, 0)  4.68 us
    pallas_call x1, Pallas kernels, per_device(): call(inner_kernel, [inner, inner, (2, 24, X), (2, 24, X), edge, (9, 8, 2...  3.08 us
    pallas_call x1, Pallas kernels, per_device(): call(prep_kernel, [(NC, Z, X), small], [whole, (2, Z, X), (2, Z, X), pltp...  2.02 us
    pallas_call x1, Pallas kernels, per_device(): call(edge_kernel, [edge, edge, (2, 8, X), (2, 8, X), (near, 8, X)], [(NF,...  1.93 us
  transfers between devices with their start and end apart: 7, of which 5 were waited for; matrix products, arithmetic and copies ran while one was open for 0% of the time, Pallas kernels for 7%

profile of v5, /device:TPU:4, one launch (start us, length us, event | category | flops | bytes accessed | tf_op | source)
XLA Modules:
  0.0 66.1 jit_solution(18050824828210284056)
XLA Ops:
  0.6 0.0 copy-start
  0.6 2.0 %shard_map.77 = (f32[6,32,128]{2,1,0:T(8,128)}, f32[3,32,128]{2,1,0:T(8,128)}) custom-call(f32[32,32,128]{2,1,0:T(8,128)} %bitcast.3, f32[2,32,128]{2,1,0:T(8,128)} %mass_hbm.1, f32[2,32,128]{2,1,0:T(8,128)} %internal_hbm.1, f32[2,32,128]{2,1,0:T(8,128)} %velocity_hbm.1), custom_call_target="tpu_custom_call" | custom-call | flops 2000000 | bytes 2000000 | tf_op jit(solution)/shard_map/pallas_call | solution.py:658
  2.7 0.0 copy-done
  2.7 0.0 copy-start.4
  2.7 0.0 copy-start.1
  2.7 2.1 %collective-permute-start.1 = (f32[32,8,128]{2,1,0:T(8,128)S(1)}, f32[32,8,128]{2,1,0:T(8,128)S(1)}, u32[]{:S(2)}, u32[]{:S(2)}) collective-permute-start(f32[32,8,128]{2,1,0:T(8,128)S(1)} %shard_map.80), channel_id=1, source_target_pairs={{0,31},{1,0},{2,1},{3,2},{4,3},{5,4},{6,5},{7,6},{8,7},{9,8},{10,9... | collective-permute-start | bytes 393224 | tf_op jit(solution)/shard_map/ppermute | solution.py:644
  4.8 0.0 copy-done.4
  4.8 6.8 %collective-permute-start = (f32[3,32,128]{2,1,0:T(8,128)S(1)}, f32[3,32,128]{2,1,0:T(8,128)S(1)}, u32[]{:S(2)}, u32[]{:S(2)}) collective-permute-start(f32[3,32,128]{2,1,0:T(8,128)S(1)} %copy-done.4), channel_id=1, source_target_pairs={{0,480},{32,0},{64,32},{96,64},{128,96},{160,128},{192,160},{224,1... | collective-permute-start | bytes 147464 | tf_op jit(solution)/shard_map/ppermute | solution.py:644
  11.7 0.0 copy-done.1
  11.7 0.0 copy-start.3
  11.7 0.5 shard_map.78
  12.2 0.0 copy-start.2
  12.2 1.2 %collective-permute-done.side_ref = f32[3,32,128]{2,1,0:T(8,128)S(1)} collective-permute-done((f32[3,32,128]{2,1,0:T(8,128)S(1)}, f32[3,32,128]{2,1,0:T(8,128)S(1)}, u32[]{:S(2)}, u32[]{:S(2)}) %collective-permute-start) | collective-permute-done | bytes 49184 | tf_op jit(solution)/shard_map/ppermute | solution.py:644
  13.4 0.3 shard_map.81
  13.7 4.1 %collective-permute-start.2 = (f32[18,8,128]{2,1,0:T(8,128)S(1)}, f32[18,8,128]{2,1,0:T(8,128)S(1)}, u32[]{:S(2)}, u32[]{:S(2)}) collective-permute-start(f32[18,8,128]{2,1,0:T(8,128)S(1)} %shard_map.81), channel_id=1, source_target_pairs={{0,31},{1,0},{2,1},{3,2},{4,3},{5,4},{6,5},{7,6},{8,7},{9,8},{10,9... | collective-permute-start | bytes 221192 | tf_op jit(solution)/shard_map/ppermute | solution.py:644
  17.9 0.0 copy-done.3
  17.9 0.0 copy-done.2
  17.9 3.1 %shard_map.79 = (f32[32,24,128]{2,1,0:T(8,128)S(1)}, f32[32,24,128]{2,1,0:T(8,128)S(1)}, f32[2,24,128]{2,1,0:T(8,128)S(1)}, f32[2,24,128]{2,1,0:T(8,128)S(1)}, f...) custom-call(f32[32,32,128]{2,1,0:T(8,128)S(1)} %bitcast.6, f32[6,32,128]{2,1,0:T(8,128)S(1)} %copy-done.1, ...), custom_call_target="tpu_custom_call" | custom-call | flops 2000000 | bytes 2000000 | tf_op jit(solution)/shard_map/pallas_call | solution.py:673
  21.0 0.0 collective-permute-done.2.corner_ref
  21.0 0.0 collective-permute-done.1.below_ref
  21.0 1.9 %shard_map.82 = (f32[32,8,128]{2,1,0:T(8,128)S(1)}, f32[32,8,128]{2,1,0:T(8,128)S(1)}, f32[2,8,128]{2,1,0:T(8,128)S(1)}, f32[2,8,128]{2,1,0:T(8,128)S(1)}, f32[16,8,128]{2,1,0:T(8,128)}) custom-call(f32[32,32,128]{2,1,0:T(8,128)S(1)} %bitcast.7, f32[6,32,128]{2,1,0:T(8,128)S(1)} %copy-done.1, f32[16,32,128]{2,1,0:T(8,128)S(1)} %get-tuple-element.36.warm_ref, ...), custom_call_target="tpu_custom_call" | custom-call | flops 2000000 | bytes 2000000 | tf_op jit(solution)/shard_map/pallas_call | solution.py:678
  22.9 11.5 %all-to-all-start = ((f32[16,8,128]{2,1,0:T(8,128)}), f32[16,8,128]{2,1,0:T(8,128)S(1)}, u32[]{:S(2)}, u32[]{:S(2)}) async-start(f32[16,8,128]{2,1,0:T(8,128)} %get-tuple-element.52), calls=%async_computation | async-start | bytes 131072 | tf_op jit(solution)/shard_map/all_to_all | solution.py:648
  34.4 3.1 %collective-permute-start.3 = (f32[2,2,32,128]{3,2,1,0:T(8,128)S(1)}, f32[2,2,32,128]{3,2,1,0:T(8,128)S(1)}, u32[]{:S(2)}, u32[]{:S(2)}) collective-permute-start(f32[2,2,32,128]{3,2,1,0:T(8,128)S(1)} %shard_map.83.mine_ref), channel_id=1, source_target_pairs={{0,32},{32,64},{64,96},{96,128},{128,160},{160,192},{192,224},{224... | collective-permute-start | bytes 196616 | tf_op jit(solution)/shard_map/ppermute | solution.py:644
  37.5 0.8 %all-to-all-done = f32[16,8,128]{2,1,0:T(8,128)S(1)} async-done(((f32[16,8,128]{2,1,0:T(8,128)}), f32[16,8,128]{2,1,0:T(8,128)S(1)}, u32[]{:S(2)}, u32[]{:S(2)}) %all-to-all-start) | async-done | bytes 65568 | tf_op jit(solution)/shard_map/all_to_all | solution.py:648
  38.4 4.6 %collective-permute-done.3.got_ref = f32[2,2,32,128]{3,2,1,0:T(8,128)S(1)} collective-permute-done((f32[2,2,32,128]{3,2,1,0:T(8,128)S(1)}, f32[2,2,32,128]{3,2,1,0:T(8,128)S(1)}, u32[]{:S(2)}, u32[]{:S(2)}) %collective-permute-start.3) | collective-permute-done | bytes 65568 | tf_op jit(solution)/shard_map/ppermute | solution.py:644
  42.9 0.7 %broadcast_in_dim.3 = f32[32,8,128]{2,1,0:T(8,128)} broadcast(f32[8,128]{1,0:T(8,128)S(1)} %reduce_sum.9), dimensions={1,2} | broadcast | bytes 135168 | tf_op jit(solution)/shard_map/broadcast_in_dim | solution.py:688
  43.6 8.7 %all-to-all-start.1 = ((f32[32,8,128]{2,1,0:T(8,128)}), f32[32,8,128]{2,1,0:T(8,128)S(1)}, u32[]{:S(2)}, u32[]{:S(2)}) async-start(f32[32,8,128]{2,1,0:T(8,128)} %broadcast_in_dim.3), calls=%async_computation.1 | async-start | bytes 262144 | tf_op jit(solution)/shard_map/all_to_all | solution.py:648
  52.3 0.9 %shard_map.84 = (f32[32,32,128]{2,1,0:T(8,128)S(1)}, f32[32,32,128]{2,1,0:T(8,128)S(1)}, f32[256,128]{1,0:T(8,128)S(1)}) custom-call(f32[32,24,128]{2,1,0:T(8,128)S(1)} %get-tuple-element.40.ad_ref, f32[32,24,128]{2,1,0:T(8,128)S(1)} %get-tuple-element.41.bd_ref, f32[32,8,128]{2,1,0:T(8,128)S(1)} %get-tuple-element.46.ade_ref, ...), custom_call_target="tpu_custom_call" | custom-call | flops 2000000 | bytes 2000000 | tf_op jit(solution)/shard_map/pallas_call | solution.py:689
  53.2 1.9 %collective-permute-start.4 = (f32[256,128]{1,0:T(8,128)S(1)}, f32[256,128]{1,0:T(8,128)S(1)}, u32[]{:S(2)}, u32[]{:S(2)}) collective-permute-start(f32[256,128]{1,0:T(8,128)S(1)} %get-tuple-element.56), channel_id=1, source_target_pairs={{0,1},{1,2},{2,3},{3,4},{4,5},{5,6},{6,7},{7,8},{8,9},{9,10},{10,1... | collective-permute-start | bytes 393224 | tf_op jit(solution)/shard_map/ppermute | solution.py:644
  55.1 5.9 %collective-permute-done.4.above_ref = f32[256,128]{1,0:T(8,128)S(1)} collective-permute-done((f32[256,128]{1,0:T(8,128)S(1)}, f32[256,128]{1,0:T(8,128)S(1)}, u32[]{:S(2)}, u32[]{:S(2)}) %collective-permute-start.4) | collective-permute-done | bytes 131104 | tf_op jit(solution)/shard_map/ppermute | solution.py:644
  61.0 3.9 %all-to-all-done.1.sums_ref = f32[32,8,128]{2,1,0:T(8,128)S(1)} async-done(((f32[32,8,128]{2,1,0:T(8,128)}), f32[32,8,128]{2,1,0:T(8,128)S(1)}, u32[]{:S(2)}, u32[]{:S(2)}) %all-to-all-start.1) | async-done | bytes 131104 | tf_op jit(solution)/shard_map/all_to_all | solution.py:648
  64.9 1.3 %shard_map.85 = (f32[32,32,128]{2,1,0:T(8,128)}, f32[8,128]{1,0:T(8,128)}) custom-call(f32[32,32,128]{2,1,0:T(8,128)S(1)} %bitcast.8, f32[32,32,128]{2,1,0:T(8,128)S(1)} %get-tuple-element.54.a_ref, f32[32,32,128]{2,1,0:T(8,128)S(1)} %get-tuple-element.55.b_ref, f32[256,128]{1,0:T(8,128)S(1)} %collective-permute-done.4.above_ref, ...), custom_call_target="tpu_custom_call" | custom-call | flops 2000000 | bytes 2000000 | tf_op jit(solution)/shard_map/pallas_call | solution.py:691
  (3 shorter events, 0.0 us)
Async XLA Ops:
  0.6 2.0 %copy-start = (f32[8,2,2,32,128]{4,3,2,1,0:T(8,128)S(1)}, f32[8,2,2,32,128]{4,3,2,1,0:T(8,128)}, u32[]{:S(2)}) copy-start(f32[8,2,2,32,128]{4,3,2,1,0:T(8,128)} %param.6) | copy-start | bytes 1572868
  2.7 2.1 %copy-start.4 = (f32[3,32,128]{2,1,0:T(8,128)S(1)}, f32[3,32,128]{2,1,0:T(8,128)}, u32[]{:S(2)}) copy-start(f32[3,32,128]{2,1,0:T(8,128)} %get-tuple-element.32) | copy-start | bytes 147460
  2.7 9.0 %copy-start.1 = (f32[6,32,128]{2,1,0:T(8,128)S(1)}, f32[6,32,128]{2,1,0:T(8,128)}, u32[]{:S(2)}) copy-start(f32[6,32,128]{2,1,0:T(8,128)} %get-tuple-element.31.coef_ref) | copy-start | bytes 294916
  2.7 18.3 %collective-permute-start.1 = (f32[32,8,128]{2,1,0:T(8,128)S(1)}, f32[32,8,128]{2,1,0:T(8,128)S(1)}, u32[]{:S(2)}, u32[]{:S(2)}) collective-permute-start(f32[32,8,128]{2,1,0:T(8,128)S(1)} %shard_map.80), channel_id=1, source_target_pairs={{0,31},{1,0},{2,1},{3,2},{4,3},{5,4},{6,5},{7,6},{8,7},{9,8},{10,9... | collective-permute-start | bytes 393224 | tf_op jit(solution)/shard_map/ppermute | solution.py:644
  4.8 8.6 %collective-permute-start = (f32[3,32,128]{2,1,0:T(8,128)S(1)}, f32[3,32,128]{2,1,0:T(8,128)S(1)}, u32[]{:S(2)}, u32[]{:S(2)}) collective-permute-start(f32[3,32,128]{2,1,0:T(8,128)S(1)} %copy-done.4), channel_id=1, source_target_pairs={{0,480},{32,0},{64,32},{96,64},{128,96},{160,128},{192,160},{224,1... | collective-permute-start | bytes 147464 | tf_op jit(solution)/shard_map/ppermute | solution.py:644
  11.7 6.2 %copy-start.3 = (bf16[256,256]{1,0:T(8,128)(2,1)S(1)}, bf16[256,256]{1,0:T(8,128)(2,1)}, u32[]{:S(2)}) copy-start(bf16[256,256]{1,0:T(8,128)(2,1)} %constant.6.clone.wm_ref) | copy-start | bytes 393220
  12.2 5.7 %copy-start.2 = (bf16[2,256,256]{2,1,0:T(8,128)(2,1)S(1)}, bf16[2,256,256]{2,1,0:T(8,128)(2,1)}, u32[]{:S(2)}) copy-start(bf16[2,256,256]{2,1,0:T(8,128)(2,1)} %constant.7.clone.wp_ref) | copy-start | bytes 786436
  13.7 7.2 %collective-permute-start.2 = (f32[18,8,128]{2,1,0:T(8,128)S(1)}, f32[18,8,128]{2,1,0:T(8,128)S(1)}, u32[]{:S(2)}, u32[]{:S(2)}) collective-permute-start(f32[18,8,128]{2,1,0:T(8,128)S(1)} %shard_map.81), channel_id=1, source_target_pairs={{0,31},{1,0},{2,1},{3,2},{4,3},{5,4},{6,5},{7,6},{8,7},{9,8},{10,9... | collective-permute-start | bytes 221192 | tf_op jit(solution)/shard_map/ppermute | solution.py:644
  22.9 15.4 %all-to-all-start = ((f32[16,8,128]{2,1,0:T(8,128)}), f32[16,8,128]{2,1,0:T(8,128)S(1)}, u32[]{:S(2)}, u32[]{:S(2)}) async-start(f32[16,8,128]{2,1,0:T(8,128)} %get-tuple-element.52), calls=%async_computation | async-start | bytes 131072 | tf_op jit(solution)/shard_map/all_to_all | solution.py:648
  34.4 8.5 %collective-permute-start.3 = (f32[2,2,32,128]{3,2,1,0:T(8,128)S(1)}, f32[2,2,32,128]{3,2,1,0:T(8,128)S(1)}, u32[]{:S(2)}, u32[]{:S(2)}) collective-permute-start(f32[2,2,32,128]{3,2,1,0:T(8,128)S(1)} %shard_map.83.mine_ref), channel_id=1, source_target_pairs={{0,32},{32,64},{64,96},{96,128},{128,160},{160,192},{192,224},{224... | collective-permute-start | bytes 196616 | tf_op jit(solution)/shard_map/ppermute | solution.py:644
  43.6 21.3 %all-to-all-start.1 = ((f32[32,8,128]{2,1,0:T(8,128)}), f32[32,8,128]{2,1,0:T(8,128)S(1)}, u32[]{:S(2)}, u32[]{:S(2)}) async-start(f32[32,8,128]{2,1,0:T(8,128)} %broadcast_in_dim.3), calls=%async_computation.1 | async-start | bytes 262144 | tf_op jit(solution)/shard_map/all_to_all | solution.py:648
  53.2 7.8 %collective-permute-start.4 = (f32[256,128]{1,0:T(8,128)S(1)}, f32[256,128]{1,0:T(8,128)S(1)}, u32[]{:S(2)}, u32[]{:S(2)}) collective-permute-start(f32[256,128]{1,0:T(8,128)S(1)} %get-tuple-element.56), channel_id=1, source_target_pairs={{0,1},{1,2},{2,3},{3,4},{4,5},{5,6},{6,7},{7,8},{8,9},{9,10},{10,1... | collective-permute-start | bytes 393224 | tf_op jit(solution)/shard_map/ppermute | solution.py:644

commit v6 on v5

--- a/solution.py
+++ b/solution.py
@@ -134,11 +134,6 @@
         pack_ref[2, tile(t), :] = acc
 
 
-def rows_kernel(q_ref, rows_ref):
-    for f in range(NF):
-        rows_ref[f] = q_ref[f, 0:8, :]
-
-
 def pairs():
     return [(k, m, (k + m) % K) for k in range(K) for m in range(5 if k < 4 else 4)]
 
@@ -238,12 +233,14 @@
         packed[n, rows, X : 2 * X] = part
 
 
-def corner_kernel(side_ref, last_ref, coef_ref, corner_ref, packed):
+def wire_kernel(q_ref, side_ref, last_ref, coef_ref, rows_ref, packed):
     join(side_ref, last_ref, packed, 0, 0, lanes())
+    for f in range(NF):
+        rows_ref[f] = q_ref[f, 0:8, :]
     for n in range(6):
-        corner_ref[n] = packed[n, :, 0:X]
-        corner_ref[6 + n] = packed[n, :, X : 2 * X]
-        corner_ref[12 + n] = coef_ref[n, 0:8, :]
+        rows_ref[NF + n] = packed[n, :, 0:X]
+        rows_ref[NF + 6 + n] = packed[n, :, X : 2 * X]
+        rows_ref[NF + 12 + n] = coef_ref[n, 0:8, :]
 
 
 def split(x):
@@ -447,7 +444,7 @@
 
 
 def edge_kernel(
-    q_ref, coef_ref, warm_ref, below_ref, corner_ref, tail_ref, packed_ref, inner_ref, wm_ref, wp_ref,
+    q_ref, coef_ref, warm_ref, below_ref, tail_ref, packed_ref, inner_ref, wm_ref, wp_ref,
     ad_ref, bd_ref, ap_ref, bp_ref, sums_ref,
     em, ec, wm, packed, pa, qp, am, tm, red, extra,
 ):
@@ -455,10 +452,10 @@
     red[...] = jnp.zeros_like(red)
     for n in range(NC):
         ec[n, 0:8, :] = coef_ref[n, 24:32, :]
-        ec[n, 8:16, :] = corner_ref[12 + n]
+        ec[n, 8:16, :] = below_ref[NF + 12 + n]
         packed[n, 0:8, :] = packed_ref[3 + n]
-        packed[n, 8:16, 0:X] = corner_ref[n]
-        packed[n, 8:16, X : 2 * X] = corner_ref[6 + n]
+        packed[n, 8:16, 0:X] = below_ref[NF + n]
+        packed[n, 8:16, X : 2 * X] = below_ref[NF + 6 + n]
     for n in range(3):
         pa[n, 0:8, :] = packed_ref[n]
     packed_steps(packed, wp_ref, pa, (qp, ap_ref, bp_ref), (6, 8, 8), (4, 6), 8, lane)
@@ -663,13 +660,10 @@
         in_specs=[pl.BlockSpec(memory_space=pl.ANY)] * 4,
     )(q, mass, internal, velocity)
     side = ring(pack, GX, -1)
-    later, _ = lax.optimization_barrier((q, pack))
-    (rows,) = call(rows_kernel, [edge], cost=1000)(later)
-    below = ring(rows, GZ, -1)
     warm, last, own = call(own_kernel, [half, (6, Z, X), (8, X)], [(5, 8, X)])(q, coef)
     side, warm, last, own = lax.optimization_barrier((side, warm, last, own))
-    (corner,) = call(corner_kernel, [(18, 8, X)], [(6, 8, 2 * X)], cost=1000)(side, last, coef)
-    corner = ring(corner, GZ, -1)
+    (rows,) = call(wire_kernel, [(NF + 18, 8, X)], [(6, 8, 2 * X)], cost=1000)(q, side, last, coef)
+    below = ring(rows, GZ, -1)
     ad, bd, ap, bp, tail, packed, part = call(
         inner_kernel,
         [inner, inner, (2, 24, X), (2, 24, X), edge, (9, 8, 2 * X), (8, X)],
@@ -680,7 +674,7 @@
         [edge, edge, (2, 8, X), (2, 8, X), (near, 8, X)],
         [(NF, 16, X), (NC, 16, X), (K, 2, 16, X), (6, 16, 2 * X), (3, 16, 2 * X), (2, 8, X)]
         + [(K, 4, 16, X), (K, 2, 16, X), red, red],
-    )(q, coef, warm, below, corner, tail, packed, part, wm, wp)
+    )(q, coef, warm, below, tail, packed, part, wm, wp)
     sums = jnp.sum(gathered(sums, NEAR), axis=0)
     (give,) = call(give_kernel, [(2, 2, Z, X)])(ap, bp, ape, bpe)
     got = ring(give, GX, 1)

time: 66.5 us -> 64.9 us (0.976)
  starting transfers between devices: 38.2 us -> 36.4 us
  local copies, waits for them, and re-layouts: 0.69 us -> 1.56 us
    ppermute x5 -> x4, starting transfers between devices: 18.1 us -> 12.9 us  [ring(): lax.ppermute(array, axes, [(i, (i + step) % size) for i in range(size)])]
    all_to_all x2, starting transfers between devices: 20.1 us -> 23.5 us  [gathered(): return lax.all_to_all(array, axes, 0, 0)]
    unnamed x10 -> x8, local copies, waits for them, and re-layouts: 0.03 us -> 0.9 us
    ppermute x5 -> x4, waiting for transfers between devices: 11.6 us -> 11 us  [ring(): lax.ppermute(array, axes, [(i, (i + step) % size) for i in range(size)])]
  transfers between devices with their start and end apart: 7 -> 6, of which waited for: 5 -> 6; matrix products, arithmetic and copies ran while one was open for 0% -> 0% of each run, Pallas kernels for 7% -> 7%
where the time goes in v6:
time: 64.9 us; the launch traced here: 64.5 us
  starting transfers between devices  36.4 us (56%)
  waiting for transfers between devices  15.7 us (24%)
  Pallas kernels  10.1 us (16%)
  local copies, waits for them, and re-layouts  1.56 us (2%)
  between operations  0.74 us (1%)
    all_to_all x2, starting transfers between devices, gathered(): return lax.all_to_all(array, axes, 0, 0)  23.5 us
    ppermute x4, starting transfers between devices, ring(): lax.ppermute(array, axes, [(i, (i + step) % size) for i in range(size)])  12.9 us
    ppermute x4, waiting for transfers between devices, ring(): lax.ppermute(array, axes, [(i, (i + step) % size) for i in range(size)])  11 us
    all_to_all x2, waiting for transfers between devices, gathered(): return lax.all_to_all(array, axes, 0, 0)  4.68 us
    pallas_call x1, Pallas kernels, per_device(): call(inner_kernel, [inner, inner, (2, 24, X), (2, 24, X), edge, (9, 8, 2...  3.06 us
    pallas_call x1, Pallas kernels, per_device(): call(prep_kernel, [(NC, Z, X), small], [whole, (2, Z, X), (2, Z, X), pltp...  2.02 us
    pallas_call x1, Pallas kernels, per_device(): call(edge_kernel, [edge, edge, (2, 8, X), (2, 8, X), (near, 8, X)], [(NF,...  1.92 us
  transfers between devices with their start and end apart: 6, of which 6 were waited for; matrix products, arithmetic and copies ran while one was open for 0% of the time, Pallas kernels for 7%

profile of v6, /device:TPU:4, one launch (start us, length us, event | category | flops | bytes accessed | tf_op | source)
XLA Modules:
  0.0 64.5 jit_solution(8696694138474070838)
XLA Ops:
  0.6 0.0 copy-start
  0.6 2.0 %shard_map.77 = (f32[6,32,128]{2,1,0:T(8,128)}, f32[3,32,128]{2,1,0:T(8,128)}) custom-call(f32[32,32,128]{2,1,0:T(8,128)} %bitcast.3, f32[2,32,128]{2,1,0:T(8,128)} %mass_hbm.1, f32[2,32,128]{2,1,0:T(8,128)} %internal_hbm.1, f32[2,32,128]{2,1,0:T(8,128)} %velocity_hbm.1), custom_call_target="tpu_custom_call" | custom-call | flops 2000000 | bytes 2000000 | tf_op jit(solution)/shard_map/pallas_call | solution.py:655
  2.7 6.0 %collective-permute-start = (f32[3,32,128]{2,1,0:T(8,128)}, f32[3,32,128]{2,1,0:T(8,128)S(1)}, u32[]{:S(2)}, u32[]{:S(2)}) collective-permute-start(f32[3,32,128]{2,1,0:T(8,128)} %get-tuple-element.31), channel_id=1, source_target_pairs={{0,480},{32,0},{64,32},{96,64},{128,96},{160,128},{192,160},{224,1... | collective-permute-start | bytes 147464 | tf_op jit(solution)/shard_map/ppermute | solution.py:641
  8.7 0.0 copy-done
  8.7 0.0 copy-start.1
  8.7 0.9 %copy-done.1 = f32[6,32,128]{2,1,0:T(8,128)S(1)} copy-done((f32[6,32,128]{2,1,0:T(8,128)S(1)}, f32[6,32,128]{2,1,0:T(8,128)}, u32[]{:S(2)}) %copy-start.1) | copy-done | bytes 98328
  9.6 0.5 shard_map.78
  10.1 0.6 collective-permute-done.side_ref
  10.7 0.0 copy-start.2
  10.7 0.0 copy-start.3
  10.7 0.3 shard_map.80
  11.1 1.9 %collective-permute-start.1 = (f32[50,8,128]{2,1,0:T(8,128)S(1)}, f32[50,8,128]{2,1,0:T(8,128)S(1)}, u32[]{:S(2)}, u32[]{:S(2)}) collective-permute-start(f32[50,8,128]{2,1,0:T(8,128)S(1)} %shard_map.80), channel_id=1, source_target_pairs={{0,31},{1,0},{2,1},{3,2},{4,3},{5,4},{6,5},{7,6},{8,7},{9,8},{10,9... | collective-permute-start | bytes 614408 | tf_op jit(solution)/shard_map/ppermute | solution.py:641
  13.0 0.0 copy-done.2
  13.0 0.0 copy-done.3
  13.0 3.1 %shard_map.79 = (f32[32,24,128]{2,1,0:T(8,128)S(1)}, f32[32,24,128]{2,1,0:T(8,128)S(1)}, f32[2,24,128]{2,1,0:T(8,128)S(1)}, f32[2,24,128]{2,1,0:T(8,128)S(1)}, f...) custom-call(f32[32,32,128]{2,1,0:T(8,128)S(1)} %bitcast.6, f32[6,32,128]{2,1,0:T(8,128)S(1)} %copy-done.1, ...), custom_call_target="tpu_custom_call" | custom-call | flops 2000000 | bytes 2000000 | tf_op jit(solution)/shard_map/pallas_call | solution.py:667
  16.1 0.2 collective-permute-done.1.below_ref
  16.3 1.9 %shard_map.81 = (f32[32,8,128]{2,1,0:T(8,128)S(1)}, f32[32,8,128]{2,1,0:T(8,128)S(1)}, f32[2,8,128]{2,1,0:T(8,128)S(1)}, f32[2,8,128]{2,1,0:T(8,128)S(1)}, f32[16,8,128]{2,1,0:T(8,128)}) custom-call(f32[32,32,128]{2,1,0:T(8,128)S(1)} %bitcast.7, f32[6,32,128]{2,1,0:T(8,128)S(1)} %copy-done.1, f32[16,32,128]{2,1,0:T(8,128)S(1)} %get-tuple-element.35.warm_ref, ...), custom_call_target="tpu_custom_call" | custom-call | flops 2000000 | bytes 2000000 | tf_op jit(solution)/shard_map/pallas_call | solution.py:672
  18.2 13.9 %all-to-all-start = ((f32[16,8,128]{2,1,0:T(8,128)}), f32[16,8,128]{2,1,0:T(8,128)S(1)}, u32[]{:S(2)}, u32[]{:S(2)}) async-start(f32[16,8,128]{2,1,0:T(8,128)} %get-tuple-element.50), calls=%async_computation | async-start | bytes 131072 | tf_op jit(solution)/shard_map/all_to_all | solution.py:645
  32.1 3.1 %collective-permute-start.2 = (f32[2,2,32,128]{3,2,1,0:T(8,128)S(1)}, f32[2,2,32,128]{3,2,1,0:T(8,128)S(1)}, u32[]{:S(2)}, u32[]{:S(2)}) collective-permute-start(f32[2,2,32,128]{3,2,1,0:T(8,128)S(1)} %shard_map.82.mine_ref), channel_id=1, source_target_pairs={{0,32},{32,64},{64,96},{96,128},{128,160},{160,192},{192,224},{224... | collective-permute-start | bytes 196616 | tf_op jit(solution)/shard_map/ppermute | solution.py:641
  35.2 0.8 %all-to-all-done = f32[16,8,128]{2,1,0:T(8,128)S(1)} async-done(((f32[16,8,128]{2,1,0:T(8,128)}), f32[16,8,128]{2,1,0:T(8,128)S(1)}, u32[]{:S(2)}, u32[]{:S(2)}) %all-to-all-start) | async-done | bytes 65568 | tf_op jit(solution)/shard_map/all_to_all | solution.py:645
  36.0 4.3 %collective-permute-done.2.got_ref = f32[2,2,32,128]{3,2,1,0:T(8,128)S(1)} collective-permute-done((f32[2,2,32,128]{3,2,1,0:T(8,128)S(1)}, f32[2,2,32,128]{3,2,1,0:T(8,128)S(1)}, u32[]{:S(2)}, u32[]{:S(2)}) %collective-permute-start.2) | collective-permute-done | bytes 65568 | tf_op jit(solution)/shard_map/ppermute | solution.py:641
  40.3 0.7 %broadcast_in_dim.3 = f32[32,8,128]{2,1,0:T(8,128)} broadcast(f32[8,128]{1,0:T(8,128)S(1)} %reduce_sum.9), dimensions={1,2} | broadcast | bytes 135168 | tf_op jit(solution)/shard_map/broadcast_in_dim | solution.py:682
  41.0 9.6 %all-to-all-start.1 = ((f32[32,8,128]{2,1,0:T(8,128)}), f32[32,8,128]{2,1,0:T(8,128)S(1)}, u32[]{:S(2)}, u32[]{:S(2)}) async-start(f32[32,8,128]{2,1,0:T(8,128)} %broadcast_in_dim.3), calls=%async_computation.1 | async-start | bytes 262144 | tf_op jit(solution)/shard_map/all_to_all | solution.py:645
  50.6 0.9 %shard_map.83 = (f32[32,32,128]{2,1,0:T(8,128)S(1)}, f32[32,32,128]{2,1,0:T(8,128)S(1)}, f32[256,128]{1,0:T(8,128)S(1)}) custom-call(f32[32,24,128]{2,1,0:T(8,128)S(1)} %get-tuple-element.39.ad_ref, f32[32,24,128]{2,1,0:T(8,128)S(1)} %get-tuple-element.40.bd_ref, f32[32,8,128]{2,1,0:T(8,128)S(1)} %get-tuple-element.44.ade_ref, ...), custom_call_target="tpu_custom_call" | custom-call | flops 2000000 | bytes 2000000 | tf_op jit(solution)/shard_map/pallas_call | solution.py:683
  51.5 1.9 %collective-permute-start.3 = (f32[256,128]{1,0:T(8,128)S(1)}, f32[256,128]{1,0:T(8,128)S(1)}, u32[]{:S(2)}, u32[]{:S(2)}) collective-permute-start(f32[256,128]{1,0:T(8,128)S(1)} %get-tuple-element.54), channel_id=1, source_target_pairs={{0,1},{1,2},{2,3},{3,4},{4,5},{5,6},{6,7},{7,8},{8,9},{9,10},{10,1... | collective-permute-start | bytes 393224 | tf_op jit(solution)/shard_map/ppermute | solution.py:641
  53.5 5.9 %collective-permute-done.3.above_ref = f32[256,128]{1,0:T(8,128)S(1)} collective-permute-done((f32[256,128]{1,0:T(8,128)S(1)}, f32[256,128]{1,0:T(8,128)S(1)}, u32[]{:S(2)}, u32[]{:S(2)}) %collective-permute-start.3) | collective-permute-done | bytes 131104 | tf_op jit(solution)/shard_map/ppermute | solution.py:641
  59.3 3.9 %all-to-all-done.1.sums_ref = f32[32,8,128]{2,1,0:T(8,128)S(1)} async-done(((f32[32,8,128]{2,1,0:T(8,128)}), f32[32,8,128]{2,1,0:T(8,128)S(1)}, u32[]{:S(2)}, u32[]{:S(2)}) %all-to-all-start.1) | async-done | bytes 131104 | tf_op jit(solution)/shard_map/all_to_all | solution.py:645
  63.2 1.3 %shard_map.84 = (f32[32,32,128]{2,1,0:T(8,128)}, f32[8,128]{1,0:T(8,128)}) custom-call(f32[32,32,128]{2,1,0:T(8,128)S(1)} %bitcast.8, f32[32,32,128]{2,1,0:T(8,128)S(1)} %get-tuple-element.52.a_ref, f32[32,32,128]{2,1,0:T(8,128)S(1)} %get-tuple-element.53.b_ref, f32[256,128]{1,0:T(8,128)S(1)} %collective-permute-done.3.above_ref, ...), custom_call_target="tpu_custom_call" | custom-call | flops 2000000 | bytes 2000000 | tf_op jit(solution)/shard_map/pallas_call | solution.py:685
  (2 shorter events, 0.0 us)
Async XLA Ops:
  0.6 8.1 %copy-start = (f32[8,2,2,32,128]{4,3,2,1,0:T(8,128)S(1)}, f32[8,2,2,32,128]{4,3,2,1,0:T(8,128)}, u32[]{:S(2)}) copy-start(f32[8,2,2,32,128]{4,3,2,1,0:T(8,128)} %param.6) | copy-start | bytes 1572868
  2.7 8.1 %collective-permute-start = (f32[3,32,128]{2,1,0:T(8,128)}, f32[3,32,128]{2,1,0:T(8,128)S(1)}, u32[]{:S(2)}, u32[]{:S(2)}) collective-permute-start(f32[3,32,128]{2,1,0:T(8,128)} %get-tuple-element.31), channel_id=1, source_target_pairs={{0,480},{32,0},{64,32},{96,64},{128,96},{160,128},{192,160},{224,1... | collective-permute-start | bytes 147464 | tf_op jit(solution)/shard_map/ppermute | solution.py:641
  8.7 0.9 %copy-start.1 = (f32[6,32,128]{2,1,0:T(8,128)S(1)}, f32[6,32,128]{2,1,0:T(8,128)}, u32[]{:S(2)}) copy-start(f32[6,32,128]{2,1,0:T(8,128)} %get-tuple-element.30.coef_ref) | copy-start | bytes 294916
  10.7 2.3 %copy-start.2 = (bf16[2,256,256]{2,1,0:T(8,128)(2,1)S(1)}, bf16[2,256,256]{2,1,0:T(8,128)(2,1)}, u32[]{:S(2)}) copy-start(bf16[2,256,256]{2,1,0:T(8,128)(2,1)} %constant.7.clone.wp_ref) | copy-start | bytes 786436
  10.7 2.3 %copy-start.3 = (bf16[256,256]{1,0:T(8,128)(2,1)S(1)}, bf16[256,256]{1,0:T(8,128)(2,1)}, u32[]{:S(2)}) copy-start(bf16[256,256]{1,0:T(8,128)(2,1)} %constant.6.clone.wm_ref) | copy-start | bytes 393220
  11.1 5.2 %collective-permute-start.1 = (f32[50,8,128]{2,1,0:T(8,128)S(1)}, f32[50,8,128]{2,1,0:T(8,128)S(1)}, u32[]{:S(2)}, u32[]{:S(2)}) collective-permute-start(f32[50,8,128]{2,1,0:T(8,128)S(1)} %shard_map.80), channel_id=1, source_target_pairs={{0,31},{1,0},{2,1},{3,2},{4,3},{5,4},{6,5},{7,6},{8,7},{9,8},{10,9... | collective-permute-start | bytes 614408 | tf_op jit(solution)/shard_map/ppermute | solution.py:641
  18.2 17.8 %all-to-all-start = ((f32[16,8,128]{2,1,0:T(8,128)}), f32[16,8,128]{2,1,0:T(8,128)S(1)}, u32[]{:S(2)}, u32[]{:S(2)}) async-start(f32[16,8,128]{2,1,0:T(8,128)} %get-tuple-element.50), calls=%async_computation | async-start | bytes 131072 | tf_op jit(solution)/shard_map/all_to_all | solution.py:645
  32.1 8.3 %collective-permute-start.2 = (f32[2,2,32,128]{3,2,1,0:T(8,128)S(1)}, f32[2,2,32,128]{3,2,1,0:T(8,128)S(1)}, u32[]{:S(2)}, u32[]{:S(2)}) collective-permute-start(f32[2,2,32,128]{3,2,1,0:T(8,128)S(1)} %shard_map.82.mine_ref), channel_id=1, source_target_pairs={{0,32},{32,64},{64,96},{96,128},{128,160},{160,192},{192,224},{224... | collective-permute-start | bytes 196616 | tf_op jit(solution)/shard_map/ppermute | solution.py:641
  41.0 22.2 %all-to-all-start.1 = ((f32[32,8,128]{2,1,0:T(8,128)}), f32[32,8,128]{2,1,0:T(8,128)S(1)}, u32[]{:S(2)}, u32[]{:S(2)}) async-start(f32[32,8,128]{2,1,0:T(8,128)} %broadcast_in_dim.3), calls=%async_computation.1 | async-start | bytes 262144 | tf_op jit(solution)/shard_map/all_to_all | solution.py:645
  51.5 7.8 %collective-permute-start.3 = (f32[256,128]{1,0:T(8,128)S(1)}, f32[256,128]{1,0:T(8,128)S(1)}, u32[]{:S(2)}, u32[]{:S(2)}) collective-permute-start(f32[256,128]{1,0:T(8,128)S(1)} %get-tuple-element.54), channel_id=1, source_target_pairs={{0,1},{1,2},{2,3},{3,4},{4,5},{5,6},{6,7},{7,8},{8,9},{9,10},{10,1... | collective-permute-start | bytes 393224 | tf_op jit(solution)/shard_map/ppermute | solution.py:641

commit v7 on v6

--- a/solution.py
+++ b/solution.py
@@ -95,7 +95,7 @@
 
 
 def prep_kernel(
-    q_hbm, mass_hbm, internal_hbm, velocity_hbm, coef_ref, pack_ref, q, mass, internal, sems
+    q_hbm, mass_hbm, internal_hbm, velocity_hbm, coef_ref, pack_ref, rows_ref, corner_ref, q, mass, internal, sems
 ):
     copies = [
         pltpu.make_async_copy(src, dst, sems.at[i])
@@ -132,6 +132,10 @@
         for i in range(1, NC):
             acc = jnp.where(group == i, pltpu.roll(coef_ref[i, tile(t), :], 8 * i, 1), acc)
         pack_ref[2, tile(t), :] = acc
+    for n in range(3):
+        corner_ref[n] = pack_ref[n, 0:8, :]
+    for f in range(NA):
+        rows_ref[f] = q[f, 0:8, :] if f < NF else coef_ref[f - NF, 0:8, :]
 
 
 def pairs():
@@ -182,31 +186,41 @@
     return out
 
 
-def own_kernel(q_ref, coef_ref, warm_ref, last_ref, sums_ref, red):
-    lane = lanes()
-    red[...] = jnp.zeros_like(red)
+def each():
+    return [(k, y) for k in range(K) for y in range(2)]
+
+
+def last_columns(field, coef, last_ref, at, lane):
     group = lane >> 3
-    for t in range(Z // 8):
-        last = [None] * 3
+    got = []
+    for c in range(2):
+        acc = None
         for y in range(2):
             for k in range(K):
                 i = 8 * y + k
-                fields = [q_ref[4 * k + 2 * c + y, tile(t), :] for c in range(2)]
-                fields.append(
-                    coef_ref[y, tile(t), :] * fields[0] + coef_ref[2 + y, tile(t), :] * fields[1]
-                )
-                warm_ref[2 * k + y, tile(t), :] = fields[2]
-                for n in range(2):
-                    part = pltpu.roll(fields[n], (8 * i + 8) % X, 1) if i < 15 else fields[n]
-                    last[n] = part if i == 0 else jnp.where(group == i, part, last[n])
-        full = [
-            fill([pltpu.roll(coef_ref[2 * n + y, tile(t), :], 8, 1) for y in range(2)], lane)
-            for n in range(3)
-        ]
-        last[2] = full[0] * last[0] + full[1] * last[1]
-        for n in range(3):
-            last_ref[n, tile(t), :] = last[n]
-            last_ref[3 + n, tile(t), :] = full[n]
+                part = field(4 * k + 2 * c + y)
+                part = pltpu.roll(part, (8 * i + 8) % X, 1) if i < 15 else part
+                acc = part if i == 0 else jnp.where(group == i, part, acc)
+        got.append(acc)
+    full = [fill([pltpu.roll(coef(2 * n + y), 8, 1) for y in range(2)], lane) for n in range(3)]
+    got.append(full[0] * got[0] + full[1] * got[1])
+    for n, part in enumerate(got + full):
+        last_ref[n, at : at + 8, :] = part
+
+
+def own_kernel(q_ref, coef_ref, wm_ref, wp_ref, warm_ref, last_ref, sums_ref, red):
+    lane = lanes()
+    red[...] = jnp.zeros_like(red)
+    for t in range(Z // 8):
+        for k, y in each():
+            warm_ref[2 * k + y, tile(t), :] = (
+                coef_ref[y, tile(t), :] * q_ref[4 * k + y, tile(t), :]
+                + coef_ref[2 + y, tile(t), :] * q_ref[4 * k + 2 + y, tile(t), :]
+            )
+        last_columns(
+            lambda f: q_ref[f, tile(t), :], lambda n: coef_ref[n, tile(t), :],
+            last_ref, 8 * t, lane,
+        )
     for k, m, l in pairs():
         acc = jnp.zeros((8, X), F32)
         for p in range(4):
@@ -233,16 +247,6 @@
         packed[n, rows, X : 2 * X] = part
 
 
-def wire_kernel(q_ref, side_ref, last_ref, coef_ref, rows_ref, packed):
-    join(side_ref, last_ref, packed, 0, 0, lanes())
-    for f in range(NF):
-        rows_ref[f] = q_ref[f, 0:8, :]
-    for n in range(6):
-        rows_ref[NF + n] = packed[n, :, 0:X]
-        rows_ref[NF + 6 + n] = packed[n, :, X : 2 * X]
-        rows_ref[NF + 12 + n] = coef_ref[n, 0:8, :]
-
-
 def split(x):
     high = x.astype(jnp.bfloat16)
     return high, (x - high.astype(F32)).astype(jnp.bfloat16)
@@ -254,10 +258,6 @@
 
 def rest(at, other):
     return 16.0 * (at(-1) + at(1) + other) - (at(-2) + at(2)) - 60.0 * at(0)
-
-
-def each():
-    return [(k, y) for k in range(K) for y in range(2)]
 
 
 def main_rates(count, weights, r_at, e_at, t_at):
@@ -372,8 +372,8 @@
 
 
 def inner_kernel(
-    q_ref, coef_ref, warm_ref, side_ref, last_ref, own_ref, wm_ref, wp_ref,
-    ad_ref, bd_ref, ap_ref, bp_ref, tail_ref, packed_ref, sums_ref,
+    q_ref, coef_ref, warm_ref, side_ref, last_ref, own_ref, below_ref, wm_ref, wp_ref,
+    ad_ref, bd_ref, ap_ref, bp_ref, tail_ref, packed_ref, under_ref, kept_ref, sums_ref,
     packed, pa, qp, am, tm, red, extra,
 ):
     lane = lanes()
@@ -386,6 +386,8 @@
         packed_ref[n] = pa[n, 22:30, :]
     for n in range(6):
         packed_ref[3 + n] = packed[n, 24:32, :]
+        kept_ref[n] = coef_ref[n, 24:32, :]
+    last_columns(lambda f: below_ref[f], lambda n: below_ref[NF + n], under_ref, 0, lane)
     keep = inside(8)
 
     def vectors(j, carry):
@@ -444,18 +446,17 @@
 
 
 def edge_kernel(
-    q_ref, coef_ref, warm_ref, below_ref, tail_ref, packed_ref, inner_ref, wm_ref, wp_ref,
+    q_ref, kept_ref, warm_ref, below_ref, corner_ref, last_ref, tail_ref, packed_ref, inner_ref, wm_ref, wp_ref,
     ad_ref, bd_ref, ap_ref, bp_ref, sums_ref,
     em, ec, wm, packed, pa, qp, am, tm, red, extra,
 ):
     lane = lanes()
     red[...] = jnp.zeros_like(red)
     for n in range(NC):
-        ec[n, 0:8, :] = coef_ref[n, 24:32, :]
-        ec[n, 8:16, :] = below_ref[NF + 12 + n]
+        ec[n, 0:8, :] = kept_ref[n]
+        ec[n, 8:16, :] = below_ref[NF + n]
         packed[n, 0:8, :] = packed_ref[3 + n]
-        packed[n, 8:16, 0:X] = below_ref[NF + n]
-        packed[n, 8:16, X : 2 * X] = below_ref[NF + 6 + n]
+    join(corner_ref, last_ref, packed, 0, 8, lane)
     for n in range(3):
         pa[n, 0:8, :] = packed_ref[n]
     packed_steps(packed, wp_ref, pa, (qp, ap_ref, bp_ref), (6, 8, 8), (4, 6), 8, lane)
@@ -641,6 +642,14 @@
     return lax.ppermute(array, axes, [(i, (i + step) % size) for i in range(size)])
 
 
+def diagonal(array):
+    gx, gz = lax.axis_size(GX), lax.axis_size(GZ)
+    pairs_of = [
+        (i * gz + j, (i - 1) % gx * gz + (j - 1) % gz) for i in range(gx) for j in range(gz)
+    ]
+    return lax.ppermute(array, GX + GZ, pairs_of)
+
+
 def gathered(array, axes):
     return lax.all_to_all(array, axes, 0, 0)
 
@@ -652,29 +661,30 @@
     half, small, red = (2 * K, Z, X), (3, Z, X), (20, 8, X)
     wm, wp = (jnp.asarray(w) for w in bands())
     q = tangents.reshape(whole)
-    coef, pack = call(
+    coef, pack, rows, corner = call(
         prep_kernel,
-        [(NC, Z, X), small],
+        [(NC, Z, X), small, (NA, 8, X), (3, 8, X)],
         [whole, (2, Z, X), (2, Z, X), pltpu.SemaphoreType.DMA((4,))],
         limit=60,
         in_specs=[pl.BlockSpec(memory_space=pl.ANY)] * 4,
     )(q, mass, internal, velocity)
     side = ring(pack, GX, -1)
-    warm, last, own = call(own_kernel, [half, (6, Z, X), (8, X)], [(5, 8, X)])(q, coef)
-    side, warm, last, own = lax.optimization_barrier((side, warm, last, own))
-    (rows,) = call(wire_kernel, [(NF + 18, 8, X)], [(6, 8, 2 * X)], cost=1000)(q, side, last, coef)
     below = ring(rows, GZ, -1)
-    ad, bd, ap, bp, tail, packed, part = call(
+    corner = diagonal(corner)
+    warm, last, own = call(own_kernel, [half, (6, Z, X), (8, X)], [(5, 8, X)])(
+        q, coef, wm, wp
+    )
+    ad, bd, ap, bp, tail, packed, under, kept, part = call(
         inner_kernel,
-        [inner, inner, (2, 24, X), (2, 24, X), edge, (9, 8, 2 * X), (8, X)],
+        [inner, inner, (2, 24, X), (2, 24, X), edge, (9, 8, 2 * X), (6, 8, X), (6, 8, X), (8, X)],
         [(6, Z, 2 * X), (3, Z, 2 * X), (2, 24, X), (K, 4, Z, X), (K, 2, Z, X), red, red],
-    )(q, coef, warm, side, last, own, wm, wp)
+    )(q, coef, warm, side, last, own, below, wm, wp)
     ade, bde, ape, bpe, sums = call(
         edge_kernel,
         [edge, edge, (2, 8, X), (2, 8, X), (near, 8, X)],
         [(NF, 16, X), (NC, 16, X), (K, 2, 16, X), (6, 16, 2 * X), (3, 16, 2 * X), (2, 8, X)]
         + [(K, 4, 16, X), (K, 2, 16, X), red, red],
-    )(q, coef, warm, below, tail, packed, part, wm, wp)
+    )(q, kept, warm, below, corner, under, tail, packed, part, wm, wp)
     sums = jnp.sum(gathered(sums, NEAR), axis=0)
     (give,) = call(give_kernel, [(2, 2, Z, X)])(ap, bp, ape, bpe)
     got = ring(give, GX, 1)

time: 64.9 us -> 64.5 us (level)
  local copies, waits for them, and re-layouts: 1.56 us -> 3.42 us
  starting transfers between devices: 36.4 us -> 34.8 us
  waiting for transfers between devices: 15.7 us -> 14.9 us
    all_to_all x2, starting transfers between devices: 23.5 us -> 19.1 us  [gathered(): return lax.all_to_all(array, axes, 0, 0)]
    ppermute x0 -> x1, starting transfers between devices: none -> 1.92 us  [diagonal(): return lax.ppermute(array, GX + GZ, pairs_of)]
    unnamed x8 -> x10, local copies, waits for them, and re-layouts: 0.9 us -> 2.75 us
    ppermute x4, starting transfers between devices: 12.9 us -> 13.8 us  [ring(): lax.ppermute(array, axes, [(i, (i + step) % size) for i in range(size)])]
    ppermute x4, waiting for transfers between devices: 11 us -> 10.2 us  [ring(): lax.ppermute(array, axes, [(i, (i + step) % size) for i in range(size)])]
    pallas_call x3 -> x2, Pallas kernels: 2.87 us -> 2.62 us  [the longest x1 2.09 us: per_device(): call(prep_kernel, [(NC, Z, X), small, (NA, 8, X), (3, 8, X)], [whole, (2,...]
  transfers between devices with their start and end apart: 6 -> 7, of which waited for: 6 -> 4; matrix products, arithmetic and copies ran while one was open for 0% -> 0% of each run, Pallas kernels for 7% -> 7%
where the time goes in v7:
time: 64.5 us; the launch traced here: 64 us
  starting transfers between devices  34.8 us (54%)
  waiting for transfers between devices  14.9 us (23%)
  Pallas kernels  10.2 us (16%)
  local copies, waits for them, and re-layouts  3.42 us (5%)
  between operations  0.77 us (1%)
    all_to_all x2, starting transfers between devices, gathered(): return lax.all_to_all(array, axes, 0, 0)  19.1 us
    ppermute x4, starting transfers between devices, ring(): lax.ppermute(array, axes, [(i, (i + step) % size) for i in range(size)])  13.8 us
    ppermute x4, waiting for transfers between devices, ring(): lax.ppermute(array, axes, [(i, (i + step) % size) for i in range(size)])  10.2 us
    all_to_all x2, waiting for transfers between devices, gathered(): return lax.all_to_all(array, axes, 0, 0)  4.68 us
    pallas_call x1, Pallas kernels, per_device(): call(inner_kernel, [inner, inner, (2, 24, X), (2, 24, X), edge, (9, 8, 2...  3.16 us
    unnamed x10, local copies, waits for them, and re-layouts  2.75 us
    pallas_call x1, Pallas kernels, per_device(): call(edge_kernel, [edge, edge, (2, 8, X), (2, 8, X), (near, 8, X)], [(NF,...  2.2 us
    pallas_call x1, Pallas kernels, per_device(): call(prep_kernel, [(NC, Z, X), small, (NA, 8, X), (3, 8, X)], [whole, (2,...  2.09 us
  transfers between devices with their start and end apart: 7, of which 4 were waited for; matrix products, arithmetic and copies ran while one was open for 0% of the time, Pallas kernels for 7%

profile of v7, /device:TPU:4, one launch (start us, length us, event | category | flops | bytes accessed | tf_op | source)
XLA Modules:
  0.0 64.0 jit_solution(4803960625333439856)
XLA Ops:
  0.6 0.0 copy-start
  0.6 2.1 %shard_map.77 = (f32[6,32,128]{2,1,0:T(8,128)}, f32[3,32,128]{2,1,0:T(8,128)}, f32[38,8,128]{2,1,0:T(8,128)}, f32[3,8,128]{2,1,0:T(8,128)}) custom-call(f32[32,32,128]{2,1,0:T(8,128)} %bitcast.3, f32[2,32,128]{2,1,0:T(8,128)} %mass_hbm.1, f32[2,32,128]{2,1,0:T(8,128)} %internal_hbm.1, f32[2,32,128]{2,1,0:T(8,128)} %velocity_hbm.1), custom_call_target="tpu_custom_call" | custom-call | flops 2000000 | bytes 2000000 | tf_op jit(solution)/shard_map/pallas_call | solution.py:664
  2.7 1.9 %collective-permute-start.1 = (f32[38,8,128]{2,1,0:T(8,128)}, f32[38,8,128]{2,1,0:T(8,128)S(1)}, u32[]{:S(2)}, u32[]{:S(2)}) collective-permute-start(f32[38,8,128]{2,1,0:T(8,128)} %get-tuple-element.35), channel_id=1, source_target_pairs={{0,31},{1,0},{2,1},{3,2},{4,3},{5,4},{6,5},{7,6},{8,7},{9,8},{10,9... | collective-permute-start | bytes 466952 | tf_op jit(solution)/shard_map/ppermute | solution.py:642
  4.7 6.8 %collective-permute-start = (f32[3,32,128]{2,1,0:T(8,128)}, f32[3,32,128]{2,1,0:T(8,128)S(1)}, u32[]{:S(2)}, u32[]{:S(2)}) collective-permute-start(f32[3,32,128]{2,1,0:T(8,128)} %get-tuple-element.32), channel_id=1, source_target_pairs={{0,480},{32,0},{64,32},{96,64},{128,96},{160,128},{192,160},{224,1... | collective-permute-start | bytes 147464 | tf_op jit(solution)/shard_map/ppermute | solution.py:642
  11.5 1.9 %collective-permute-start.2 = (f32[3,8,128]{2,1,0:T(8,128)}, f32[3,8,128]{2,1,0:T(8,128)S(1)}, u32[]{:S(2)}, u32[]{:S(2)}) collective-permute-start(f32[3,8,128]{2,1,0:T(8,128)} %get-tuple-element.39), channel_id=1, source_target_pairs={{0,511},{1,480},{2,481},{3,482},{4,483},{5,484},{6,485},{7,486},{8... | collective-permute-start | bytes 36872 | tf_op jit(solution)/shard_map/ppermute | solution.py:650
  13.4 0.0 copy-done
  13.5 0.0 copy-start.1
  13.5 0.9 %copy-done.1 = bf16[2,256,256]{2,1,0:T(8,128)(2,1)S(1)} copy-done((bf16[2,256,256]{2,1,0:T(8,128)(2,1)S(1)}, bf16[2,256,256]{2,1,0:T(8,128)(2,1)}, u32[]{:S(2)}) %copy-start.1) | copy-done | bytes 262168
  14.4 0.0 copy-start.3
  14.4 0.9 %copy-done.3 = bf16[256,256]{1,0:T(8,128)(2,1)S(1)} copy-done((bf16[256,256]{1,0:T(8,128)(2,1)S(1)}, bf16[256,256]{1,0:T(8,128)(2,1)}, u32[]{:S(2)}) %copy-start.3) | copy-done | bytes 131096
  15.3 0.0 copy-start.4
  15.3 0.9 %copy-done.4 = f32[6,32,128]{2,1,0:T(8,128)S(1)} copy-done((f32[6,32,128]{2,1,0:T(8,128)S(1)}, f32[6,32,128]{2,1,0:T(8,128)}, u32[]{:S(2)}) %copy-start.4) | copy-done | bytes 98328
  16.2 0.5 shard_map.78
  16.7 0.0 collective-permute-done.side_ref
  16.7 0.0 collective-permute-done.1.below_ref
  16.8 0.0 copy-start.2
  16.8 3.2 %shard_map.79 = (f32[32,24,128]{2,1,0:T(8,128)S(1)}, f32[32,24,128]{2,1,0:T(8,128)S(1)}, f32[2,24,128]{2,1,0:T(8,128)S(1)}, f32[2,24,128]{2,1,0:T(8,128)S(1)}, f...) custom-call(f32[32,32,128]{2,1,0:T(8,128)S(1)} %bitcast.5, ...), custom_call_target="tpu_custom_call" | custom-call | flops 2000000 | bytes 2000000 | tf_op jit(solution)/shard_map/pallas_call | solution.py:677
  19.9 0.0 collective-permute-done.2.corner_ref
  19.9 0.0 copy-done.2
  20.0 2.2 %shard_map.80 = (f32[32,8,128]{2,1,0:T(8,128)S(1)}, f32[32,8,128]{2,1,0:T(8,128)S(1)}, f32[2,8,128]{2,1,0:T(8,128)S(1)}, f32[2,8,128]{2,1,0:T(8,128)S(1)}, f32[16,8,128]{2,1,0:T(8,128)}) custom-call(f32[32,32,128]{2,1,0:T(8,128)S(1)} %bitcast.6, f32[6,8,128]{2,1,0:T(8,128)S(1)} %get-tuple-element.38.kept_ref, f32[16,32,128]{2,1,0:T(8,128)S(1)} %get-tuple-element.31.warm_ref, ...), custom_call_target="tpu_custom_call" | custom-call | flops 2000000 | bytes 2000000 | tf_op jit(solution)/shard_map/pallas_call | solution.py:682
  22.2 13.7 %all-to-all-start = ((f32[16,8,128]{2,1,0:T(8,128)}), f32[16,8,128]{2,1,0:T(8,128)S(1)}, u32[]{:S(2)}, u32[]{:S(2)}) async-start(f32[16,8,128]{2,1,0:T(8,128)} %get-tuple-element.50), calls=%async_computation | async-start | bytes 131072 | tf_op jit(solution)/shard_map/all_to_all | solution.py:654
  35.8 3.1 %collective-permute-start.3 = (f32[2,2,32,128]{3,2,1,0:T(8,128)S(1)}, f32[2,2,32,128]{3,2,1,0:T(8,128)S(1)}, u32[]{:S(2)}, u32[]{:S(2)}) collective-permute-start(f32[2,2,32,128]{3,2,1,0:T(8,128)S(1)} %shard_map.81.mine_ref), channel_id=1, source_target_pairs={{0,32},{32,64},{64,96},{96,128},{128,160},{160,192},{192,224},{224... | collective-permute-start | bytes 196616 | tf_op jit(solution)/shard_map/ppermute | solution.py:642
  38.9 0.8 %all-to-all-done = f32[16,8,128]{2,1,0:T(8,128)S(1)} async-done(((f32[16,8,128]{2,1,0:T(8,128)}), f32[16,8,128]{2,1,0:T(8,128)S(1)}, u32[]{:S(2)}, u32[]{:S(2)}) %all-to-all-start) | async-done | bytes 65568 | tf_op jit(solution)/shard_map/all_to_all | solution.py:654
  39.8 4.3 %collective-permute-done.3.got_ref = f32[2,2,32,128]{3,2,1,0:T(8,128)S(1)} collective-permute-done((f32[2,2,32,128]{3,2,1,0:T(8,128)S(1)}, f32[2,2,32,128]{3,2,1,0:T(8,128)S(1)}, u32[]{:S(2)}, u32[]{:S(2)}) %collective-permute-start.3) | collective-permute-done | bytes 65568 | tf_op jit(solution)/shard_map/ppermute | solution.py:642
  44.1 0.7 %broadcast_in_dim.3 = f32[32,8,128]{2,1,0:T(8,128)} broadcast(f32[8,128]{1,0:T(8,128)S(1)} %reduce_sum.9), dimensions={1,2} | broadcast | bytes 135168 | tf_op jit(solution)/shard_map/broadcast_in_dim | solution.py:692
  44.8 5.4 %all-to-all-start.1 = ((f32[32,8,128]{2,1,0:T(8,128)}), f32[32,8,128]{2,1,0:T(8,128)S(1)}, u32[]{:S(2)}, u32[]{:S(2)}) async-start(f32[32,8,128]{2,1,0:T(8,128)} %broadcast_in_dim.3), calls=%async_computation.1 | async-start | bytes 262144 | tf_op jit(solution)/shard_map/all_to_all | solution.py:654
  50.2 0.9 %shard_map.82 = (f32[32,32,128]{2,1,0:T(8,128)S(1)}, f32[32,32,128]{2,1,0:T(8,128)S(1)}, f32[256,128]{1,0:T(8,128)S(1)}) custom-call(f32[32,24,128]{2,1,0:T(8,128)S(1)} %get-tuple-element.36.ad_ref, f32[32,24,128]{2,1,0:T(8,128)S(1)} %get-tuple-element.37.bd_ref, f32[32,8,128]{2,1,0:T(8,128)S(1)} %get-tuple-element.44.ade_ref, ...), custom_call_target="tpu_custom_call" | custom-call | flops 2000000 | bytes 2000000 | tf_op jit(solution)/shard_map/pallas_call | solution.py:693
  51.1 1.9 %collective-permute-start.4 = (f32[256,128]{1,0:T(8,128)S(1)}, f32[256,128]{1,0:T(8,128)S(1)}, u32[]{:S(2)}, u32[]{:S(2)}) collective-permute-start(f32[256,128]{1,0:T(8,128)S(1)} %get-tuple-element.54), channel_id=1, source_target_pairs={{0,1},{1,2},{2,3},{3,4},{4,5},{5,6},{6,7},{7,8},{8,9},{9,10},{10,1... | collective-permute-start | bytes 393224 | tf_op jit(solution)/shard_map/ppermute | solution.py:642
  53.0 5.9 %collective-permute-done.4.above_ref = f32[256,128]{1,0:T(8,128)S(1)} collective-permute-done((f32[256,128]{1,0:T(8,128)S(1)}, f32[256,128]{1,0:T(8,128)S(1)}, u32[]{:S(2)}, u32[]{:S(2)}) %collective-permute-start.4) | collective-permute-done | bytes 131104 | tf_op jit(solution)/shard_map/ppermute | solution.py:642
  58.9 3.9 %all-to-all-done.1.sums_ref = f32[32,8,128]{2,1,0:T(8,128)S(1)} async-done(((f32[32,8,128]{2,1,0:T(8,128)}), f32[32,8,128]{2,1,0:T(8,128)S(1)}, u32[]{:S(2)}, u32[]{:S(2)}) %all-to-all-start.1) | async-done | bytes 131104 | tf_op jit(solution)/shard_map/all_to_all | solution.py:654
  62.8 1.3 %shard_map.83 = (f32[32,32,128]{2,1,0:T(8,128)}, f32[8,128]{1,0:T(8,128)}) custom-call(f32[32,32,128]{2,1,0:T(8,128)S(1)} %bitcast.7, f32[32,32,128]{2,1,0:T(8,128)S(1)} %get-tuple-element.52.a_ref, f32[32,32,128]{2,1,0:T(8,128)S(1)} %get-tuple-element.53.b_ref, f32[256,128]{1,0:T(8,128)S(1)} %collective-permute-done.4.above_ref, ...), custom_call_target="tpu_custom_call" | custom-call | flops 2000000 | bytes 2000000 | tf_op jit(solution)/shard_map/pallas_call | solution.py:695
  (2 shorter events, 0.0 us)
Async XLA Ops:
  0.6 12.8 %copy-start = (f32[8,2,2,32,128]{4,3,2,1,0:T(8,128)S(1)}, f32[8,2,2,32,128]{4,3,2,1,0:T(8,128)}, u32[]{:S(2)}) copy-start(f32[8,2,2,32,128]{4,3,2,1,0:T(8,128)} %param.6) | copy-start | bytes 1572868
  2.7 14.0 %collective-permute-start.1 = (f32[38,8,128]{2,1,0:T(8,128)}, f32[38,8,128]{2,1,0:T(8,128)S(1)}, u32[]{:S(2)}, u32[]{:S(2)}) collective-permute-start(f32[38,8,128]{2,1,0:T(8,128)} %get-tuple-element.35), channel_id=1, source_target_pairs={{0,31},{1,0},{2,1},{3,2},{4,3},{5,4},{6,5},{7,6},{8,7},{9,8},{10,9... | collective-permute-start | bytes 466952 | tf_op jit(solution)/shard_map/ppermute | solution.py:642
  4.7 12.1 %collective-permute-start = (f32[3,32,128]{2,1,0:T(8,128)}, f32[3,32,128]{2,1,0:T(8,128)S(1)}, u32[]{:S(2)}, u32[]{:S(2)}) collective-permute-start(f32[3,32,128]{2,1,0:T(8,128)} %get-tuple-element.32), channel_id=1, source_target_pairs={{0,480},{32,0},{64,32},{96,64},{128,96},{160,128},{192,160},{224,1... | collective-permute-start | bytes 147464 | tf_op jit(solution)/shard_map/ppermute | solution.py:642
  11.5 8.4 %collective-permute-start.2 = (f32[3,8,128]{2,1,0:T(8,128)}, f32[3,8,128]{2,1,0:T(8,128)S(1)}, u32[]{:S(2)}, u32[]{:S(2)}) collective-permute-start(f32[3,8,128]{2,1,0:T(8,128)} %get-tuple-element.39), channel_id=1, source_target_pairs={{0,511},{1,480},{2,481},{3,482},{4,483},{5,484},{6,485},{7,486},{8... | collective-permute-start | bytes 36872 | tf_op jit(solution)/shard_map/ppermute | solution.py:650
  13.5 1.0 %copy-start.1 = (bf16[2,256,256]{2,1,0:T(8,128)(2,1)S(1)}, bf16[2,256,256]{2,1,0:T(8,128)(2,1)}, u32[]{:S(2)}) copy-start(bf16[2,256,256]{2,1,0:T(8,128)(2,1)} %constant.7.clone.wp_ref) | copy-start | bytes 786436
  14.4 0.9 %copy-start.3 = (bf16[256,256]{1,0:T(8,128)(2,1)S(1)}, bf16[256,256]{1,0:T(8,128)(2,1)}, u32[]{:S(2)}) copy-start(bf16[256,256]{1,0:T(8,128)(2,1)} %constant.6.clone.wm_ref) | copy-start | bytes 393220
  15.3 0.9 %copy-start.4 = (f32[6,32,128]{2,1,0:T(8,128)S(1)}, f32[6,32,128]{2,1,0:T(8,128)}, u32[]{:S(2)}) copy-start(f32[6,32,128]{2,1,0:T(8,128)} %get-tuple-element.30.coef_ref) | copy-start | bytes 294916
  16.8 3.2 %copy-start.2 = (bf16[2,256,256]{2,1,0:T(8,128)(2,1)S(1)}, bf16[2,256,256]{2,1,0:T(8,128)(2,1)}, u32[]{:S(2)}) copy-start(bf16[2,256,256]{2,1,0:T(8,128)(2,1)} %constant.7.clone.wp_ref) | copy-start | bytes 786436
  22.2 17.6 %all-to-all-start = ((f32[16,8,128]{2,1,0:T(8,128)}), f32[16,8,128]{2,1,0:T(8,128)S(1)}, u32[]{:S(2)}, u32[]{:S(2)}) async-start(f32[16,8,128]{2,1,0:T(8,128)} %get-tuple-element.50), calls=%async_computation | async-start | bytes 131072 | tf_op jit(solution)/shard_map/all_to_all | solution.py:654
  35.8 8.3 %collective-permute-start.3 = (f32[2,2,32,128]{3,2,1,0:T(8,128)S(1)}, f32[2,2,32,128]{3,2,1,0:T(8,128)S(1)}, u32[]{:S(2)}, u32[]{:S(2)}) collective-permute-start(f32[2,2,32,128]{3,2,1,0:T(8,128)S(1)} %shard_map.81.mine_ref), channel_id=1, source_target_pairs={{0,32},{32,64},{64,96},{96,128},{128,160},{160,192},{192,224},{224... | collective-permute-start | bytes 196616 | tf_op jit(solution)/shard_map/ppermute | solution.py:642
  44.8 18.0 %all-to-all-start.1 = ((f32[32,8,128]{2,1,0:T(8,128)}), f32[32,8,128]{2,1,0:T(8,128)S(1)}, u32[]{:S(2)}, u32[]{:S(2)}) async-start(f32[32,8,128]{2,1,0:T(8,128)} %broadcast_in_dim.3), calls=%async_computation.1 | async-start | bytes 262144 | tf_op jit(solution)/shard_map/all_to_all | solution.py:654
  51.1 7.8 %collective-permute-start.4 = (f32[256,128]{1,0:T(8,128)S(1)}, f32[256,128]{1,0:T(8,128)S(1)}, u32[]{:S(2)}, u32[]{:S(2)}) collective-permute-start(f32[256,128]{1,0:T(8,128)S(1)} %get-tuple-element.54), channel_id=1, source_target_pairs={{0,1},{1,2},{2,3},{3,4},{4,5},{5,6},{6,7},{7,8},{8,9},{9,10},{10,1... | collective-permute-start | bytes 393224 | tf_op jit(solution)/shard_map/ppermute | solution.py:642

commit v8 on v7

--- a/solution.py
+++ b/solution.py
@@ -51,7 +51,7 @@
         packed.append(v)
     return [
         np.concatenate(main, axis=1).astype(jnp.bfloat16),
-        np.stack(packed).astype(jnp.bfloat16),
+        *(v.astype(jnp.bfloat16) for v in packed),
     ]
 
 
@@ -208,9 +208,19 @@
         last_ref[n, at : at + 8, :] = part
 
 
-def own_kernel(q_ref, coef_ref, wm_ref, wp_ref, warm_ref, last_ref, sums_ref, red):
+def square_kernel(q_ref, sums_ref, red):
+    red[...] = jnp.zeros_like(red)
+    for k, m, l in pairs():
+        acc = jnp.zeros((8, X), F32)
+        for p in range(4):
+            for t in range(Z // 8):
+                acc = acc + q_ref[4 * k + p, tile(t), :] * q_ref[4 * l + p, tile(t), :]
+        put(red, m, k, acc)
+    sums_ref[...] = columns(jnp.zeros((8, X), F32), lanes(), red, None, (0,))
+
+
+def own_kernel(q_ref, coef_ref, square_ref, warm_ref, last_ref, sums_ref):
     lane = lanes()
-    red[...] = jnp.zeros_like(red)
     for t in range(Z // 8):
         for k, y in each():
             warm_ref[2 * k + y, tile(t), :] = (
@@ -221,19 +231,13 @@
             lambda f: q_ref[f, tile(t), :], lambda n: coef_ref[n, tile(t), :],
             last_ref, 8 * t, lane,
         )
-    for k, m, l in pairs():
-        acc = jnp.zeros((8, X), F32)
-        for p in range(4):
-            for t in range(Z // 8):
-                acc = acc + q_ref[4 * k + p, tile(t), :] * q_ref[4 * l + p, tile(t), :]
-        put(red, m, k, acc)
     speed = jnp.zeros((8, X), F32)
     for y in range(2):
         for t in range(Z // 8):
             v = coef_ref[4 + y, tile(t), :]
             speed = speed + v * v
-    result = jnp.where(lane == 40, jnp.sum(speed, axis=1, keepdims=True), 0.0)
-    sums_ref[...] = columns(result, lane, red, None, (0,))
+    total = jnp.sum(speed, axis=1, keepdims=True)
+    sums_ref[...] = jnp.where(lane == 40, total, square_ref[...])
 
 
 def join(side_ref, last_ref, packed, t, at, lane):
@@ -289,7 +293,7 @@
 def packed_rate(speed, weights, at):
     def along(n, w):
         high, low = split(at(n, 0))
-        return product(high, weights[w]) + product(low, weights[w])
+        return product(high, weights[1 + w]) + product(low, weights[1 + w])
 
     rate_r = speed * along(0, 0) + (viscosity / 12.0) * (
         along(0, 1) + rest(lambda d: at(0, d), turned(at(0, 0)))
@@ -372,7 +376,7 @@
 
 
 def inner_kernel(
-    q_ref, coef_ref, warm_ref, side_ref, last_ref, own_ref, below_ref, wm_ref, wp_ref,
+    q_ref, coef_ref, warm_ref, side_ref, last_ref, own_ref, below_ref, w_ref,
     ad_ref, bd_ref, ap_ref, bp_ref, tail_ref, packed_ref, under_ref, kept_ref, sums_ref,
     packed, pa, qp, am, tm, red, extra,
 ):
@@ -380,7 +384,7 @@
     red[...] = jnp.zeros_like(red)
     for t in range(Z // 8):
         join(side_ref, last_ref, packed, t, 8 * t, lane)
-    packed_steps(packed, wp_ref, pa, (qp, ap_ref, bp_ref), (2, 2, 28), (4, 4), 24, lane)
+    packed_steps(packed, w_ref, pa, (qp, ap_ref, bp_ref), (2, 2, 28), (4, 4), 24, lane)
     packed_sums(extra, (qp, ap_ref, bp_ref), 3, lane)
     for n in range(3):
         packed_ref[n] = pa[n, 22:30, :]
@@ -395,7 +399,7 @@
         order = [(k, y, r) for k, y in planes for r in (2, 10, 18, 22)]
         parts = main_rates(
             len(order),
-            wm_ref,
+            w_ref.at[0],
             lambda i: q_ref[4 * order[i][0] + order[i][1], order[i][2] : order[i][2] + 8, :],
             lambda i: q_ref[4 * order[i][0] + 2 + order[i][1], order[i][2] : order[i][2] + 8, :],
             lambda i: warm_ref[2 * order[i][0] + order[i][1], order[i][2] : order[i][2] + 8, :],
@@ -416,7 +420,7 @@
         order = [(k, y, r) for k, y in planes for r in (4, 12, 20)]
         parts = main_rates(
             len(order),
-            wm_ref,
+            w_ref.at[0],
             lambda i: am[order[i][0], order[i][1], order[i][2] : order[i][2] + 8, :],
             lambda i: am[order[i][0], 2 + order[i][1], order[i][2] : order[i][2] + 8, :],
             lambda i: tm[order[i][0], order[i][1], order[i][2] : order[i][2] + 8, :],
@@ -446,7 +450,7 @@
 
 
 def edge_kernel(
-    q_ref, kept_ref, warm_ref, below_ref, corner_ref, last_ref, tail_ref, packed_ref, inner_ref, wm_ref, wp_ref,
+    q_ref, kept_ref, warm_ref, below_ref, corner_ref, last_ref, tail_ref, packed_ref, inner_ref, w_ref,
     ad_ref, bd_ref, ap_ref, bp_ref, sums_ref,
     em, ec, wm, packed, pa, qp, am, tm, red, extra,
 ):
@@ -459,7 +463,7 @@
     join(corner_ref, last_ref, packed, 0, 8, lane)
     for n in range(3):
         pa[n, 0:8, :] = packed_ref[n]
-    packed_steps(packed, wp_ref, pa, (qp, ap_ref, bp_ref), (6, 8, 8), (4, 6), 8, lane)
+    packed_steps(packed, w_ref, pa, (qp, ap_ref, bp_ref), (6, 8, 8), (4, 6), 8, lane)
     packed_sums(extra, (qp, ap_ref, bp_ref), 1, lane)
     keep = inside(8)
     for k in range(K):
@@ -476,7 +480,7 @@
     order = each()
     parts = main_rates(
         16,
-        wm_ref,
+        w_ref.at[0],
         lambda i: em[4 * order[i][0] + order[i][1], 6:14, :],
         lambda i: em[4 * order[i][0] + 2 + order[i][1], 6:14, :],
         lambda i: wm[order[i][0], order[i][1], 6:14, :],
@@ -498,7 +502,7 @@
         )
     parts = main_rates(
         16,
-        wm_ref,
+        w_ref.at[0],
         lambda i: am[order[i][0], order[i][1], 6:14, :],
         lambda i: am[order[i][0], 2 + order[i][1], 6:14, :],
         lambda i: tm[order[i][0], order[i][1], 6:14, :],
@@ -552,7 +556,7 @@
                             down_ref[r : r + 4, :] = part[4:8, :]
 
 
-def finish_kernel(cells, q_ref, a_ref, b_ref, above_ref, sums_ref, out_ref, growth_ref, first):
+def finish_kernel(cells, q_ref, a_ref, b_ref, above_ref, sums_ref, out_hbm, growth_ref, first, out, sems):
     lane = lanes()
     row = lax.broadcasted_iota(jnp.int32, (8, X), 0)
     for n, ref in enumerate((a_ref, b_ref)):
@@ -607,6 +611,7 @@
             growth = jnp.where((row == j) & (lane == i), low[i][j], growth)
     growth_ref[...] = growth
     square = step * step
+    copies = []
     for p in range(4):
         for t in range(Z // 8):
             adv = []
@@ -622,7 +627,11 @@
                 v = inverse[k][0] * adv[0]
                 for j in range(1, k + 1):
                     v = v + inverse[k][j] * adv[j]
-                out_ref[4 * k + p, tile(t), :] = v
+                out[p, k, tile(t), :] = v
+        copies.append(pltpu.make_async_copy(out.at[p], out_hbm.at[:, p], sems.at[p]))
+        copies[p].start()
+    for copy in copies:
+        copy.wait()
 
 
 def call(body, outs, scratch=(), cost=2000000, limit=24, **more):
@@ -659,7 +668,7 @@
     near, far = lax.axis_size(NEAR), lax.axis_size(FAR)
     whole, inner, edge = (NF, Z, X), (NF, 24, X), (NF, 8, X)
     half, small, red = (2 * K, Z, X), (3, Z, X), (20, 8, X)
-    wm, wp = (jnp.asarray(w) for w in bands())
+    weights = jnp.asarray(np.stack(bands()))
     q = tangents.reshape(whole)
     coef, pack, rows, corner = call(
         prep_kernel,
@@ -671,20 +680,19 @@
     side = ring(pack, GX, -1)
     below = ring(rows, GZ, -1)
     corner = diagonal(corner)
-    warm, last, own = call(own_kernel, [half, (6, Z, X), (8, X)], [(5, 8, X)])(
-        q, coef, wm, wp
-    )
+    (square,) = call(square_kernel, [(8, X)], [(5, 8, X)])(q)
+    warm, last, own = call(own_kernel, [half, (6, Z, X), (8, X)])(q, coef, square)
     ad, bd, ap, bp, tail, packed, under, kept, part = call(
         inner_kernel,
         [inner, inner, (2, 24, X), (2, 24, X), edge, (9, 8, 2 * X), (6, 8, X), (6, 8, X), (8, X)],
         [(6, Z, 2 * X), (3, Z, 2 * X), (2, 24, X), (K, 4, Z, X), (K, 2, Z, X), red, red],
-    )(q, coef, warm, side, last, own, below, wm, wp)
+    )(q, coef, warm, side, last, own, below, weights)
     ade, bde, ape, bpe, sums = call(
         edge_kernel,
         [edge, edge, (2, 8, X), (2, 8, X), (near, 8, X)],
         [(NF, 16, X), (NC, 16, X), (K, 2, 16, X), (6, 16, 2 * X), (3, 16, 2 * X), (2, 8, X)]
         + [(K, 4, 16, X), (K, 2, 16, X), red, red],
-    )(q, kept, warm, below, corner, under, tail, packed, part, wm, wp)
+    )(q, kept, warm, below, corner, under, tail, packed, part, weights)
     sums = jnp.sum(gathered(sums, NEAR), axis=0)
     (give,) = call(give_kernel, [(2, 2, Z, X)])(ap, bp, ape, bpe)
     got = ring(give, GX, 1)
@@ -693,7 +701,10 @@
     a, b, down = call(place_kernel, [whole, whole, (8 * NF, X)])(ad, bd, ade, bde, give, got)
     above = ring(down, GZ, 1)
     out, growth = call(
-        functools.partial(finish_kernel, cells), [whole, (8, X)], [(2, NF, 8, X)]
+        functools.partial(finish_kernel, cells),
+        [(K, 4, Z, X), (8, X)],
+        [(2, NF, 8, X), (4, K, Z, X), pltpu.SemaphoreType.DMA((4,))],
+        out_specs=[pl.BlockSpec(memory_space=pl.ANY), pl.BlockSpec(memory_space=pltpu.VMEM)],
     )(q, a, b, above, sums)
     return (out.reshape(tangents.shape), growth[:, :K])
 

time: 64.5 us -> 63.5 us (0.984)
  local copies, waits for them, and re-layouts: 3.42 us -> 1.22 us
  Pallas kernels: 10.2 us -> 11 us
    unnamed x10 -> x6, local copies, waits for them, and re-layouts: 2.75 us -> 0.56 us
    pallas_call x2 -> x3, Pallas kernels: 1.81 us -> 2.59 us  [the longest x1 1.85 us: per_device(): call(functools.partial(finish_kernel, cells), [(K, 4, Z, X), (8, X)], [(2...]
  transfers between devices with their start and end apart: 7 -> 7, of which waited for: 4 -> 4; matrix products, arithmetic and copies ran while one was open for 0% -> 0% of each run, Pallas kernels for 7% -> 8%
where the time goes in v8:
time: 63.5 us; the launch traced here: 63.1 us
  starting transfers between devices  35.2 us (55%)
  waiting for transfers between devices  14.9 us (23%)
  Pallas kernels  11 us (17%)
  local copies, waits for them, and re-layouts  1.22 us (2%)
  between operations  0.77 us (1%)
    all_to_all x2, starting transfers between devices, gathered(): return lax.all_to_all(array, axes, 0, 0)  19.3 us
    ppermute x4, starting transfers between devices, ring(): lax.ppermute(array, axes, [(i, (i + step) % size) for i in range(size)])  13.8 us
    ppermute x4, waiting for transfers between devices, ring(): lax.ppermute(array, axes, [(i, (i + step) % size) for i in range(size)])  10.2 us
    all_to_all x2, waiting for transfers between devices, gathered(): return lax.all_to_all(array, axes, 0, 0)  4.68 us
    pallas_call x1, Pallas kernels, per_device(): call(inner_kernel, [inner, inner, (2, 24, X), (2, 24, X), edge, (9, 8, 2...  3.18 us
    pallas_call x1, Pallas kernels, per_device(): call(edge_kernel, [edge, edge, (2, 8, X), (2, 8, X), (near, 8, X)], [(NF,...  2.21 us
    pallas_call x1, Pallas kernels, per_device(): call(prep_kernel, [(NC, Z, X), small, (NA, 8, X), (3, 8, X)], [whole, (2,...  2.09 us
    ppermute x1, starting transfers between devices, diagonal(): return lax.ppermute(array, GX + GZ, pairs_of)  2.05 us
  transfers between devices with their start and end apart: 7, of which 4 were waited for; matrix products, arithmetic and copies ran while one was open for 0% of the time, Pallas kernels for 8%

profile of v8, /device:TPU:4, one launch (start us, length us, event | category | flops | bytes accessed | tf_op | source)
XLA Modules:
  0.0 63.1 jit_solution(13266282194555434839)
XLA Ops:
  0.6 0.0 copy-start
  0.6 2.1 %shard_map.68 = (f32[6,32,128]{2,1,0:T(8,128)}, f32[3,32,128]{2,1,0:T(8,128)}, f32[38,8,128]{2,1,0:T(8,128)}, f32[3,8,128]{2,1,0:T(8,128)}) custom-call(f32[32,32,128]{2,1,0:T(8,128)} %bitcast.3, f32[2,32,128]{2,1,0:T(8,128)} %mass_hbm.1, f32[2,32,128]{2,1,0:T(8,128)} %internal_hbm.1, f32[2,32,128]{2,1,0:T(8,128)} %velocity_hbm.1), custom_call_target="tpu_custom_call" | custom-call | flops 2000000 | bytes 2000000 | tf_op jit(solution)/shard_map/pallas_call | solution.py:673
  2.7 1.9 %collective-permute-start.1 = (f32[38,8,128]{2,1,0:T(8,128)}, f32[38,8,128]{2,1,0:T(8,128)S(1)}, u32[]{:S(2)}, u32[]{:S(2)}) collective-permute-start(f32[38,8,128]{2,1,0:T(8,128)} %get-tuple-element.35), channel_id=1, source_target_pairs={{0,31},{1,0},{2,1},{3,2},{4,3},{5,4},{6,5},{7,6},{8,7},{9,8},{10,9... | collective-permute-start | bytes 466952 | tf_op jit(solution)/shard_map/ppermute | solution.py:651
  4.7 6.8 %collective-permute-start = (f32[3,32,128]{2,1,0:T(8,128)}, f32[3,32,128]{2,1,0:T(8,128)S(1)}, u32[]{:S(2)}, u32[]{:S(2)}) collective-permute-start(f32[3,32,128]{2,1,0:T(8,128)} %get-tuple-element.32), channel_id=1, source_target_pairs={{0,480},{32,0},{64,32},{96,64},{128,96},{160,128},{192,160},{224,1... | collective-permute-start | bytes 147464 | tf_op jit(solution)/shard_map/ppermute | solution.py:651
  11.5 0.0 copy-start.2
  11.5 2.1 %collective-permute-start.2 = (f32[3,8,128]{2,1,0:T(8,128)}, f32[3,8,128]{2,1,0:T(8,128)S(1)}, u32[]{:S(2)}, u32[]{:S(2)}) collective-permute-start(f32[3,8,128]{2,1,0:T(8,128)} %get-tuple-element.39), channel_id=1, source_target_pairs={{0,511},{1,480},{2,481},{3,482},{4,483},{5,484},{6,485},{7,486},{8... | collective-permute-start | bytes 36872 | tf_op jit(solution)/shard_map/ppermute | solution.py:659
  13.6 0.0 copy-done
  13.6 0.3 shard_map.69.square_ref
  13.9 0.0 copy-start.1
  13.9 0.0 copy-done.2
  13.9 0.4 shard_map.70
  14.4 0.0 collective-permute-done.side_ref
  14.4 0.0 collective-permute-done.1.below_ref
  14.4 0.5 copy-done.1
  14.9 3.2 %shard_map.71 = (f32[32,24,128]{2,1,0:T(8,128)S(1)}, f32[32,24,128]{2,1,0:T(8,128)S(1)}, f32[2,24,128]{2,1,0:T(8,128)S(1)}, f32[2,24,128]{2,1,0:T(8,128)S(1)}, f...) custom-call(f32[32,32,128]{2,1,0:T(8,128)S(1)} %bitcast.6, ...), custom_call_target="tpu_custom_call" | custom-call | flops 2000000 | bytes 2000000 | tf_op jit(solution)/shard_map/pallas_call | solution.py:685
  18.1 0.0 collective-permute-done.2.corner_ref
  18.1 2.2 %shard_map.72 = (f32[32,8,128]{2,1,0:T(8,128)S(1)}, f32[32,8,128]{2,1,0:T(8,128)S(1)}, f32[2,8,128]{2,1,0:T(8,128)S(1)}, f32[2,8,128]{2,1,0:T(8,128)S(1)}, f32[16,8,128]{2,1,0:T(8,128)}) custom-call(f32[32,32,128]{2,1,0:T(8,128)S(1)} %bitcast.7, f32[6,8,128]{2,1,0:T(8,128)S(1)} %get-tuple-element.38.kept_ref, f32[16,32,128]{2,1,0:T(8,128)S(1)} %get-tuple-element.31.warm_ref, ...), custom_call_target="tpu_custom_call" | custom-call | flops 2000000 | bytes 2000000 | tf_op jit(solution)/shard_map/pallas_call | solution.py:690
  20.3 13.7 %all-to-all-start = ((f32[16,8,128]{2,1,0:T(8,128)}), f32[16,8,128]{2,1,0:T(8,128)S(1)}, u32[]{:S(2)}, u32[]{:S(2)}) async-start(f32[16,8,128]{2,1,0:T(8,128)} %get-tuple-element.50), calls=%async_computation | async-start | bytes 131072 | tf_op jit(solution)/shard_map/all_to_all | solution.py:663
  34.0 3.1 %collective-permute-start.3 = (f32[2,2,32,128]{3,2,1,0:T(8,128)S(1)}, f32[2,2,32,128]{3,2,1,0:T(8,128)S(1)}, u32[]{:S(2)}, u32[]{:S(2)}) collective-permute-start(f32[2,2,32,128]{3,2,1,0:T(8,128)S(1)} %shard_map.73.mine_ref), channel_id=1, source_target_pairs={{0,32},{32,64},{64,96},{96,128},{128,160},{160,192},{192,224},{224... | collective-permute-start | bytes 196616 | tf_op jit(solution)/shard_map/ppermute | solution.py:651
  37.1 0.8 %all-to-all-done = f32[16,8,128]{2,1,0:T(8,128)S(1)} async-done(((f32[16,8,128]{2,1,0:T(8,128)}), f32[16,8,128]{2,1,0:T(8,128)S(1)}, u32[]{:S(2)}, u32[]{:S(2)}) %all-to-all-start) | async-done | bytes 65568 | tf_op jit(solution)/shard_map/all_to_all | solution.py:663
  37.9 4.3 %collective-permute-done.3.got_ref = f32[2,2,32,128]{3,2,1,0:T(8,128)S(1)} collective-permute-done((f32[2,2,32,128]{3,2,1,0:T(8,128)S(1)}, f32[2,2,32,128]{3,2,1,0:T(8,128)S(1)}, u32[]{:S(2)}, u32[]{:S(2)}) %collective-permute-start.3) | collective-permute-done | bytes 65568 | tf_op jit(solution)/shard_map/ppermute | solution.py:651
  42.3 0.7 %broadcast_in_dim.3 = f32[32,8,128]{2,1,0:T(8,128)} broadcast(f32[8,128]{1,0:T(8,128)S(1)} %reduce_sum.9), dimensions={1,2} | broadcast | bytes 135168 | tf_op jit(solution)/shard_map/broadcast_in_dim | solution.py:700
  42.9 5.7 %all-to-all-start.1 = ((f32[32,8,128]{2,1,0:T(8,128)}), f32[32,8,128]{2,1,0:T(8,128)S(1)}, u32[]{:S(2)}, u32[]{:S(2)}) async-start(f32[32,8,128]{2,1,0:T(8,128)} %broadcast_in_dim.3), calls=%async_computation.1 | async-start | bytes 262144 | tf_op jit(solution)/shard_map/all_to_all | solution.py:663
  48.6 0.9 %shard_map.74 = (f32[32,32,128]{2,1,0:T(8,128)S(1)}, f32[32,32,128]{2,1,0:T(8,128)S(1)}, f32[256,128]{1,0:T(8,128)S(1)}) custom-call(f32[32,24,128]{2,1,0:T(8,128)S(1)} %get-tuple-element.36.ad_ref, f32[32,24,128]{2,1,0:T(8,128)S(1)} %get-tuple-element.37.bd_ref, f32[32,8,128]{2,1,0:T(8,128)S(1)} %get-tuple-element.44.ade_ref, ...), custom_call_target="tpu_custom_call" | custom-call | flops 2000000 | bytes 2000000 | tf_op jit(solution)/shard_map/pallas_call | solution.py:701
  49.5 1.9 %collective-permute-start.4 = (f32[256,128]{1,0:T(8,128)S(1)}, f32[256,128]{1,0:T(8,128)S(1)}, u32[]{:S(2)}, u32[]{:S(2)}) collective-permute-start(f32[256,128]{1,0:T(8,128)S(1)} %get-tuple-element.54), channel_id=1, source_target_pairs={{0,1},{1,2},{2,3},{3,4},{4,5},{5,6},{6,7},{7,8},{8,9},{9,10},{10,1... | collective-permute-start | bytes 393224 | tf_op jit(solution)/shard_map/ppermute | solution.py:651
  51.5 5.9 %collective-permute-done.4.above_ref = f32[256,128]{1,0:T(8,128)S(1)} collective-permute-done((f32[256,128]{1,0:T(8,128)S(1)}, f32[256,128]{1,0:T(8,128)S(1)}, u32[]{:S(2)}, u32[]{:S(2)}) %collective-permute-start.4) | collective-permute-done | bytes 131104 | tf_op jit(solution)/shard_map/ppermute | solution.py:651
  57.3 3.9 %all-to-all-done.1.sums_ref = f32[32,8,128]{2,1,0:T(8,128)S(1)} async-done(((f32[32,8,128]{2,1,0:T(8,128)}), f32[32,8,128]{2,1,0:T(8,128)S(1)}, u32[]{:S(2)}, u32[]{:S(2)}) %all-to-all-start.1) | async-done | bytes 131104 | tf_op jit(solution)/shard_map/all_to_all | solution.py:663
  61.2 1.9 %shard_map.75 = (f32[8,4,32,128]{3,2,1,0:T(8,128)}, f32[8,128]{1,0:T(8,128)}) custom-call(f32[32,32,128]{2,1,0:T(8,128)S(1)} %bitcast.8, f32[32,32,128]{2,1,0:T(8,128)S(1)} %get-tuple-element.52.a_ref, f32[32,32,128]{2,1,0:T(8,128)S(1)} %get-tuple-element.53.b_ref, f32[256,128]{1,0:T(8,128)S(1)} %collective-permute-done.4.above_ref, ...), custom_call_target="tpu_custom_call" | custom-call | flops 2000000 | bytes 2000000 | tf_op jit(solution)/shard_map/pallas_call | solution.py:703
  (2 shorter events, 0.0 us)
Async XLA Ops:
  0.6 13.0 %copy-start = (f32[8,2,2,32,128]{4,3,2,1,0:T(8,128)S(1)}, f32[8,2,2,32,128]{4,3,2,1,0:T(8,128)}, u32[]{:S(2)}) copy-start(f32[8,2,2,32,128]{4,3,2,1,0:T(8,128)} %param.5) | copy-start | bytes 1572868
  2.7 11.6 %collective-permute-start.1 = (f32[38,8,128]{2,1,0:T(8,128)}, f32[38,8,128]{2,1,0:T(8,128)S(1)}, u32[]{:S(2)}, u32[]{:S(2)}) collective-permute-start(f32[38,8,128]{2,1,0:T(8,128)} %get-tuple-element.35), channel_id=1, source_target_pairs={{0,31},{1,0},{2,1},{3,2},{4,3},{5,4},{6,5},{7,6},{8,7},{9,8},{10,9... | collective-permute-start | bytes 466952 | tf_op jit(solution)/shard_map/ppermute | solution.py:651
  4.7 9.7 %collective-permute-start = (f32[3,32,128]{2,1,0:T(8,128)}, f32[3,32,128]{2,1,0:T(8,128)S(1)}, u32[]{:S(2)}, u32[]{:S(2)}) collective-permute-start(f32[3,32,128]{2,1,0:T(8,128)} %get-tuple-element.32), channel_id=1, source_target_pairs={{0,480},{32,0},{64,32},{96,64},{128,96},{160,128},{192,160},{224,1... | collective-permute-start | bytes 147464 | tf_op jit(solution)/shard_map/ppermute | solution.py:651
  11.5 2.4 %copy-start.2 = (f32[6,32,128]{2,1,0:T(8,128)S(1)}, f32[6,32,128]{2,1,0:T(8,128)}, u32[]{:S(2)}) copy-start(f32[6,32,128]{2,1,0:T(8,128)} %get-tuple-element.30.coef_ref) | copy-start | bytes 294916
  11.5 6.6 %collective-permute-start.2 = (f32[3,8,128]{2,1,0:T(8,128)}, f32[3,8,128]{2,1,0:T(8,128)S(1)}, u32[]{:S(2)}, u32[]{:S(2)}) collective-permute-start(f32[3,8,128]{2,1,0:T(8,128)} %get-tuple-element.39), channel_id=1, source_target_pairs={{0,511},{1,480},{2,481},{3,482},{4,483},{5,484},{6,485},{7,486},{8... | collective-permute-start | bytes 36872 | tf_op jit(solution)/shard_map/ppermute | solution.py:659
  13.9 1.0 %copy-start.1 = (bf16[3,256,256]{2,1,0:T(8,128)(2,1)S(1)}, bf16[3,256,256]{2,1,0:T(8,128)(2,1)}, u32[]{:S(2)}) copy-start(bf16[3,256,256]{2,1,0:T(8,128)(2,1)} %constant.4.clone.w_ref) | copy-start | bytes 1179652
  20.3 17.6 %all-to-all-start = ((f32[16,8,128]{2,1,0:T(8,128)}), f32[16,8,128]{2,1,0:T(8,128)S(1)}, u32[]{:S(2)}, u32[]{:S(2)}) async-start(f32[16,8,128]{2,1,0:T(8,128)} %get-tuple-element.50), calls=%async_computation | async-start | bytes 131072 | tf_op jit(solution)/shard_map/all_to_all | solution.py:663
  34.0 8.3 %collective-permute-start.3 = (f32[2,2,32,128]{3,2,1,0:T(8,128)S(1)}, f32[2,2,32,128]{3,2,1,0:T(8,128)S(1)}, u32[]{:S(2)}, u32[]{:S(2)}) collective-permute-start(f32[2,2,32,128]{3,2,1,0:T(8,128)S(1)} %shard_map.73.mine_ref), channel_id=1, source_target_pairs={{0,32},{32,64},{64,96},{96,128},{128,160},{160,192},{192,224},{224... | collective-permute-start | bytes 196616 | tf_op jit(solution)/shard_map/ppermute | solution.py:651
  42.9 18.3 %all-to-all-start.1 = ((f32[32,8,128]{2,1,0:T(8,128)}), f32[32,8,128]{2,1,0:T(8,128)S(1)}, u32[]{:S(2)}, u32[]{:S(2)}) async-start(f32[32,8,128]{2,1,0:T(8,128)} %broadcast_in_dim.3), calls=%async_computation.1 | async-start | bytes 262144 | tf_op jit(solution)/shard_map/all_to_all | solution.py:663
  49.5 7.8 %collective-permute-start.4 = (f32[256,128]{1,0:T(8,128)S(1)}, f32[256,128]{1,0:T(8,128)S(1)}, u32[]{:S(2)}, u32[]{:S(2)}) collective-permute-start(f32[256,128]{1,0:T(8,128)S(1)} %get-tuple-element.54), channel_id=1, source_target_pairs={{0,1},{1,2},{2,3},{3,4},{4,5},{5,6},{6,7},{7,8},{8,9},{9,10},{10,1... | collective-permute-start | bytes 393224 | tf_op jit(solution)/shard_map/ppermute | solution.py:651

commit v9 on v8

--- a/solution.py
+++ b/solution.py
@@ -556,7 +556,7 @@
                             down_ref[r : r + 4, :] = part[4:8, :]
 
 
-def finish_kernel(cells, q_ref, a_ref, b_ref, above_ref, sums_ref, out_hbm, growth_ref, first, out, sems):
+def finish_kernel(cells, q_ref, a_ref, b_ref, above_ref, sums_ref, out_ref, growth_ref, first):
     lane = lanes()
     row = lax.broadcasted_iota(jnp.int32, (8, X), 0)
     for n, ref in enumerate((a_ref, b_ref)):
@@ -611,7 +611,6 @@
             growth = jnp.where((row == j) & (lane == i), low[i][j], growth)
     growth_ref[...] = growth
     square = step * step
-    copies = []
     for p in range(4):
         for t in range(Z // 8):
             adv = []
@@ -627,11 +626,7 @@
                 v = inverse[k][0] * adv[0]
                 for j in range(1, k + 1):
                     v = v + inverse[k][j] * adv[j]
-                out[p, k, tile(t), :] = v
-        copies.append(pltpu.make_async_copy(out.at[p], out_hbm.at[:, p], sems.at[p]))
-        copies[p].start()
-    for copy in copies:
-        copy.wait()
+                out_ref[4 * k + p, tile(t), :] = v
 
 
 def call(body, outs, scratch=(), cost=2000000, limit=24, **more):
@@ -701,10 +696,7 @@
     a, b, down = call(place_kernel, [whole, whole, (8 * NF, X)])(ad, bd, ade, bde, give, got)
     above = ring(down, GZ, 1)
     out, growth = call(
-        functools.partial(finish_kernel, cells),
-        [(K, 4, Z, X), (8, X)],
-        [(2, NF, 8, X), (4, K, Z, X), pltpu.SemaphoreType.DMA((4,))],
-        out_specs=[pl.BlockSpec(memory_space=pl.ANY), pl.BlockSpec(memory_space=pltpu.VMEM)],
+        functools.partial(finish_kernel, cells), [whole, (8, X)], [(2, NF, 8, X)]
     )(q, a, b, above, sums)
     return (out.reshape(tangents.shape), growth[:, :K])
 

time: 63.5 us -> 62.9 us (level)
  no operation moved by 1% of the time
where the time goes in v9:
time: 62.9 us; the launch traced here: 62.5 us
  starting transfers between devices  35.2 us (56%)
  waiting for transfers between devices  14.9 us (24%)
  Pallas kernels  10.4 us (17%)
  local copies, waits for them, and re-layouts  1.22 us (2%)
  between operations  0.77 us (1%)
    all_to_all x2, starting transfers between devices, gathered(): return lax.all_to_all(array, axes, 0, 0)  19.3 us
    ppermute x4, starting transfers between devices, ring(): lax.ppermute(array, axes, [(i, (i + step) % size) for i in range(size)])  13.8 us
    ppermute x4, waiting for transfers between devices, ring(): lax.ppermute(array, axes, [(i, (i + step) % size) for i in range(size)])  10.2 us
    all_to_all x2, waiting for transfers between devices, gathered(): return lax.all_to_all(array, axes, 0, 0)  4.68 us
    pallas_call x1, Pallas kernels, per_device(): call(inner_kernel, [inner, inner, (2, 24, X), (2, 24, X), edge, (9, 8, 2...  3.18 us
    pallas_call x1, Pallas kernels, per_device(): call(edge_kernel, [edge, edge, (2, 8, X), (2, 8, X), (near, 8, X)], [(NF,...  2.21 us
    pallas_call x1, Pallas kernels, per_device(): call(prep_kernel, [(NC, Z, X), small, (NA, 8, X), (3, 8, X)], [whole, (2,...  2.09 us
    ppermute x1, starting transfers between devices, diagonal(): return lax.ppermute(array, GX + GZ, pairs_of)  2.05 us
  transfers between devices with their start and end apart: 7, of which 4 were waited for; matrix products, arithmetic and copies ran while one was open for 0% of the time, Pallas kernels for 8%

profile of v9, /device:TPU:4, one launch (start us, length us, event | category | flops | bytes accessed | tf_op | source)
XLA Modules:
  0.0 62.5 jit_solution(10022871192677081090)
XLA Ops:
  0.6 0.0 copy-start
  0.6 2.1 %shard_map.68 = (f32[6,32,128]{2,1,0:T(8,128)}, f32[3,32,128]{2,1,0:T(8,128)}, f32[38,8,128]{2,1,0:T(8,128)}, f32[3,8,128]{2,1,0:T(8,128)}) custom-call(f32[32,32,128]{2,1,0:T(8,128)} %bitcast.3, f32[2,32,128]{2,1,0:T(8,128)} %mass_hbm.1, f32[2,32,128]{2,1,0:T(8,128)} %internal_hbm.1, f32[2,32,128]{2,1,0:T(8,128)} %velocity_hbm.1), custom_call_target="tpu_custom_call" | custom-call | flops 2000000 | bytes 2000000 | tf_op jit(solution)/shard_map/pallas_call | solution.py:668
  2.7 1.9 %collective-permute-start.1 = (f32[38,8,128]{2,1,0:T(8,128)}, f32[38,8,128]{2,1,0:T(8,128)S(1)}, u32[]{:S(2)}, u32[]{:S(2)}) collective-permute-start(f32[38,8,128]{2,1,0:T(8,128)} %get-tuple-element.35), channel_id=1, source_target_pairs={{0,31},{1,0},{2,1},{3,2},{4,3},{5,4},{6,5},{7,6},{8,7},{9,8},{10,9... | collective-permute-start | bytes 466952 | tf_op jit(solution)/shard_map/ppermute | solution.py:646
  4.7 6.8 %collective-permute-start = (f32[3,32,128]{2,1,0:T(8,128)}, f32[3,32,128]{2,1,0:T(8,128)S(1)}, u32[]{:S(2)}, u32[]{:S(2)}) collective-permute-start(f32[3,32,128]{2,1,0:T(8,128)} %get-tuple-element.32), channel_id=1, source_target_pairs={{0,480},{32,0},{64,32},{96,64},{128,96},{160,128},{192,160},{224,1... | collective-permute-start | bytes 147464 | tf_op jit(solution)/shard_map/ppermute | solution.py:646
  11.5 0.0 copy-start.2
  11.5 2.1 %collective-permute-start.2 = (f32[3,8,128]{2,1,0:T(8,128)}, f32[3,8,128]{2,1,0:T(8,128)S(1)}, u32[]{:S(2)}, u32[]{:S(2)}) collective-permute-start(f32[3,8,128]{2,1,0:T(8,128)} %get-tuple-element.39), channel_id=1, source_target_pairs={{0,511},{1,480},{2,481},{3,482},{4,483},{5,484},{6,485},{7,486},{8... | collective-permute-start | bytes 36872 | tf_op jit(solution)/shard_map/ppermute | solution.py:654
  13.6 0.0 copy-done
  13.6 0.3 shard_map.69.square_ref
  13.9 0.0 copy-start.1
  13.9 0.0 copy-done.2
  13.9 0.4 shard_map.70
  14.4 0.0 collective-permute-done.side_ref
  14.4 0.0 collective-permute-done.1.below_ref
  14.4 0.5 copy-done.1
  14.9 3.2 %shard_map.71 = (f32[32,24,128]{2,1,0:T(8,128)S(1)}, f32[32,24,128]{2,1,0:T(8,128)S(1)}, f32[2,24,128]{2,1,0:T(8,128)S(1)}, f32[2,24,128]{2,1,0:T(8,128)S(1)}, f...) custom-call(f32[32,32,128]{2,1,0:T(8,128)S(1)} %bitcast.6, ...), custom_call_target="tpu_custom_call" | custom-call | flops 2000000 | bytes 2000000 | tf_op jit(solution)/shard_map/pallas_call | solution.py:680
  18.1 0.0 collective-permute-done.2.corner_ref
  18.1 2.2 %shard_map.72 = (f32[32,8,128]{2,1,0:T(8,128)S(1)}, f32[32,8,128]{2,1,0:T(8,128)S(1)}, f32[2,8,128]{2,1,0:T(8,128)S(1)}, f32[2,8,128]{2,1,0:T(8,128)S(1)}, f32[16,8,128]{2,1,0:T(8,128)}) custom-call(f32[32,32,128]{2,1,0:T(8,128)S(1)} %bitcast.7, f32[6,8,128]{2,1,0:T(8,128)S(1)} %get-tuple-element.38.kept_ref, f32[16,32,128]{2,1,0:T(8,128)S(1)} %get-tuple-element.31.warm_ref, ...), custom_call_target="tpu_custom_call" | custom-call | flops 2000000 | bytes 2000000 | tf_op jit(solution)/shard_map/pallas_call | solution.py:685
  20.3 13.7 %all-to-all-start = ((f32[16,8,128]{2,1,0:T(8,128)}), f32[16,8,128]{2,1,0:T(8,128)S(1)}, u32[]{:S(2)}, u32[]{:S(2)}) async-start(f32[16,8,128]{2,1,0:T(8,128)} %get-tuple-element.50), calls=%async_computation | async-start | bytes 131072 | tf_op jit(solution)/shard_map/all_to_all | solution.py:658
  34.0 3.1 %collective-permute-start.3 = (f32[2,2,32,128]{3,2,1,0:T(8,128)S(1)}, f32[2,2,32,128]{3,2,1,0:T(8,128)S(1)}, u32[]{:S(2)}, u32[]{:S(2)}) collective-permute-start(f32[2,2,32,128]{3,2,1,0:T(8,128)S(1)} %shard_map.73.mine_ref), channel_id=1, source_target_pairs={{0,32},{32,64},{64,96},{96,128},{128,160},{160,192},{192,224},{224... | collective-permute-start | bytes 196616 | tf_op jit(solution)/shard_map/ppermute | solution.py:646
  37.1 0.8 %all-to-all-done = f32[16,8,128]{2,1,0:T(8,128)S(1)} async-done(((f32[16,8,128]{2,1,0:T(8,128)}), f32[16,8,128]{2,1,0:T(8,128)S(1)}, u32[]{:S(2)}, u32[]{:S(2)}) %all-to-all-start) | async-done | bytes 65568 | tf_op jit(solution)/shard_map/all_to_all | solution.py:658
  37.9 4.3 %collective-permute-done.3.got_ref = f32[2,2,32,128]{3,2,1,0:T(8,128)S(1)} collective-permute-done((f32[2,2,32,128]{3,2,1,0:T(8,128)S(1)}, f32[2,2,32,128]{3,2,1,0:T(8,128)S(1)}, u32[]{:S(2)}, u32[]{:S(2)}) %collective-permute-start.3) | collective-permute-done | bytes 65568 | tf_op jit(solution)/shard_map/ppermute | solution.py:646
  42.3 0.7 %broadcast_in_dim.3 = f32[32,8,128]{2,1,0:T(8,128)} broadcast(f32[8,128]{1,0:T(8,128)S(1)} %reduce_sum.9), dimensions={1,2} | broadcast | bytes 135168 | tf_op jit(solution)/shard_map/broadcast_in_dim | solution.py:695
  42.9 5.7 %all-to-all-start.1 = ((f32[32,8,128]{2,1,0:T(8,128)}), f32[32,8,128]{2,1,0:T(8,128)S(1)}, u32[]{:S(2)}, u32[]{:S(2)}) async-start(f32[32,8,128]{2,1,0:T(8,128)} %broadcast_in_dim.3), calls=%async_computation.1 | async-start | bytes 262144 | tf_op jit(solution)/shard_map/all_to_all | solution.py:658
  48.6 0.9 %shard_map.74 = (f32[32,32,128]{2,1,0:T(8,128)S(1)}, f32[32,32,128]{2,1,0:T(8,128)S(1)}, f32[256,128]{1,0:T(8,128)S(1)}) custom-call(f32[32,24,128]{2,1,0:T(8,128)S(1)} %get-tuple-element.36.ad_ref, f32[32,24,128]{2,1,0:T(8,128)S(1)} %get-tuple-element.37.bd_ref, f32[32,8,128]{2,1,0:T(8,128)S(1)} %get-tuple-element.44.ade_ref, ...), custom_call_target="tpu_custom_call" | custom-call | flops 2000000 | bytes 2000000 | tf_op jit(solution)/shard_map/pallas_call | solution.py:696
  49.5 1.9 %collective-permute-start.4 = (f32[256,128]{1,0:T(8,128)S(1)}, f32[256,128]{1,0:T(8,128)S(1)}, u32[]{:S(2)}, u32[]{:S(2)}) collective-permute-start(f32[256,128]{1,0:T(8,128)S(1)} %get-tuple-element.54), channel_id=1, source_target_pairs={{0,1},{1,2},{2,3},{3,4},{4,5},{5,6},{6,7},{7,8},{8,9},{9,10},{10,1... | collective-permute-start | bytes 393224 | tf_op jit(solution)/shard_map/ppermute | solution.py:646
  51.5 5.9 %collective-permute-done.4.above_ref = f32[256,128]{1,0:T(8,128)S(1)} collective-permute-done((f32[256,128]{1,0:T(8,128)S(1)}, f32[256,128]{1,0:T(8,128)S(1)}, u32[]{:S(2)}, u32[]{:S(2)}) %collective-permute-start.4) | collective-permute-done | bytes 131104 | tf_op jit(solution)/shard_map/ppermute | solution.py:646
  57.3 3.9 %all-to-all-done.1.sums_ref = f32[32,8,128]{2,1,0:T(8,128)S(1)} async-done(((f32[32,8,128]{2,1,0:T(8,128)}), f32[32,8,128]{2,1,0:T(8,128)S(1)}, u32[]{:S(2)}, u32[]{:S(2)}) %all-to-all-start.1) | async-done | bytes 131104 | tf_op jit(solution)/shard_map/all_to_all | solution.py:658
  61.2 1.3 %shard_map.75 = (f32[32,32,128]{2,1,0:T(8,128)}, f32[8,128]{1,0:T(8,128)}) custom-call(f32[32,32,128]{2,1,0:T(8,128)S(1)} %bitcast.8, f32[32,32,128]{2,1,0:T(8,128)S(1)} %get-tuple-element.52.a_ref, f32[32,32,128]{2,1,0:T(8,128)S(1)} %get-tuple-element.53.b_ref, f32[256,128]{1,0:T(8,128)S(1)} %collective-permute-done.4.above_ref, ...), custom_call_target="tpu_custom_call" | custom-call | flops 2000000 | bytes 2000000 | tf_op jit(solution)/shard_map/pallas_call | solution.py:698
  (2 shorter events, 0.0 us)
Async XLA Ops:
  0.6 13.0 %copy-start = (f32[8,2,2,32,128]{4,3,2,1,0:T(8,128)S(1)}, f32[8,2,2,32,128]{4,3,2,1,0:T(8,128)}, u32[]{:S(2)}) copy-start(f32[8,2,2,32,128]{4,3,2,1,0:T(8,128)} %param.5) | copy-start | bytes 1572868
  2.7 11.6 %collective-permute-start.1 = (f32[38,8,128]{2,1,0:T(8,128)}, f32[38,8,128]{2,1,0:T(8,128)S(1)}, u32[]{:S(2)}, u32[]{:S(2)}) collective-permute-start(f32[38,8,128]{2,1,0:T(8,128)} %get-tuple-element.35), channel_id=1, source_target_pairs={{0,31},{1,0},{2,1},{3,2},{4,3},{5,4},{6,5},{7,6},{8,7},{9,8},{10,9... | collective-permute-start | bytes 466952 | tf_op jit(solution)/shard_map/ppermute | solution.py:646
  4.7 9.7 %collective-permute-start = (f32[3,32,128]{2,1,0:T(8,128)}, f32[3,32,128]{2,1,0:T(8,128)S(1)}, u32[]{:S(2)}, u32[]{:S(2)}) collective-permute-start(f32[3,32,128]{2,1,0:T(8,128)} %get-tuple-element.32), channel_id=1, source_target_pairs={{0,480},{32,0},{64,32},{96,64},{128,96},{160,128},{192,160},{224,1... | collective-permute-start | bytes 147464 | tf_op jit(solution)/shard_map/ppermute | solution.py:646
  11.5 2.4 %copy-start.2 = (f32[6,32,128]{2,1,0:T(8,128)S(1)}, f32[6,32,128]{2,1,0:T(8,128)}, u32[]{:S(2)}) copy-start(f32[6,32,128]{2,1,0:T(8,128)} %get-tuple-element.30.coef_ref) | copy-start | bytes 294916
  11.5 6.6 %collective-permute-start.2 = (f32[3,8,128]{2,1,0:T(8,128)}, f32[3,8,128]{2,1,0:T(8,128)S(1)}, u32[]{:S(2)}, u32[]{:S(2)}) collective-permute-start(f32[3,8,128]{2,1,0:T(8,128)} %get-tuple-element.39), channel_id=1, source_target_pairs={{0,511},{1,480},{2,481},{3,482},{4,483},{5,484},{6,485},{7,486},{8... | collective-permute-start | bytes 36872 | tf_op jit(solution)/shard_map/ppermute | solution.py:654
  13.9 1.0 %copy-start.1 = (bf16[3,256,256]{2,1,0:T(8,128)(2,1)S(1)}, bf16[3,256,256]{2,1,0:T(8,128)(2,1)}, u32[]{:S(2)}) copy-start(bf16[3,256,256]{2,1,0:T(8,128)(2,1)} %constant.4.clone.w_ref) | copy-start | bytes 1179652
  20.3 17.6 %all-to-all-start = ((f32[16,8,128]{2,1,0:T(8,128)}), f32[16,8,128]{2,1,0:T(8,128)S(1)}, u32[]{:S(2)}, u32[]{:S(2)}) async-start(f32[16,8,128]{2,1,0:T(8,128)} %get-tuple-element.50), calls=%async_computation | async-start | bytes 131072 | tf_op jit(solution)/shard_map/all_to_all | solution.py:658
  34.0 8.3 %collective-permute-start.3 = (f32[2,2,32,128]{3,2,1,0:T(8,128)S(1)}, f32[2,2,32,128]{3,2,1,0:T(8,128)S(1)}, u32[]{:S(2)}, u32[]{:S(2)}) collective-permute-start(f32[2,2,32,128]{3,2,1,0:T(8,128)S(1)} %shard_map.73.mine_ref), channel_id=1, source_target_pairs={{0,32},{32,64},{64,96},{96,128},{128,160},{160,192},{192,224},{224... | collective-permute-start | bytes 196616 | tf_op jit(solution)/shard_map/ppermute | solution.py:646
  42.9 18.3 %all-to-all-start.1 = ((f32[32,8,128]{2,1,0:T(8,128)}), f32[32,8,128]{2,1,0:T(8,128)S(1)}, u32[]{:S(2)}, u32[]{:S(2)}) async-start(f32[32,8,128]{2,1,0:T(8,128)} %broadcast_in_dim.3), calls=%async_computation.1 | async-start | bytes 262144 | tf_op jit(solution)/shard_map/all_to_all | solution.py:658
  49.5 7.8 %collective-permute-start.4 = (f32[256,128]{1,0:T(8,128)S(1)}, f32[256,128]{1,0:T(8,128)S(1)}, u32[]{:S(2)}, u32[]{:S(2)}) collective-permute-start(f32[256,128]{1,0:T(8,128)S(1)} %get-tuple-element.54), channel_id=1, source_target_pairs={{0,1},{1,2},{2,3},{3,4},{4,5},{5,6},{6,7},{7,8},{8,9},{9,10},{10,1... | collective-permute-start | bytes 393224 | tf_op jit(solution)/shard_map/ppermute | solution.py:646
